TPU v7x, 32 devices: a whole 2x2x4 slice. The times are simulated.
32 devices in a mesh: dp: 8 (over z, x), fsdp: 4 (over y, core).
Axes of the slice: x: 2, y: 2, z: 4, core: 2. Of those that a mesh axis runs over, the one named last changes fastest.
Arguments:
- tokens: bfloat16 [4096, 17, 192], P(('dp', 'fsdp')), may hold values from -6 to 6
- out_grad: bfloat16 [4096, 17, 192], P(('dp', 'fsdp')), may hold values from -6 to 6
- flat_params: bfloat16 [2, 296960], P(None, ('dp', 'fsdp')), may hold values from -1.5 to 1.5, as said below
- feat_count: int32 [4096], P(('dp', 'fsdp')), may hold values from 1 to 16
- table_ids: int32 [4096], P(('dp', 'fsdp')), may hold values from 0 to 51
- table_counts: int32 [52], replicated, may hold values from 64 to 1024
Outputs:
- out_tokens: float32 [4096, 17, 192], P(('dp', 'fsdp'))
- in_grad: float32 [4096, 17, 192], P(('dp', 'fsdp'))
- param_grad: float32 [2, 296960], P(None, ('dp', 'fsdp'))
Inputs may be any that keep to these rules, and one draw needn't show every extreme that they name: `feat_count`: slot s of a row holds a feature for 1 <= s <= the row's count. `flat_params`: the norm gains lie between 0.5 and 1.5.
All inputs are finite; a program needn't handle non-finite values.
Results may differ from a plain program's by a relative error of at most 0.013.
The roundings to bfloat16 on the way count: a program that leaves them out, or rounds other values in their place, can miss the bound.
Values may be sent and summed in bfloat16 or wider, within the bound.
No kernel may reach another device: no remote copies, remote signals or barrier semaphores. Data moves between devices by JAX's collectives and lax.ppermute only.
A program may use at most 192 MiB of HBM per device.

v0:
```python
import math

import jax
import jax.numpy as jnp
from jax import lax
from jax.sharding import PartitionSpec as P

HEADS = 8
HEAD_DIM = 24
FF = 256


norm_epsilon = 1e-05
masked_score = -1000000000.0


def param_layout(model_width, hidden_units):
    return (
        ("norm1_gain", (model_width,)),
        ("norm1_bias", (model_width,)),
        ("w_qkv", (model_width, 3 * model_width)),
        ("b_query", (model_width,)),
        ("b_value", (model_width,)),
        ("w_out", (model_width, model_width)),
        ("b_out", (model_width,)),
        ("norm2_gain", (model_width,)),
        ("norm2_bias", (model_width,)),
        ("w_gate_up", (model_width, 2 * hidden_units)),
        ("b_gate_up", (2 * hidden_units,)),
        ("w_down", (hidden_units, model_width)),
        ("b_down", (model_width,)),
    )


def unpack_params(layer_flat, model_width, hidden_units):
    params = {}
    position = 0
    for entry_name, entry_shape in param_layout(model_width, hidden_units):
        entry_size = math.prod(entry_shape)
        piece_value = layer_flat[position : position + entry_size].reshape(entry_shape)
        if len(entry_shape) == 1:
            piece_value = piece_value.astype(jnp.float32)
        params[entry_name] = piece_value
        position = position + entry_size
    return params


def pack_gradients(gradients, model_width, hidden_units):
    pieces = [
        gradients[entry_name].reshape(-1)
        for entry_name, entry_shape in param_layout(model_width, hidden_units)
    ]
    joined = jnp.concatenate(pieces)
    return joined


def layer_norm(values, norm_gain, norm_bias):
    centre = values - jnp.mean(values, axis=-1, keepdims=True)
    variance = jnp.mean(centre * centre, axis=-1, keepdims=True)
    return centre * lax.rsqrt(variance + norm_epsilon) * norm_gain + norm_bias


def smooth_gate(gate_part, up_part):
    return jax.nn.gelu(gate_part, approximate=False) * up_part


def layer_pass(inputs, params, valid_slots):
    batch_rows, slot_count, model_width = inputs.shape
    hidden_units = params["w_down"].shape[0]
    score_scale = 1.0 / math.sqrt(HEAD_DIM)
    head_shape = (batch_rows, slot_count, HEADS, HEAD_DIM)
    flat_rows = inputs.reshape(batch_rows * slot_count, model_width)
    normed = layer_norm(flat_rows, params["norm1_gain"], params["norm1_bias"]).astype(jnp.bfloat16)
    projected = jnp.dot(normed, params["w_qkv"], preferred_element_type=jnp.float32)
    queries = (projected[:, :model_width] + params["b_query"]).astype(jnp.bfloat16)
    key_part = projected[:, model_width : 2 * model_width].astype(jnp.bfloat16)
    value_part = (projected[:, 2 * model_width :] + params["b_value"]).astype(jnp.bfloat16)
    query_heads = queries.reshape(head_shape)
    key_heads = key_part.reshape(head_shape)
    value_heads = value_part.reshape(head_shape)
    scores = (
        jnp.einsum("rqhd,rkhd->rhqk", query_heads, key_heads, preferred_element_type=jnp.float32)
        * score_scale
    )
    scores = jnp.where(valid_slots[:, None, None, :], scores, masked_score)
    largest = jnp.max(scores, axis=-1, keepdims=True)
    weights_exp = jnp.exp(scores - largest)
    attention = weights_exp / jnp.sum(weights_exp, axis=-1, keepdims=True)
    attention_low = attention.astype(jnp.bfloat16)
    mixed_heads = jnp.einsum(
        "rhqk,rkhd->rqhd", attention_low, value_heads, preferred_element_type=jnp.float32
    )
    mixed_low = mixed_heads.reshape(batch_rows * slot_count, model_width).astype(jnp.bfloat16)
    middle = flat_rows + (
        jnp.dot(mixed_low, params["w_out"], preferred_element_type=jnp.float32) + params["b_out"]
    )
    normed_two = layer_norm(middle, params["norm2_gain"], params["norm2_bias"]).astype(jnp.bfloat16)
    gate_up = (
        jnp.dot(normed_two, params["w_gate_up"], preferred_element_type=jnp.float32)
        + params["b_gate_up"]
    )
    gate_part = gate_up[:, :hidden_units]
    up_part = gate_up[:, hidden_units:]
    hidden_low = smooth_gate(gate_part, up_part).astype(jnp.bfloat16)
    result = middle + (
        jnp.dot(hidden_low, params["w_down"], preferred_element_type=jnp.float32) + params["b_down"]
    )
    kept_values = {
        "flat_rows": flat_rows,
        "normed": normed,
        "query_heads": query_heads,
        "key_heads": key_heads,
        "value_heads": value_heads,
        "attention": attention,
        "attention_low": attention_low,
        "mixed_low": mixed_low,
        "middle": middle,
        "normed_two": normed_two,
        "gate_part": gate_part,
        "up_part": up_part,
        "hidden_low": hidden_low,
    }
    return (result.reshape(inputs.shape), kept_values)


def layer_back(inputs, params, valid_slots, upstream):
    batch_rows, slot_count, model_width = inputs.shape
    score_scale = 1.0 / math.sqrt(HEAD_DIM)
    head_shape = (batch_rows, slot_count, HEADS, HEAD_DIM)
    unused_result, kept = layer_pass(inputs, params, valid_slots)
    grad_rows = upstream.reshape(batch_rows * slot_count, model_width)
    d_branch = grad_rows.astype(jnp.bfloat16)
    grad_w_down = jnp.einsum(
        "nf,nd->fd", kept["hidden_low"], d_branch, preferred_element_type=jnp.float32
    )
    grad_b_down = jnp.sum(d_branch.astype(jnp.float32), axis=0)
    d_hidden = jnp.einsum(
        "nd,fd->nf", d_branch, params["w_down"], preferred_element_type=jnp.float32
    )
    unused_gate, gate_pull = jax.vjp(smooth_gate, kept["gate_part"], kept["up_part"])
    d_gate, d_up = gate_pull(d_hidden)
    d_gate_up = jnp.concatenate([d_gate, d_up], axis=1).astype(jnp.bfloat16)
    grad_w_gate_up = jnp.einsum(
        "nd,ne->de", kept["normed_two"], d_gate_up, preferred_element_type=jnp.float32
    )
    grad_b_gate_up = jnp.sum(d_gate_up.astype(jnp.float32), axis=0)
    d_normed_two = jnp.einsum(
        "ne,de->nd", d_gate_up, params["w_gate_up"], preferred_element_type=jnp.float32
    )
    unused_norm_two, norm_pull_two = jax.vjp(
        layer_norm, kept["middle"], params["norm2_gain"], params["norm2_bias"]
    )
    d_middle_norm, grad_norm2_gain, grad_norm2_bias = norm_pull_two(d_normed_two)
    d_middle = grad_rows + d_middle_norm
    d_attended = d_middle.astype(jnp.bfloat16)
    grad_w_out = jnp.einsum(
        "nd,ne->de", kept["mixed_low"], d_attended, preferred_element_type=jnp.float32
    )
    grad_b_out = jnp.sum(d_attended.astype(jnp.float32), axis=0)
    d_mixed = jnp.einsum(
        "ne,de->nd", d_attended, params["w_out"], preferred_element_type=jnp.float32
    )
    d_mixed = d_mixed.astype(jnp.bfloat16).reshape(head_shape)
    d_attention = jnp.einsum(
        "rqhd,rkhd->rhqk", d_mixed, kept["value_heads"], preferred_element_type=jnp.float32
    )
    d_value = jnp.einsum(
        "rhqk,rqhd->rkhd", kept["attention_low"], d_mixed, preferred_element_type=jnp.float32
    )
    attention = kept["attention"]
    d_scores = attention * (d_attention - jnp.sum(attention * d_attention, axis=-1, keepdims=True))
    d_scores_low = d_scores.astype(jnp.bfloat16)
    d_query = (
        jnp.einsum(
            "rhqk,rkhd->rqhd", d_scores_low, kept["key_heads"], preferred_element_type=jnp.float32
        )
        * score_scale
    )
    d_key = (
        jnp.einsum(
            "rhqk,rqhd->rkhd", d_scores_low, kept["query_heads"], preferred_element_type=jnp.float32
        )
        * score_scale
    )
    token_total = batch_rows * slot_count
    d_project = jnp.concatenate(
        [
            d_query.reshape(token_total, model_width),
            d_key.reshape(token_total, model_width),
            d_value.reshape(token_total, model_width),
        ],
        axis=1,
    ).astype(jnp.bfloat16)
    grad_w_qkv = jnp.einsum(
        "nd,ne->de", kept["normed"], d_project, preferred_element_type=jnp.float32
    )
    grad_b_query = jnp.sum(d_project[:, :model_width].astype(jnp.float32), axis=0)
    grad_b_value = jnp.sum(d_project[:, 2 * model_width :].astype(jnp.float32), axis=0)
    d_normed = jnp.einsum(
        "ne,de->nd", d_project, params["w_qkv"], preferred_element_type=jnp.float32
    )
    unused_norm_one, norm_pull_one = jax.vjp(
        layer_norm, kept["flat_rows"], params["norm1_gain"], params["norm1_bias"]
    )
    d_rows_norm, grad_norm1_gain, grad_norm1_bias = norm_pull_one(d_normed)
    d_inputs = d_middle + d_rows_norm
    gradients = {
        "norm1_gain": grad_norm1_gain,
        "norm1_bias": grad_norm1_bias,
        "w_qkv": grad_w_qkv,
        "b_query": grad_b_query,
        "b_value": grad_b_value,
        "w_out": grad_w_out,
        "b_out": grad_b_out,
        "norm2_gain": grad_norm2_gain,
        "norm2_bias": grad_norm2_bias,
        "w_gate_up": grad_w_gate_up,
        "b_gate_up": grad_b_gate_up,
        "w_down": grad_w_down,
        "b_down": grad_b_down,
    }
    return (d_inputs.reshape(inputs.shape), gradients)


def body(tokens, out_grad, flat_params, feat_count, table_ids, table_counts):
    batch_rows, slot_count, model_width = tokens.shape
    hidden_units = FF
    layer_total = flat_params.shape[0]
    slot_index = jnp.arange(slot_count, dtype=jnp.int32)
    valid_slots = slot_index[None, :] <= feat_count[:, None]
    counts_float = table_counts.astype(jnp.float32)
    table_index = jnp.arange(table_counts.shape[0], dtype=jnp.int32)
    table_match = (table_ids[:, None] == table_index[None, :]).astype(jnp.float32)
    row_count = jnp.sum(table_match * counts_float[None, :], axis=1)
    row_scale = jnp.sqrt(jnp.mean(counts_float) / row_count)
    seed_grad = (
        out_grad.astype(jnp.float32)
        * row_scale[:, None, None]
        * valid_slots[:, :, None].astype(jnp.float32)
    )
    layer_inputs = []
    current = tokens.astype(jnp.float32)
    for layer_index in range(layer_total):
        layer_flat = lax.all_gather(flat_params[layer_index], ("dp", "fsdp"), axis=0, tiled=True)
        layer_inputs.append(current)
        current, unused_kept = layer_pass(
            current, unpack_params(layer_flat, model_width, hidden_units), valid_slots
        )
    upstream = seed_grad
    grad_list = [None] * layer_total
    for layer_index in reversed(range(layer_total)):
        layer_flat = lax.all_gather(flat_params[layer_index], ("dp", "fsdp"), axis=0, tiled=True)
        upstream, gradients = layer_back(
            layer_inputs[layer_index],
            unpack_params(layer_flat, model_width, hidden_units),
            valid_slots,
            upstream,
        )
        packed = pack_gradients(gradients, model_width, hidden_units)
        grad_list[layer_index] = lax.psum_scatter(
            packed, ("dp", "fsdp"), scatter_dimension=0, tiled=True
        )
    param_grad = jnp.stack(grad_list)
    return (current, upstream, param_grad)


def solution(mesh):
    placed = (
        P(("dp", "fsdp"), None, None),
        P(("dp", "fsdp"), None, None),
        P(None, ("dp", "fsdp")),
        P(("dp", "fsdp")),
        P(("dp", "fsdp")),
        P(),
    )
    return jax.shard_map(
        body,
        mesh=mesh,
        in_specs=placed,
        out_specs=(
            P(("dp", "fsdp"), None, None),
            P(("dp", "fsdp"), None, None),
            P(None, ("dp", "fsdp")),
        ),
        check_vma=False,
    )
```

profile of v0, /device:TPU:0, one launch (start us, length us, event | category | flops | bytes accessed | tf_op | source)
XLA Modules:
  0.0 1087.6 jit_solution(15960626670858584785)
XLA Ops:
  34.2 112.6 %all-reduce.11.cloned.1.call-done = (bf16[296960]{0:T(1024)(128)(2,1)}, bf16[296960]{0:T(1024)(128)(2,1)}) async-done(((bf16[296960]{0:T(1024)(128)(2,1)}, bf16[296960]{0:T(1024)(128)(2,1)}), (bf16[296960]{0:T(1024)(128)(2,1)}, bf16[296960]{0:T(1024)(128)(2,1)})) %all-reduce.11.cloned.1.call-update) | async-done | bytes 1187856
  146.8 6.6 reshape.455
  158.7 7.0 reshape.457
  189.4 15.9 %reshape.469 = bf16[128,17,8,24]{1,0,3,2:T(8,128)(2,1)} reshape(bf16[2176,192]{0,1:T(8,128)(2,1)} %get-tuple-element.60) | data formatting | bytes 1671168 | tf_op jit(solution)/shard_map/reshape | solution.py:78
  205.3 16.0 %reshape.470 = bf16[128,17,8,24]{1,0,3,2:T(8,128)(2,1)} reshape(bf16[2176,192]{0,1:T(8,128)(2,1)} %slice.331) | data formatting | bytes 1671168 | tf_op jit(solution)/shard_map/reshape | solution.py:79
  221.2 15.0 %reshape.468 = bf16[128,17,8,24]{1,0,3,2:T(8,128)(2,1)} reshape(bf16[2176,192]{0,1:T(8,128)(2,1)S(1)} %get-tuple-element.61) | data formatting | bytes 1671168 | tf_op jit(solution)/shard_map/reshape | solution.py:80
  236.3 11.4 %copy.247 = bf16[128,17,8,24]{3,1,2,0:T(8,128)(2,1)} copy(bf16[128,17,8,24]{1,0,3,2:T(8,128)(2,1)} %reshape.468) | data formatting | bytes 1671168 | tf_op jit(solution)/shard_map/reshape | solution.py:80
  247.7 24.6 %fusion.19 = f32[128,8,17,17]{2,3,1,0:T(8,128)} fusion(bf16[128,17,8,24]{1,0,3,2:T(8,128)(2,1)} %reshape.470, bf16[128,17,8,24]{1,0,3,2:T(8,128)(2,1)} %reshape.469), kind=kOutput, calls=%fused_computation.27 | convolution fusion | flops 14204928 | bytes 2854912 | tf_op jit(solution)/shard_map/rqhd,rkhd->rhqk/dot_general | solution.py:82
  272.3 9.2 copy.213
  283.4 11.0 %copy.215 = bf16[128,8,17,17]{3,2,1,0:T(8,128)(2,1)} copy(bf16[128,8,17,17]{0,1,3,2:T(8,128)(2,1)S(1)} %fusion.102) | data formatting | bytes 1183744 | tf_op jit(solution)/shard_map/convert_element_type | solution.py:89
  294.4 8.3 convert_bitcast_fusion.3
  302.7 10.3 copy.216
  331.8 15.0 %reshape.472 = bf16[128,17,8,24]{1,0,3,2:T(8,128)(2,1)} reshape(bf16[2176,192]{0,1:T(8,128)(2,1)S(1)} %get-tuple-element.58) | data formatting | bytes 1671168 | tf_op jit(solution)/shard_map/reshape | solution.py:78
  346.8 16.0 %reshape.473 = bf16[128,17,8,24]{1,0,3,2:T(8,128)(2,1)} reshape(bf16[2176,192]{0,1:T(8,128)(2,1)} %slice.330) | data formatting | bytes 1671168 | tf_op jit(solution)/shard_map/reshape | solution.py:79
  362.8 15.0 %reshape.471 = bf16[128,17,8,24]{1,0,3,2:T(8,128)(2,1)} reshape(bf16[2176,192]{0,1:T(8,128)(2,1)S(1)} %get-tuple-element.59) | data formatting | bytes 1671168 | tf_op jit(solution)/shard_map/reshape | solution.py:80
  377.8 11.4 %copy.233 = bf16[128,17,8,24]{3,1,2,0:T(8,128)(2,1)} copy(bf16[128,17,8,24]{1,0,3,2:T(8,128)(2,1)} %reshape.471) | data formatting | bytes 1671168 | tf_op jit(solution)/shard_map/reshape | solution.py:80
  389.2 24.6 %fusion.12 = f32[128,8,17,17]{2,3,1,0:T(8,128)} fusion(bf16[128,17,8,24]{1,0,3,2:T(8,128)(2,1)} %reshape.473, bf16[128,17,8,24]{1,0,3,2:T(8,128)(2,1)} %reshape.472), kind=kOutput, calls=%fused_computation.20 | convolution fusion | flops 14204928 | bytes 2854912 | tf_op jit(solution)/shard_map/rqhd,rkhd->rhqk/dot_general | solution.py:82
  413.8 9.2 copy.223
  424.4 11.0 %copy.225 = bf16[128,8,17,17]{3,2,1,0:T(8,128)(2,1)} copy(bf16[128,8,17,17]{0,1,3,2:T(8,128)(2,1)S(1)} %fusion.101) | data formatting | bytes 1183744 | tf_op jit(solution)/shard_map/convert_element_type | solution.py:89
  435.4 8.2 convert_bitcast_fusion.2
  443.6 10.3 copy.226
  453.9 6.4 convert_element_type.264
  464.5 6.6 add_convert_fusion.1
  482.1 16.3 %reshape.474 = bf16[128,17,8,24]{1,0,3,2:T(8,128)(2,1)} reshape(bf16[2176,192]{0,1:T(8,128)(2,1)} %convolution_convert_fusion.1) | data formatting | bytes 1671168 | tf_op jit(solution)/shard_map/reshape | solution.py:163
  498.4 21.8 %convert_bitcast_fusion.1 = bf16[128,17,8,24]{1,3,2,0:T(8,128)(2,1)} fusion(bf16[128,8,17,17]{3,2,1,0:T(8,128)(2,1)} %copy.225, bf16[128,17,8,24]{1,0,3,2:T(8,128)(2,1)} %reshape.474), kind=kOutput, calls=%fused_computation.9 | convolution fusion | flops 14622720 | bytes 2263040 | tf_op jit(solution)/shard_map/rhqk,rqhd->rkhd/dot_general | solution.py:167
  520.3 21.9 %fusion.8 = f32[128,8,17,17]{2,3,1,0:T(8,128)} fusion(bf16[128,17,8,24]{3,1,2,0:T(8,128)(2,1)} %copy.233, bf16[128,17,8,24]{1,0,3,2:T(8,128)(2,1)} %reshape.474), kind=kOutput, calls=%fused_computation.16 | convolution fusion | flops 14204928 | bytes 2854912 | tf_op jit(solution)/shard_map/rqhd,rkhd->rhqk/dot_general | solution.py:164
  542.2 9.7 copy.235
  554.0 11.4 %copy.237 = bf16[128,8,17,17]{3,2,1,0:T(8,128)(2,1)} copy(bf16[128,8,17,17]{0,1,3,2:T(8,128)(2,1)S(1)} %multiply_convert_fusion.9) | data formatting | bytes 1183744 | tf_op jit(solution)/shard_map/convert_element_type | solution.py:172
  565.5 21.9 %fusion.1 = bf16[128,17,8,24]{1,3,2,0:T(8,128)(2,1)} fusion(bf16[128,8,17,17]{3,2,1,0:T(8,128)(2,1)} %copy.237, bf16[128,17,8,24]{1,0,3,2:T(8,128)(2,1)} %reshape.472), kind=kOutput, calls=%fused_computation.5 | convolution fusion | flops 15040512 | bytes 2263040 | tf_op jit(solution)/shard_map/rhqk,rqhd->rkhd/dot_general | solution.py:180
  587.3 20.0 %fusion = bf16[128,17,8,24]{1,3,2,0:T(8,128)(2,1)} fusion(bf16[128,8,17,17]{3,2,1,0:T(8,128)(2,1)} %copy.237, bf16[128,17,8,24]{1,0,3,2:T(8,128)(2,1)} %reshape.473), kind=kOutput, calls=%fused_computation.4 | convolution fusion | flops 15040512 | bytes 2263040 | tf_op jit(solution)/shard_map/rhqk,rkhd->rqhd/dot_general | solution.py:174
  607.3 10.3 copy.244
  623.2 10.3 copy.238
  633.5 6.3 reshape.384
  639.8 10.3 copy.241
  677.7 15.2 %reshape.475 = bf16[128,17,8,24]{1,0,3,2:T(8,128)(2,1)} reshape(bf16[2176,192]{0,1:T(8,128)(2,1)S(1)} %convolution_convert_fusion) | data formatting | bytes 1671168 | tf_op jit(solution)/shard_map/reshape | solution.py:163
  692.9 21.9 %convert_bitcast_fusion = bf16[128,17,8,24]{1,3,2,0:T(8,128)(2,1)} fusion(bf16[128,8,17,17]{3,2,1,0:T(8,128)(2,1)} %copy.215, bf16[128,17,8,24]{1,0,3,2:T(8,128)(2,1)} %reshape.475), kind=kOutput, calls=%fused_computation.8 | convolution fusion | flops 14622720 | bytes 2263040 | tf_op jit(solution)/shard_map/rhqk,rqhd->rkhd/dot_general | solution.py:167
  714.9 22.1 %fusion.4 = f32[128,8,17,17]{2,3,1,0:T(8,128)} fusion(bf16[128,17,8,24]{3,1,2,0:T(8,128)(2,1)} %copy.247, bf16[128,17,8,24]{1,0,3,2:T(8,128)(2,1)} %reshape.475), kind=kOutput, calls=%fused_computation.12 | convolution fusion | flops 14204928 | bytes 2854912 | tf_op jit(solution)/shard_map/rqhd,rkhd->rhqk/dot_general | solution.py:164
  737.0 9.8 copy.249
  749.7 11.5 %copy.251 = bf16[128,8,17,17]{3,2,1,0:T(8,128)(2,1)} copy(bf16[128,8,17,17]{0,1,3,2:T(8,128)(2,1)} %multiply_convert_fusion.8) | data formatting | bytes 1183744 | tf_op jit(solution)/shard_map/convert_element_type | solution.py:172
  761.2 22.0 %fusion.3 = bf16[128,17,8,24]{1,3,2,0:T(8,128)(2,1)} fusion(bf16[128,8,17,17]{3,2,1,0:T(8,128)(2,1)} %copy.251, bf16[128,17,8,24]{1,0,3,2:T(8,128)(2,1)} %reshape.469), kind=kOutput, calls=%fused_computation.7 | convolution fusion | flops 15040512 | bytes 2263040 | tf_op jit(solution)/shard_map/rhqk,rqhd->rkhd/dot_general | solution.py:180
  783.2 20.1 %fusion.2 = bf16[128,17,8,24]{1,3,2,0:T(8,128)(2,1)} fusion(bf16[128,8,17,17]{3,2,1,0:T(8,128)(2,1)} %copy.251, bf16[128,17,8,24]{1,0,3,2:T(8,128)(2,1)} %reshape.470), kind=kOutput, calls=%fused_computation.6 | convolution fusion | flops 15040512 | bytes 2263040 | tf_op jit(solution)/shard_map/rhqk,rkhd->rqhd/dot_general | solution.py:174
  825.8 10.3 copy.258
  842.4 10.3 copy.252
  859.1 10.3 copy.255
  869.3 6.5 reshape.389
  892.2 24.7 %concatenate.27 = f32[296960]{0:T(1024)} concatenate(f32[192]{0:T(256)} %get-tuple-element.20, f32[192]{0:T(256)} %get-tuple-element.30, f32[110592]{0:T(1024)} %reshape.396, f32[192]{0:T(256)} %get-tuple-element.97, f32[192]{0:T(256)} %get-tuple-element.96, f32[36864]{0:T(1024)} %reshape.397, f32[192]{0:T(256)} %get-tuple-element.44, f32[192]{0:T(256)} %get-tuple-element.24, ...), dimensions={0} | concatenate | bytes 2375680 | tf_op jit(solution)/shard_map/concatenate | solution.py:53
  916.9 25.9 %concatenate.26 = f32[296960]{0:T(1024)} concatenate(f32[192]{0:T(256)} %get-tuple-element.18, f32[192]{0:T(256)} %get-tuple-element.27, f32[110592]{0:T(1024)} %reshape.392, f32[192]{0:T(256)} %get-tuple-element.99, f32[192]{0:T(256)} %get-tuple-element.98, f32[36864]{0:T(1024)} %reshape.393, f32[192]{0:T(256)} %get-tuple-element.40, f32[192]{0:T(256)} %get-tuple-element.22, ...), dimensions={0} | concatenate | bytes 2375680 | tf_op jit(solution)/shard_map/concatenate | solution.py:53
  954.4 123.7 %all-reduce.9.cloned.1.call-done = (f32[296960]{0:T(1024)}, f32[296960]{0:T(1024)}) async-done(((f32[296960]{0:T(1024)}, f32[296960]{0:T(1024)}), (f32[296960]{0:T(1024)}, f32[296960]{0:T(1024)})) %all-reduce.9.cloned.1.call-update) | async-done | bytes 2375696
  (353 shorter events, 195.5 us)
Async XLA Ops:
  7.2 3.1 copy-start.99
  7.2 3.7 copy-start.15
  7.2 139.6 %all-reduce.11.cloned.1.call-start = ((), (), s32[]{:S(2)}) async-start(), calls=%async_computation.1 | async-start | bytes 2375680
  8.9 3.1 copy-start.100
  10.2 1067.8 %all-reduce.9.cloned.1.call-start = ((), (), s32[]{:S(2)}) async-start(), calls=%async_computation | async-start | bytes 4751360
  12.2 3.9 copy-start.98
  12.2 3.9 copy-start.48
  34.2 284.3 %copy-start.6 = (f32[2176,192]{0,1:T(8,128)}, f32[2176,192]{0,1:T(8,128)S(1)}, u32[]{:S(2)}) copy-start(f32[2176,192]{0,1:T(8,128)S(1)} %copy.217) | copy-start | bytes 5013508
  146.8 11.9 %copy-start.54 = (bf16[296960]{0:T(1024)(128)(2,1)S(1)}, bf16[296960]{0:T(1024)(128)(2,1)}, u32[]{:S(2)}) copy-start(bf16[296960]{0:T(1024)(128)(2,1)} %get-tuple-element.37) | copy-start | bytes 1781764
  154.6 20.0 %copy-start.79 = (f32[1,192]{1,0:T(1,128)}, f32[1,192]{1,0:T(1,128)S(1)}, u32[]{:S(2)}) copy-start(f32[1,192]{1,0:T(1,128)S(1)} %get-tuple-element.77) | copy-start | bytes 2308
  154.6 20.0 %copy-start.87 = (f32[1,192]{1,0:T(1,128)}, f32[1,192]{1,0:T(1,128)S(1)}, u32[]{:S(2)}) copy-start(f32[1,192]{1,0:T(1,128)S(1)} %get-tuple-element.76) | copy-start | bytes 2308
  165.7 9.0 copy-start.16
  172.8 145.7 %copy-start.45 = (bf16[192,192]{1,0:T(8,128)(2,1)}, bf16[192,192]{1,0:T(8,128)(2,1)S(1)}, u32[]{:S(2)}) copy-start(bf16[192,192]{1,0:T(8,128)(2,1)S(1)} %reshape.371) | copy-start | bytes 221188
  174.6 11.7 %copy-start.41 = (bf16[192,576]{1,0:T(8,128)(2,1)}, bf16[192,576]{1,0:T(8,128)(2,1)S(1)}, u32[]{:S(2)}) copy-start(bf16[192,576]{1,0:T(8,128)(2,1)S(1)} %reshape.367) | copy-start | bytes 663556
  313.0 5.6 copy-start.94
  319.5 8.1 copy-start.4
  321.7 5.9 copy-start.9
  321.7 5.9 copy-start.56
  321.7 5.9 copy-start.91
  453.9 6.4 copy-start.47
  453.9 6.4 copy-start.90
  462.1 14.7 %copy-start.2 = (f32[2176,192]{0,1:T(8,128)}, f32[2176,192]{0,1:T(8,128)S(1)}, u32[]{:S(2)}) copy-start(f32[2176,192]{0,1:T(8,128)S(1)} %get-tuple-element.90) | copy-start | bytes 5013508
  542.2 9.7 copy-start.35
  656.4 2.4 copy-start.26
  656.4 2.4 copy-start.39
  660.9 4.1 copy-start.13
  660.9 6.9 slice-start
  663.0 4.8 slice-start.1
  736.9 9.8 copy-start.1
  737.0 9.8 copy-start.31
  737.0 9.8 copy-start.33
  803.3 5.0 copy-start.3
  803.3 5.0 copy-start.89
  808.3 2.9 copy-start.59
  812.1 2.9 copy-start.52
  819.2 3.2 copy-start.58
  819.2 4.2 copy-start.40
  819.2 5.0 copy-start.60
  875.8 2.7 copy-start.7
  875.8 2.7 copy-start.42
  875.8 2.7 copy-start.63
  875.9 2.7 copy-start.80
  878.6 5.3 copy-start.78
  878.6 5.9 copy-start.24
  878.6 5.9 copy-start.25
  878.6 5.9 copy-start.38
  878.6 5.9 copy-start.88
  888.6 3.6 copy-start.53
  (57 other events, 77.0 us)
Sparse Core Ops, SparseCore 0:
  13.5 133.1 all-reduce.10
  942.9 135.0 all-reduce.8
where the time goes:
time: 1100 us; the launch traced here: 1090 us
  local copies, waits for them, and re-layouts  510 us (46%)
  matrix products  281 us (26%)
  waiting for transfers between devices  236 us (21%)
  other arithmetic  44.5 us (4%)
  between operations  16.1 us (1%)
    unnamed x4, waiting for transfers between devices  236 us
    reshape x4, local copies, waits for them, and re-layouts, layer_pass(): value_heads = value_part.reshape(head_shape)  52.8 us
    concatenate x2, local copies, waits for them, and re-layouts, pack_gradients(): joined = jnp.concatenate(pieces)  50.6 us
    dot_general x2, matrix products, layer_pass(): jnp.einsum('rqhd,rkhd->rhqk', query_heads, key_heads, preferred_element_t...  49.3 us
    dot_general x2, matrix products, layer_back(): jnp.einsum('rqhd,rkhd->rhqk', d_mixed, kept['value_heads'], preferred_ele...  44 us
    dot_general x2, matrix products, layer_back(): jnp.einsum('rhqk,rqhd->rkhd', d_scores_low, kept['query_heads'], preferre...  43.9 us
    dot_general x2, matrix products, layer_back(): jnp.einsum('rhqk,rqhd->rkhd', kept['attention_low'], d_mixed, preferred_e...  43.8 us
    dot_general x2, matrix products, layer_back(): jnp.einsum('rhqk,rkhd->rqhd', d_scores_low, kept['key_heads'], preferred_...  40.1 us
  transfers between devices with their start and end apart: 2, of which 2 were waited for; matrix products, arithmetic and copies ran while one was open for 3% of the time, Pallas kernels for 0%

commit v1 on v0

v1 whole, which is shorter than its diff:
```python
import math

import jax
import jax.numpy as jnp
from jax import lax
from jax.experimental import pallas as pl
from jax.experimental.pallas import tpu as pltpu
from jax.sharding import PartitionSpec as P

D = 192
FF = 256
HEADS = 8
HEAD_DIM = 24
SEQ = 17
LAYERS = 2
PSIZE = 296960
ROWS = 128
SLOTS = 18
LANES = 128
GROUP = 8
GROUPS = ROWS // GROUP
GT = SLOTS * GROUP
QL = HEADS * GT
TOKENS = SLOTS * ROWS
CHUNK = 2 * ROWS
CHUNKS = TOKENS // CHUNK
FLAT = PSIZE // LANES
PARTS = 32
BLOCK = 80
EPS = 1e-05
SCALE = 1.0 / math.sqrt(HEAD_DIM)
F32 = jnp.float32
BF16 = jnp.bfloat16


def dot(a, b, ca, cb):
    return lax.dot_general(a, b, (((ca,), (cb,)), ((), ())), preferred_element_type=F32)


def lane_half(shape):
    return lax.broadcasted_iota(jnp.int32, shape, len(shape) - 1) < 64


def swap(x):
    return pltpu.roll(x, 64, x.ndim - 1)


def low_half(x):
    return jnp.where(lane_half(x.shape), x, 0.0)


def splice(a, b):
    return jnp.where(lane_half(a.shape), swap(a), swap(b))


def after(a, b):
    return jnp.where(lane_half(a.shape), a, swap(b))


def wide(column):
    return jnp.concatenate([column, column], axis=1)


def gather_flat(blocks, layer, flat):
    for pair in range(blocks.shape[0] // 2):
        base = 145 * pair
        first = blocks[2 * pair, layer].astype(F32)
        second = blocks[2 * pair + 1, layer].astype(F32)
        flat[pl.ds(base, BLOCK), :] = first
        flat[pl.ds(base + 72, BLOCK), :] = second
        flat[pl.ds(base + 72, 1), :] = jnp.where(
            lane_half((1, LANES)), first[72:73], second[0:1]
        )


def column_of(row):
    return jnp.transpose(jnp.broadcast_to(row, (LANES, 2 * LANES)))[0:D]


def unpack(flat, w, tmp):
    def rows(start, count, stride):
        return flat[pl.ds(start, count, stride=stride), :]

    def row(index):
        return flat[pl.ds(index, 1), :]

    def pair_row(a, b):
        return jnp.concatenate([a, b], axis=1)

    w["cols"][0] = column_of(pair_row(row(0), low_half(row(1))))
    w["cols"][1] = column_of(pair_row(splice(row(1), row(2)), low_half(swap(row(2)))))
    w["cols"][2] = column_of(pair_row(row(1158), low_half(row(1159))))
    w["cols"][3] = column_of(pair_row(splice(row(1159), row(1160)), low_half(swap(row(1160)))))
    w["cols"][4] = column_of(pair_row(row(1161), low_half(row(1162))))
    w["cols"][5] = column_of(pair_row(splice(row(2318), row(2319)), low_half(swap(row(2319)))))

    e = [rows(3 + j, 96, 9) for j in range(9)]
    even = (e[0], low_half(e[1]), splice(e[1], e[2]), low_half(swap(e[2])), e[3], low_half(e[4]))
    odd = (
        splice(e[4], e[5]),
        low_half(swap(e[5])),
        e[6],
        low_half(e[7]),
        splice(e[7], e[8]),
        low_half(swap(e[8])),
    )
    zero_row = jnp.zeros((1, LANES), F32)
    bias = (
        row(867),
        low_half(row(868)),
        zero_row,
        zero_row,
        splice(row(868), row(869)),
        low_half(swap(row(869))),
    )
    first_row = lax.broadcasted_iota(jnp.int32, (16, LANES), 0) == 0
    for j in range(6):
        tmp[j, pl.ds(0, 96, stride=2), :] = even[j]
        tmp[j, pl.ds(1, 96, stride=2), :] = odd[j]
        w["qkv"][0:D, j * LANES : (j + 1) * LANES] = tmp[j, 0:D, :].astype(BF16)
        w["qkv"][D : D + 16, j * LANES : (j + 1) * LANES] = jnp.where(
            first_row, jnp.broadcast_to(bias[j], (16, LANES)), 0.0
        ).astype(BF16)

    e = [rows(870 + j, 96, 3) for j in range(3)]
    tmp[0, pl.ds(0, 96, stride=2), :] = e[0]
    tmp[1, pl.ds(0, 96, stride=2), :] = low_half(e[1])
    tmp[0, pl.ds(1, 96, stride=2), :] = splice(e[1], e[2])
    tmp[1, pl.ds(1, 96, stride=2), :] = low_half(swap(e[2]))
    w_out = jnp.concatenate([tmp[0, 0:D, :], tmp[1, 0:D, :]], axis=1)
    w["out_t"][...] = jnp.transpose(w_out)[0:D].astype(BF16)

    g = [rows(1162 + j, 192, 4) for j in range(5)]
    tiles = [splice(g[j], g[j + 1]) for j in range(4)]
    gate_up = jnp.concatenate(tiles, axis=1)
    w["gu"][...] = gate_up.astype(BF16)
    bias_row = jnp.concatenate(
        [splice(row(1930 + j), row(1931 + j)) for j in range(4)], axis=1
    )
    bias_rows = jnp.where(
        lax.broadcasted_iota(jnp.int32, (64, 2 * FF), 0) == 0,
        jnp.broadcast_to(bias_row, (64, 2 * FF)),
        0.0,
    )
    w["gu_t"][...] = jnp.transpose(jnp.concatenate([gate_up, bias_rows], axis=0))[
        :, 0 : D + 16
    ].astype(BF16)

    e = [rows(1934 + j, 128, 3) for j in range(4)]
    tmp[0, pl.ds(0, 128, stride=2), :] = splice(e[0], e[1])
    tmp[1, pl.ds(0, 128, stride=2), :] = low_half(swap(e[1]))
    tmp[0, pl.ds(1, 128, stride=2), :] = e[2]
    tmp[1, pl.ds(1, 128, stride=2), :] = low_half(e[3])
    w_down = jnp.concatenate([tmp[0, 0:FF, :], tmp[1, 0:FF, :]], axis=1)
    w["down"][...] = w_down[:, 0:D].astype(BF16)
    w["down_t"][...] = jnp.transpose(w_down)[0:D].astype(BF16)


def row_of(columns):
    turned = jnp.sum(jnp.transpose(columns), axis=0, keepdims=True)
    return turned[:, 0:LANES], jnp.concatenate(
        [turned[:, LANES:D], jnp.zeros((1, LANES - (D - LANES)), F32)], axis=1
    )


def pack(flat, acc, sums, tmp):
    def put(start, count, stride, value):
        flat[pl.ds(start, count, stride=stride), :] = value

    def put_row(index, value):
        flat[pl.ds(index, 1), :] = value

    def down(j, start, count, stride):
        return acc["down"][j, pl.ds(start, count, stride=stride), :]

    g1 = row_of(sums[0])
    b1 = row_of(sums[1])
    g2 = row_of(sums[2])
    b2 = row_of(sums[3])
    bo = row_of(sums[4])
    put_row(0, g1[0])
    put_row(1, after(g1[1], b1[0]))
    put_row(2, splice(b1[0], b1[1]))

    even = [acc["qkv"][j, pl.ds(0, 96, stride=2), :] for j in range(6)]
    odd = [acc["qkv"][j, pl.ds(1, 96, stride=2), :] for j in range(6)]
    put(3, 96, 9, even[0])
    put(4, 96, 9, after(even[1], even[2]))
    put(5, 96, 9, splice(even[2], even[3]))
    put(6, 96, 9, even[4])
    put(7, 96, 9, after(even[5], odd[0]))
    put(8, 96, 9, splice(odd[0], odd[1]))
    put(9, 96, 9, odd[2])
    put(10, 96, 9, after(odd[3], odd[4]))
    put(11, 96, 9, splice(odd[4], odd[5]))
    bias = [acc["qkv"][j, D : D + 1, :] for j in range(6)]
    put_row(867, bias[0])
    put_row(868, after(bias[1], bias[4]))
    put_row(869, splice(bias[4], bias[5]))

    w_out = jnp.transpose(
        jnp.concatenate([acc["out_t"][...], jnp.zeros((64, D), F32)], axis=0)
    )
    tmp[0, 0:D, :] = w_out[:, 0:LANES]
    tmp[1, 0:D, :] = w_out[:, LANES:]
    even = [tmp[j, pl.ds(0, 96, stride=2), :] for j in range(2)]
    odd = [tmp[j, pl.ds(1, 96, stride=2), :] for j in range(2)]
    put(870, 96, 3, even[0])
    put(871, 96, 3, after(even[1], odd[0]))
    put(872, 96, 3, splice(odd[0], odd[1]))
    put_row(1158, bo[0])
    put_row(1159, after(bo[1], g2[0]))
    put_row(1160, splice(g2[0], g2[1]))
    put_row(1161, b2[0])

    gu = [acc["gu"][j, 0 : D + 8, :] for j in range(4)]
    put_row(1162, after(b2[1], gu[0][0:1]))
    put(1166, 192, 4, splice(gu[3][0:192], acc["gu"][0, pl.ds(1, 192), :]))
    for j in range(1, 4):
        joined = splice(gu[j - 1], gu[j])
        put(1162 + j, 192, 4, joined[0:192])
        put_row(1930 + j, joined[192:193])
    put_row(1934, splice(gu[3][192:193], acc["down"][0, 0:1, :]))

    w0e, w1e = down(0, 0, 128, 2), down(1, 0, 128, 2)
    w0o, w1o = down(0, 1, 128, 2), down(1, 1, 128, 2)
    put(1935, 128, 3, splice(w0e, w1e))
    put(1936, 128, 3, w0o)
    put(1937, 128, 3, after(w1o, down(0, 2, 128, 2)))
    put_row(2319, splice(acc["down"][0, FF : FF + 1, :], acc["down"][1, FF : FF + 1, :]))


def scatter_blocks(flat, layer, blocks):
    for part in range(blocks.shape[0]):
        start = (145 * part) // 2
        blocks[part, layer] = flat[pl.ds(start, BLOCK), :].astype(BF16)


def norm(x, gain, bias):
    centre = x - jnp.sum(x, axis=0, keepdims=True) * (1.0 / D)
    variance = jnp.sum(centre * centre, axis=0, keepdims=True) * (1.0 / D)
    rstd = lax.rsqrt(variance + EPS)
    xhat = centre * rstd
    return xhat, rstd, (xhat * gain + bias).astype(BF16)


def norm_back(grad, xhat, rstd, gain):
    e = gain * grad
    mean_e = jnp.sum(e, axis=0, keepdims=True) * (1.0 / D)
    mean_ex = jnp.sum(e * xhat, axis=0, keepdims=True) * (1.0 / D)
    return rstd * (e - mean_e - xhat * mean_ex)


def fold(x):
    return x[:, 0:LANES] + x[:, LANES:]


def gelu_parts(gate):
    z = jnp.abs(gate) * (1.0 / math.sqrt(2.0))
    t = 1.0 / (1.0 + 0.3275911 * z)
    ex = jnp.exp(-z * z)
    poly = t * (
        0.254829592
        + t * (-0.284496736 + t * (1.421413741 + t * (-1.453152027 + t * 1.061405429)))
    )
    tail = 0.5 * poly * ex
    cdf = jnp.where(gate < 0.0, tail, 1.0 - tail)
    return cdf, cdf + gate * (ex * (1.0 / math.sqrt(2.0 * math.pi)))


def to_groups(x):
    n = x.shape[-1]
    x = x.reshape(2, GROUPS, GROUP, n)
    return jnp.concatenate([x[0][:, None], x[1][:, None]], axis=1).reshape(
        GROUPS, 2 * GROUP, n
    )


def from_groups(x):
    n = x.shape[-1]
    x = x.reshape(GROUPS, 2, GROUP, n)
    return jnp.concatenate([x[:, 0], x[:, 1]], axis=0).reshape(CHUNK, n)


def lanes_of(c):
    return pl.ds(pl.multiple_of(c * CHUNK, CHUNK), CHUNK)


def group_rows(c):
    return pl.ds(pl.multiple_of(c * 2 * GROUP, 2 * GROUP), 2 * GROUP)


def forward_qkv(s, w):
    gain, bias = wide(w["cols"][0]), wide(w["cols"][1])

    def step(c, carry):
        lanes = lanes_of(c)
        xhat, rstd, normed = norm(s["x"][:, lanes], gain, bias)
        s["xhat1"][:, lanes] = xhat
        s["rstd1"][:, lanes] = rstd
        s["h1"][0:D, lanes] = normed
        qkv = dot(s["h1"][:, lanes], w["qkv"][...], 0, 0)
        place = group_rows(c)
        s["q"][:, place, :] = to_groups(qkv[:, 0:D]).astype(BF16)
        for name, start in (("k", 256), ("v", 512)):
            part = qkv[:, start : start + D].reshape(2, GROUPS, GROUP, D)
            turned = jnp.concatenate(
                [
                    pltpu.roll(part[t], lax.rem(2 * c + t, GROUP), 1)[:, None]
                    for t in range(2)
                ],
                axis=1,
            )
            s[name][:, place, :] = turned.reshape(GROUPS, 2 * GROUP, D).astype(BF16)
        return carry

    lax.fori_loop(0, CHUNKS, step, 0)


def spread(values, masks):
    n = values.shape[1]
    doubled = [
        jnp.concatenate([values[8 * a : 8 * a + 8], values[8 * a : 8 * a + 8]], axis=0).astype(BF16)
        for a in range(3)
    ]
    parts = [doubled[a] * masks[m][:, 0:n] for a in range(2) for m in range(4)]
    parts.append(doubled[2] * masks[4][:, 0:n])
    return jnp.concatenate(parts, axis=0)


def collect(scores, diff):
    out = []
    for a in range(2):
        kept = scores[64 * a : 64 * a + 8]
        for j in range(1, 8):
            kept = jnp.where(diff == j, scores[64 * a + 8 * j : 64 * a + 8 * j + 8], kept)
        out.append(kept)
    out.append(scores[128:136])
    return out


def expand(rows, heads, out):
    for h in range(HEADS):
        out[h * LANES : (h + 1) * LANES, :] = rows[0:LANES] * heads[h, 0:1, :]
        out[HEADS * LANES + 16 * h : HEADS * LANES + 16 * h + 16, :] = (
            rows[LANES:GT] * heads[h, 0:1, :]
        )


def heads_joined(tiles):
    main = []
    for h in range(HEADS):
        tile = tiles[h // 2]
        start = (h % 2) * LANES
        main.append(tile[h * HEAD_DIM : (h + 1) * HEAD_DIM, start : start + LANES])
    main = jnp.concatenate(main, axis=0)
    last = tiles[4]
    head_of_row = lax.broadcasted_iota(jnp.int32, last.shape, 0) // HEAD_DIM
    head_of_lane = lax.broadcasted_iota(jnp.int32, last.shape, 1) // 16
    last = jnp.where(head_of_row == head_of_lane, last, 0.0)
    pad = jnp.zeros((64, LANES), F32)
    main = jnp.transpose(jnp.concatenate([main, pad], axis=0))[:, 0:D]
    last = jnp.transpose(jnp.concatenate([last, pad], axis=0))[:, 0:D]
    last = jnp.sum(last.reshape(HEADS, 16, D), axis=0)
    return main, last


TILES = ((0, 256), (256, 256), (512, 256), (768, 256), (1024, 128))


def forward_attention(s, env):
    diff = env["diff"][...]

    def step(g, carry):
        expand(s["q"][g], env["heads"], env["qx"])
        keys, values = s["k"][g], s["v"][g]
        count = env["count"][pl.ds(g, 1), :]
        tiles = []
        for start, n in TILES:
            scores = dot(keys, env["qx"][start : start + n, :], 1, 1)
            own = diff[:, 0:n]
            kept = collect(scores, own)
            limit = count[:, 0:n]
            slot = own.astype(F32)
            shown = [
                jnp.where(slot <= limit, kept[0] * SCALE, -1e9),
                jnp.where(slot + 8.0 <= limit, kept[1] * SCALE, -1e9),
                jnp.where(
                    own == 0, jnp.where(limit >= 16.0, kept[2] * SCALE, -1e9), -3e38
                ),
            ]
            top = jnp.max(
                jnp.maximum(jnp.maximum(shown[0], shown[1]), shown[2]), axis=0, keepdims=True
            )
            shown = [jnp.exp(part - top) for part in shown]
            total = jnp.sum(shown[0] + shown[1] + shown[2], axis=0, keepdims=True)
            inverse = 1.0 / total
            attention = jnp.concatenate([part * inverse for part in shown], axis=0)
            s["att"][g, :, start : start + n] = attention
            tiles.append(dot(values, spread(attention, env["masks"]), 0, 0))
        main, last = heads_joined(tiles)
        s["mixed"][g, 0:LANES, :] = main.astype(BF16)
        s["mixed"][g, LANES:GT, :] = last.astype(BF16)
        return carry

    lax.fori_loop(0, GROUPS, step, 0)


def forward_rest(s, w, done):
    gain, bias = wide(w["cols"][3]), wide(w["cols"][4])
    bias_out, bias_down = wide(w["cols"][2]), wide(w["cols"][5])

    def step(c, carry):
        lanes = lanes_of(c)
        mixed = from_groups(s["mixed"][:, group_rows(c), :].astype(F32)).astype(BF16)
        middle = s["x"][:, lanes] + (dot(w["out_t"][...], mixed, 1, 1) + bias_out)
        xhat, rstd, normed = norm(middle, gain, bias)
        s["xhat2"][:, lanes] = xhat
        s["rstd2"][:, lanes] = rstd
        s["h2"][0:D, lanes] = normed
        gate_up = dot(w["gu_t"][...], s["h2"][:, lanes], 1, 0)
        gate, up = gate_up[0:FF], gate_up[FF:]
        cdf, slope = gelu_parts(gate)
        gelu = gate * cdf
        act = (gelu * up).astype(BF16)
        s["act"][0:FF, lanes] = act
        s["gelu"][:, lanes] = gelu
        s["slope"][:, lanes] = slope * up
        result = middle + (dot(w["down_t"][...], act, 1, 0) + bias_down)
        done(c, lanes, result)
        return carry

    lax.fori_loop(0, CHUNKS, step, 0)


def add_tiles(ref, value):
    for j in range(ref.shape[0]):
        ref[j] += value[:, j * LANES : (j + 1) * LANES]


def add_narrow(ref, value):
    ref[0] += value[:, 0:LANES]
    ref[1, :, 0 : D - LANES] += value[:, LANES:D]


def backward_rest(s, w, acc, sums):
    gain = wide(w["cols"][3])

    def step(c, carry):
        lanes = lanes_of(c)
        grad = s["g"][:, lanes]
        branch = grad.astype(BF16)
        add_narrow(acc["down"], dot(s["act"][:, lanes], branch, 1, 1))
        d_act = dot(w["down"][...], branch, 1, 0)
        d_gate_up = jnp.concatenate(
            [d_act * s["slope"][:, lanes], d_act * s["gelu"][:, lanes]], axis=0
        ).astype(BF16)
        add_tiles(acc["gu"], dot(s["h2"][:, lanes], d_gate_up, 1, 1))
        d_normed = dot(w["gu"][...], d_gate_up, 1, 0)
        xhat = s["xhat2"][:, lanes]
        sums[2] += fold(d_normed * xhat)
        sums[3] += fold(d_normed)
        d_middle = grad + norm_back(d_normed, xhat, s["rstd2"][:, lanes], gain)
        s["g"][:, lanes] = d_middle
        d_attended = d_middle.astype(BF16)
        sums[4] += fold(d_attended.astype(F32))
        place = group_rows(c)
        s["dm"][:, place, :] = to_groups(dot(d_attended, w["out_t"][...], 0, 0)).astype(BF16)
        mixed = from_groups(s["mixed"][:, place, :].astype(F32)).astype(BF16)
        acc["out_t"][...] += dot(d_attended, mixed, 1, 0)
        return carry

    lax.fori_loop(0, CHUNKS, step, 0)


def backward_attention(s, env):
    diff = env["diff"][...]

    def step(g, carry):
        expand(s["q"][g], env["heads"], env["qx"])
        expand(s["dm"][g], env["heads"], env["dx"])
        keys, values = s["k"][g], s["v"][g]
        tiles = []
        d_values = jnp.zeros((GT, D), F32)
        d_keys = jnp.zeros((GT, D), F32)
        for start, n in TILES:
            d_mixed = env["dx"][start : start + n, :]
            kept = jnp.concatenate(collect(dot(values, d_mixed, 1, 1), diff[:, 0:n]), axis=0)
            attention = s["att"][g, :, start : start + n]
            weighted = attention * kept
            total = jnp.sum(weighted, axis=0, keepdims=True)
            d_score = spread(weighted - attention * total, env["masks"])
            d_values += dot(spread(attention, env["masks"]), d_mixed, 1, 0)
            d_keys += dot(d_score, env["qx"][start : start + n, :], 1, 0)
            tiles.append(dot(keys, d_score, 0, 0))
        main, last = heads_joined(tiles)
        s["dqkv"][g, 0:LANES, 0:D] = (main * SCALE).astype(BF16)
        s["dqkv"][g, LANES:GT, 0:D] = (last * SCALE).astype(BF16)
        for value, start, scale in ((d_keys, 256, SCALE), (d_values, 512, 1.0)):
            slots = value.reshape(SLOTS, GROUP, D)
            turned = [
                slots[k] if k % GROUP == 0 else pltpu.roll(slots[k], GROUP - k % GROUP, 0)
                for k in range(SLOTS)
            ]
            s["dqkv"][g, :, start : start + D] = (jnp.concatenate(turned, axis=0) * scale).astype(
                BF16
            )
        return carry

    lax.fori_loop(0, GROUPS, step, 0)


def backward_qkv(s, w, acc, sums, done):
    gain = wide(w["cols"][0])

    def step(c, carry):
        lanes = lanes_of(c)
        d_qkv = from_groups(s["dqkv"][:, group_rows(c), :].astype(F32)).astype(BF16)
        add_tiles(acc["qkv"], dot(s["h1"][:, lanes], d_qkv, 1, 0))
        d_normed = dot(w["qkv"][0:D, :], d_qkv, 1, 1)
        xhat = s["xhat1"][:, lanes]
        sums[0] += fold(d_normed * xhat)
        sums[1] += fold(d_normed)
        done(
            c, lanes, s["g"][:, lanes] + norm_back(d_normed, xhat, s["rstd1"][:, lanes], gain)
        )
        return carry

    lax.fori_loop(0, CHUNKS, step, 0)


def per_layer():
    return {
        "x": ((D, TOKENS), F32),
        "xhat1": ((D, TOKENS), F32),
        "rstd1": ((1, TOKENS), F32),
        "h1": ((D + 16, TOKENS), BF16),
        "q": ((GROUPS, GT, D), BF16),
        "k": ((GROUPS, GT, D), BF16),
        "v": ((GROUPS, GT, D), BF16),
        "att": ((GROUPS, 24, QL), F32),
        "mixed": ((GROUPS, GT, D), BF16),
        "xhat2": ((D, TOKENS), F32),
        "rstd2": ((1, TOKENS), F32),
        "h2": ((D + 16, TOKENS), BF16),
        "act": ((FF + 16, TOKENS), BF16),
        "gelu": ((FF, TOKENS), F32),
        "slope": ((FF, TOKENS), F32),
    }


def weights():
    return {
        "cols": ((6, D, LANES), F32),
        "qkv": ((D + 16, 6 * LANES), BF16),
        "out_t": ((D, D), BF16),
        "gu": ((D, 2 * FF), BF16),
        "gu_t": ((2 * FF, D + 16), BF16),
        "down": ((FF, D), BF16),
        "down_t": ((D, FF), BF16),
    }


def accumulators():
    return {
        "qkv": ((6, D + 16, LANES), F32),
        "out_t": ((D, D), F32),
        "gu": ((4, D + 16, LANES), F32),
        "down": ((2, FF + 16, LANES), F32),
    }


def common():
    return {
        "qx": ((QL, D), BF16),
        "dx": ((QL, D), BF16),
        "heads": ((HEADS, 16, D), BF16),
        "masks": ((5, 16, CHUNK), BF16),
        "diff": ((GROUP, CHUNK), jnp.int32),
        "count": ((GROUPS, CHUNK), F32),
        "dm": ((GROUPS, GT, D), BF16),
        "dqkv": ((GROUPS, GT, 6 * LANES), BF16),
        "g": ((D, TOKENS), F32),
        "sums": ((5, D, LANES), F32),
        "flat": ((FLAT + 8, LANES), F32),
        "tmp": ((6, FF, LANES), F32),
    }


def make_scratch():
    shapes, names = [], []
    for prefix, table in (
        ("common", common()),
        ("acc", accumulators()),
        ("s0", per_layer()),
        ("s1", per_layer()),
        ("w0", weights()),
        ("w1", weights()),
    ):
        for name, (shape, kind) in table.items():
            names.append((prefix, name))
            shapes.append(pltpu.VMEM(shape, kind))
    return names, shapes


def init_env(env, count):
    lane = lax.broadcasted_iota(jnp.int32, (GROUP, CHUNK), 1)
    sub = lax.broadcasted_iota(jnp.int32, (GROUP, CHUNK), 0)
    diff = (sub - lane) & (GROUP - 1)
    env["diff"][...] = diff
    for m in range(5):
        first = jnp.where(diff == (2 * m) % 8, 1.0, 0.0)
        second = jnp.where(diff == 2 * m + 1, 1.0, 0.0)
        env["masks"][m] = jnp.concatenate([first, second], axis=0).astype(BF16)
    feature = lax.broadcasted_iota(jnp.int32, (16, D), 1) // HEAD_DIM
    for h in range(HEADS):
        env["heads"][h] = jnp.where(feature == h, 1.0, 0.0).astype(BF16)
    row = lax.broadcasted_iota(jnp.int32, (GROUPS, LANES), 1)
    group = lax.broadcasted_iota(jnp.int32, (GROUPS, LANES), 0)
    mine = jnp.where(row // GROUP == group, jnp.broadcast_to(count, (GROUPS, LANES)), 0.0)
    here = lax.broadcasted_iota(jnp.int32, (LANES, CHUNK), 0)
    there = lax.broadcasted_iota(jnp.int32, (LANES, CHUNK), 1)
    pick = jnp.where(here % GROUP == there % GROUP, 1.0, 0.0).astype(BF16)
    env["count"][...] = dot(mine.astype(BF16), pick, 1, 0)


def ones_below(ref, rows):
    tail = ref.shape[0] - rows
    mark = lax.broadcasted_iota(jnp.int32, (tail, ref.shape[1]), 0) == 0
    ref[rows:, :] = jnp.where(mark, 1.0, 0.0).astype(BF16)


def kernel(names, tokens, out_grad, blocks, row_scale, count, out, in_grad, grads, *scratch):
    table = {}
    for (prefix, name), ref in zip(names, scratch):
        table.setdefault(prefix, {})[name] = ref
    env, acc = table["common"], table["acc"]
    s, w = [table["s0"], table["s1"]], [table["w0"], table["w1"]]
    sums = env["sums"]

    init_env(env, count[...])
    valid_slots = count[...]
    env["dqkv"][...] = jnp.zeros_like(env["dqkv"])
    for layer in range(LAYERS):
        ones_below(s[layer]["h1"], D)
        ones_below(s[layer]["h2"], D)
        ones_below(s[layer]["act"], FF)
        gather_flat(blocks, layer, env["flat"])
        unpack(env["flat"], w[layer], env["tmp"])
    for slot in range(SLOTS):
        lanes = slice(slot * ROWS, (slot + 1) * ROWS)
        if slot < SEQ:
            s[0]["x"][:, lanes] = tokens[slot].astype(F32)
            keep = jnp.where(valid_slots >= float(slot), row_scale[...], 0.0)
            env["g"][:, lanes] = out_grad[slot].astype(F32) * keep
        else:
            s[0]["x"][:, lanes] = jnp.zeros((D, ROWS), F32)
            env["g"][:, lanes] = jnp.zeros((D, ROWS), F32)

    def put(target):
        def done(c, lanes, value):
            target[2 * c] = value[:, 0:ROWS]

            @pl.when(c < CHUNKS - 1)
            def _():
                target[2 * c + 1] = value[:, ROWS:]

        return done

    def keep(target):
        def done(c, lanes, value):
            target[:, lanes] = value

        return done

    for layer in range(LAYERS):
        forward_qkv(s[layer], w[layer])
        forward_attention(s[layer], env)
        last = layer == LAYERS - 1
        forward_rest(s[layer], w[layer], put(out) if last else keep(s[layer + 1]["x"]))
    for layer in reversed(range(LAYERS)):
        sums[...] = jnp.zeros_like(sums)
        for ref in acc.values():
            ref[...] = jnp.zeros_like(ref)
        state = dict(s[layer], g=env["g"], dm=env["dm"], dqkv=env["dqkv"])
        backward_rest(state, w[layer], acc, sums)
        backward_attention(state, env)
        backward_qkv(
            state, w[layer], acc, sums, put(in_grad) if layer == 0 else keep(env["g"])
        )
        pack(env["flat"], acc, sums, env["tmp"])
        scatter_blocks(env["flat"], layer, grads)


def run_kernel(tokens, out_grad, blocks, row_scale, count):
    names, scratch = make_scratch()
    full = jax.ShapeDtypeStruct((SEQ, D, ROWS), F32)

    def body(*refs):
        kernel(names, *refs)

    return pl.pallas_call(
        body,
        out_shape=(full, full, jax.ShapeDtypeStruct(blocks.shape, BF16)),
        in_specs=[pl.BlockSpec(memory_space=pltpu.VMEM)] * 5,
        out_specs=[pl.BlockSpec(memory_space=pltpu.VMEM)] * 3,
        scratch_shapes=scratch,
        compiler_params=pltpu.CompilerParams(vmem_limit_bytes=64 * 1024 * 1024 - 256 * 1024),
    )(tokens, out_grad, blocks, row_scale, count)


AXES = ("dp", "fsdp")


def flat_to_blocks(flat):
    rows = jnp.pad(flat.reshape(LAYERS, FLAT, LANES), ((0, 0), (0, BLOCK), (0, 0)))
    starts = [(145 * part) // 2 for part in range(PARTS)]
    return jnp.stack([rows[:, start : start + BLOCK] for start in starts])


def blocks_to_flat(blocks):
    joined = []
    for pair in range(PARTS // 2):
        first, second = blocks[2 * pair], blocks[2 * pair + 1]
        seam = jnp.concatenate([first[:, 72:73, 0:64], second[:, 0:1, 64:]], axis=2)
        joined += [first[:, 0:72], seam, second[:, 1:73]]
    return jnp.concatenate(joined, axis=1).reshape(LAYERS, PSIZE)


def gather_params(flat_params):
    parts = lax.axis_size(AXES)
    if parts != PARTS:
        return flat_to_blocks(lax.all_gather(flat_params, AXES, axis=1, tiled=True))
    size = flat_params.shape[1]
    room = BLOCK * LANES - size
    padded = jnp.where(
        lax.axis_index("fsdp") % 2 == 0,
        jnp.pad(flat_params, ((0, 0), (0, room))),
        jnp.pad(flat_params, ((0, 0), (64, room - 64))),
    ).reshape(LAYERS, BLOCK, LANES)
    return lax.all_gather(padded, AXES, axis=0, tiled=False)


def reduce_grads(grads, size):
    parts = lax.axis_size(AXES)
    if parts != PARTS:
        return lax.psum_scatter(
            blocks_to_flat(grads.astype(F32)), AXES, scatter_dimension=1, tiled=True
        )
    got = lax.all_to_all(grads, AXES, 0, 0, tiled=True)
    total = jnp.sum(got.astype(F32), axis=0).reshape(LAYERS, BLOCK * LANES)
    return jnp.where(
        lax.axis_index("fsdp") % 2 == 0, total[:, 0:size], total[:, 64 : 64 + size]
    )


def body(tokens, out_grad, flat_params, feat_count, table_ids, table_counts):
    counts_float = table_counts.astype(F32)
    table_index = jnp.arange(table_counts.shape[0], dtype=jnp.int32)
    match = (table_ids[None, :] == table_index[:, None]).astype(F32)
    row_count = jnp.sum(match * counts_float[:, None], axis=0)
    row_scale = jnp.sqrt(jnp.mean(counts_float) / row_count)[None, :]
    count = feat_count.astype(F32)[None, :]
    blocks = gather_params(flat_params)
    turned = jnp.transpose(tokens, (1, 2, 0))
    turned_grad = jnp.transpose(out_grad, (1, 2, 0))
    results = [
        run_kernel(
            turned[:, :, at : at + ROWS],
            turned_grad[:, :, at : at + ROWS],
            blocks,
            row_scale[:, at : at + ROWS],
            count[:, at : at + ROWS],
        )
        for at in range(0, tokens.shape[0], ROWS)
    ]
    out, in_grad, grads = results[0]
    if len(results) > 1:
        out = jnp.concatenate([r[0] for r in results], axis=2)
        in_grad = jnp.concatenate([r[1] for r in results], axis=2)
        grads = sum(r[2].astype(F32) for r in results).astype(BF16)
    return (
        jnp.transpose(out, (2, 0, 1)),
        jnp.transpose(in_grad, (2, 0, 1)),
        reduce_grads(grads, flat_params.shape[1]),
    )


def solution(mesh):
    rows = P(AXES, None, None)
    placed = (rows, rows, P(None, AXES), P(AXES), P(AXES), P())
    return jax.shard_map(
        body,
        mesh=mesh,
        in_specs=placed,
        out_specs=(rows, rows, P(None, AXES)),
        check_vma=False,
    )
```

time: 1100 us -> 254 us (0.23); the launches traced: 1090 us -> 254 us
  local copies, waits for them, and re-layouts: 510 us -> 0.67 us
  matrix products: 281 us -> 0 us
  waiting for transfers between devices: 236 us -> 54.6 us
  Pallas kernels: 0 us -> 141 us
  other arithmetic: 44.5 us -> 6.36 us
  blocking collectives: 0 us -> 36.8 us
    dot_general x36 -> x0, matrix products: 281 us -> none  [the longest x2 49.3 us: layer_pass(): jnp.einsum('rqhd,rkhd->rhqk', query_heads, key_heads, preferred_element_t...]
    unnamed x4 -> x1, waiting for transfers between devices: 236 us -> 0.02 us
    reshape x36 -> x0, local copies, waits for them, and re-layouts: 216 us -> none  [the longest x4 52.8 us: layer_pass(): value_heads = value_part.reshape(head_shape)]
    pallas_call x0 -> x1, Pallas kernels: none -> 141 us  [run_kernel(): pl.pallas_call(body, out_shape=(full, full, jax.ShapeDtypeStruct(blocks.s...]
    convert_element_type x13 -> x0, local copies, waits for them, and re-layouts: 88.3 us -> none  [the longest x4 32.5 us: layer_pass(): mixed_heads.reshape(batch_rows * slot_count, model_width)]
    all_gather x0 -> x1, waiting for transfers between devices: none -> 54.6 us  [gather_params(): return lax.all_gather(padded, AXES, axis=0, tiled=False)]
    concatenate x2 -> x0, local copies, waits for them, and re-layouts: 50.6 us -> none  [pack_gradients(): joined = jnp.concatenate(pieces)]
    mul x5 -> x0, local copies, waits for them, and re-layouts: 43.5 us -> none  [the longest x2 20.6 us: layer_back(): jnp.einsum('rhqk,rkhd->rqhd', d_scores_low, kept['key_heads'], preferred_...]
  transfers between devices with their start and end apart: 2 -> 1, of which waited for: 2 -> 1; matrix products, arithmetic and copies ran while one was open for 3% -> 2% of each run, Pallas kernels for 0% -> 0%
where the time goes in v1:
time: 254 us
  Pallas kernels  141 us (56%)
  waiting for transfers between devices  54.6 us (21%)
  blocking collectives  36.8 us (14%)
  between operations  14.7 us (6%)
  other arithmetic  6.36 us (3%)
    pallas_call x1, Pallas kernels, run_kernel(): pl.pallas_call(body, out_shape=(full, full, jax.ShapeDtypeStruct(blocks.s...  141 us
    all_gather x1, waiting for transfers between devices, gather_params(): return lax.all_gather(padded, AXES, axis=0, tiled=False)  54.6 us
    all_to_all x1, blocking collectives, reduce_grads(): got = lax.all_to_all(grads, AXES, 0, 0, tiled=True)  36.8 us
  transfers between devices with their start and end apart: 1, of which 1 were waited for; matrix products, arithmetic and copies ran while one was open for 2% of the time, Pallas kernels for 0%

profile of v1, /device:TPU:0, one launch (start us, length us, event | category | flops | bytes accessed | tf_op | source)
XLA Modules:
  0.0 253.9 jit_solution(6750808163660048311)
XLA Ops:
  7.2 0.0 all-gather.2.cloned.1.call-start
  7.2 1.0 fusion
  8.2 0.6 copy.14
  8.8 0.0 all-gather.2.cloned.1.call-update
  8.8 0.7 convert_element_type.14
  9.5 1.3 convert_reduce_fusion.1
  11.4 0.7 select_reduce_fusion
  12.2 1.2 convert_bitcast_fusion.refs_4_
  13.4 0.5 sqrt_bitcast_fusion.refs_3_
  13.9 54.6 %all-gather.2.cloned.1.call-done.refs_2_ = bf16[32,2,80,128]{3,2,1,0:T(8,128)(2,1)} async-done(((bf16[1,2,80,128]{3,2,1,0:T(8,128)(2,1)}), bf16[32,2,80,128]{3,2,1,0:T(8,128)(2,1)}) %all-gather.2.cloned.1.call-update) | async-done | bytes 1310736 | tf_op jit(solution)/shard_map/all_gather | solution.py:741
  68.5 140.7 %shard_map.85 = (f32[17,192,128]{2,1,0:T(8,128)}, f32[17,192,128]{2,1,0:T(8,128)}, bf16[32,2,80,128]{3,2,1,0:T(8,128)(2,1)}) custom-call(bf16[17,192,128]{2,1,0:T(8,128)(2,1)} %bitcast.18, bf16[17,192,128]{2,1,0:T(8,128)(2,1)} %bitcast.19, bf16[32,2,80,128]{3,2,1,0:T(8,128)(2,1)} %all-gather.2.cloned.1.call-done.refs_2_, f32[1,128]{1,0:T(1,128)} %sqrt_bitcast_fusion.refs_3_, ...), custom_call_target="tpu_custom_call" | custom-call | tf_op jit(solution)/shard_map/pallas_call | solution.py:702
  209.2 36.8 %all_to_all.5 = bf16[32,2,80,128]{3,2,1,0:T(8,128)(2,1)S(1)} all-to-all(bf16[32,2,80,128]{3,2,1,0:T(8,128)(2,1)} %get-tuple-element.8), channel_id=1, replica_groups=mesh['dp'=8,'fsdp'=4] {'dp','fsdp'}, dimensions={0} | all-to-all | bytes 2621440 | tf_op jit(solution)/shard_map/all_to_all | solution.py:750
  246.0 0.2 convert_reduce_fusion
  246.2 0.8 slice_select_fusion
  (1 shorter events, 0.0 us)
Async XLA Ops:
  7.2 61.4 %all-gather.2.cloned.1.call-start = ((), (), s32[]{:S(2)}) async-start(), calls=%async_computation.1 | async-start | bytes 1351680 | tf_op jit(solution)/shard_map/all_gather | solution.py:741
Sparse Core Ops, SparseCore 0:
  11.4 57.0 all-gather.1

commit v2 on v1

--- a/solution.py
+++ b/solution.py
@@ -17,6 +17,9 @@
 ROWS = 128
 SLOTS = 18
 LANES = 128
+UNROLL = 4
+DEPTH = 6
+STEPS = 3
 GROUP = 8
 GROUPS = ROWS // GROUP
 GT = SLOTS * GROUP
@@ -256,16 +259,10 @@
 
 
 def gelu_parts(gate):
-    z = jnp.abs(gate) * (1.0 / math.sqrt(2.0))
-    t = 1.0 / (1.0 + 0.3275911 * z)
-    ex = jnp.exp(-z * z)
-    poly = t * (
-        0.254829592
-        + t * (-0.284496736 + t * (1.421413741 + t * (-1.453152027 + t * 1.061405429)))
-    )
-    tail = 0.5 * poly * ex
-    cdf = jnp.where(gate < 0.0, tail, 1.0 - tail)
-    return cdf, cdf + gate * (ex * (1.0 / math.sqrt(2.0 * math.pi)))
+    z = gate * (1.0 / math.sqrt(2.0))
+    cdf = 0.5 * lax.erf(z) + 0.5
+    bell = jnp.exp2(z * z * (-1.0 / math.log(2.0)))
+    return cdf, cdf + (z * bell) * (1.0 / math.sqrt(math.pi))
 
 
 def to_groups(x):
@@ -290,16 +287,31 @@
     return pl.ds(pl.multiple_of(c * 2 * GROUP, 2 * GROUP), 2 * GROUP)
 
 
+def skewed(stages):
+    def steps(i, carry):
+        held = {}
+        for tick in range(STEPS + len(stages) - 1):
+            for j, stage in enumerate(stages):
+                u = tick - j
+                if 0 <= u < STEPS:
+                    held[u] = stage(i * STEPS + u, held.get(u))
+        return carry
+
+    lax.fori_loop(0, CHUNKS // STEPS, steps, 0)
+
+
 def forward_qkv(s, w):
     gain, bias = wide(w["cols"][0]), wide(w["cols"][1])
 
-    def step(c, carry):
+    def project(c, _):
         lanes = lanes_of(c)
         xhat, rstd, normed = norm(s["x"][:, lanes], gain, bias)
         s["xhat1"][:, lanes] = xhat
         s["rstd1"][:, lanes] = rstd
         s["h1"][0:D, lanes] = normed
-        qkv = dot(s["h1"][:, lanes], w["qkv"][...], 0, 0)
+        return dot(s["h1"][:, lanes], w["qkv"][...], 0, 0)
+
+    def keep(c, qkv):
         place = group_rows(c)
         s["q"][:, place, :] = to_groups(qkv[:, 0:D]).astype(BF16)
         for name, start in (("k", 256), ("v", 512)):
@@ -312,9 +324,8 @@
                 axis=1,
             )
             s[name][:, place, :] = turned.reshape(GROUPS, 2 * GROUP, D).astype(BF16)
-        return carry
-
-    lax.fori_loop(0, CHUNKS, step, 0)
+
+    skewed((project, keep))
 
 
 def spread(values, masks):
@@ -328,97 +339,163 @@
     return jnp.concatenate(parts, axis=0)
 
 
-def collect(scores, diff):
+def collect(scores, bits):
+    n = scores.shape[1]
+    bits = [bit[:, 0:n] for bit in bits]
     out = []
     for a in range(2):
-        kept = scores[64 * a : 64 * a + 8]
-        for j in range(1, 8):
-            kept = jnp.where(diff == j, scores[64 * a + 8 * j : 64 * a + 8 * j + 8], kept)
-        out.append(kept)
+        level = [scores[64 * a + 8 * j : 64 * a + 8 * j + 8] for j in range(8)]
+        for bit in bits:
+            level = [
+                jnp.where(bit, level[2 * i + 1], level[2 * i]) for i in range(len(level) // 2)
+            ]
+        out.append(level[0])
     out.append(scores[128:136])
     return out
 
 
-def expand(rows, heads, out):
-    for h in range(HEADS):
-        out[h * LANES : (h + 1) * LANES, :] = rows[0:LANES] * heads[h, 0:1, :]
-        out[HEADS * LANES + 16 * h : HEADS * LANES + 16 * h + 16, :] = (
-            rows[LANES:GT] * heads[h, 0:1, :]
-        )
-
-
-def heads_joined(tiles):
+def blocks_of(turned, t, halves):
+    first = turned[48 * t : 48 * t + 16]
+    middle = turned[48 * t + 16 : 48 * t + 32]
+    last = turned[48 * t + 32 : 48 * t + 48]
+    none = jnp.zeros_like(first)
+    return jnp.concatenate(
+        [
+            jnp.concatenate([first, none], axis=1),
+            jnp.concatenate([middle * halves[0], middle * halves[1]], axis=1),
+            jnp.concatenate([none, last], axis=1),
+        ],
+        axis=0,
+    )
+
+
+def padded(block, t):
+    parts = [block]
+    if t > 0:
+        parts.insert(0, jnp.zeros((48 * t, block.shape[1]), BF16))
+    if t < 3:
+        parts.append(jnp.zeros((48 * (3 - t), block.shape[1]), BF16))
+    return jnp.concatenate(parts, axis=0)
+
+
+def tail_of(rows, heads):
+    return jnp.transpose(
+        jnp.concatenate([rows * heads[h, 0:1, :] for h in range(HEADS)], axis=0)
+    )
+
+
+def heads_joined(tiles, tail, heads, scale=None):
     main = []
-    for h in range(HEADS):
-        tile = tiles[h // 2]
-        start = (h % 2) * LANES
-        main.append(tile[h * HEAD_DIM : (h + 1) * HEAD_DIM, start : start + LANES])
+    for tile in tiles:
+        main += [tile[0:HEAD_DIM, 0:LANES], tile[HEAD_DIM:, LANES:]]
     main = jnp.concatenate(main, axis=0)
-    last = tiles[4]
-    head_of_row = lax.broadcasted_iota(jnp.int32, last.shape, 0) // HEAD_DIM
-    head_of_lane = lax.broadcasted_iota(jnp.int32, last.shape, 1) // 16
-    last = jnp.where(head_of_row == head_of_lane, last, 0.0)
-    pad = jnp.zeros((64, LANES), F32)
-    main = jnp.transpose(jnp.concatenate([main, pad], axis=0))[:, 0:D]
-    last = jnp.transpose(jnp.concatenate([last, pad], axis=0))[:, 0:D]
-    last = jnp.sum(last.reshape(HEADS, 16, D), axis=0)
+    if scale is not None:
+        main, tail = main * scale, tail * scale
+    main = jnp.transpose(main.astype(BF16))
+    tail = jnp.transpose(tail.astype(BF16))
+    last = tail[0:16] * heads[0, 0:1, :]
+    for h in range(1, HEADS):
+        last += tail[16 * h : 16 * h + 16] * heads[h, 0:1, :]
     return main, last
 
 
-TILES = ((0, 256), (256, 256), (512, 256), (768, 256), (1024, 128))
+def softmax(kept, diff, limit):
+    n = kept[0].shape[1]
+    own = diff[:, 0:n]
+    limit = limit[:, 0:n]
+    slot = own.astype(F32)
+    shown = [
+        jnp.where(slot <= limit, kept[0] * SCALE, -1e9),
+        jnp.where(slot + 8.0 <= limit, kept[1] * SCALE, -1e9),
+        jnp.where(own == 0, jnp.where(limit >= 16.0, kept[2] * SCALE, -1e9), -3e38),
+    ]
+    top = jnp.max(jnp.maximum(jnp.maximum(shown[0], shown[1]), shown[2]), axis=0, keepdims=True)
+    shown = [jnp.exp(part - top) for part in shown]
+    inverse = 1.0 / jnp.sum(shown[0] + shown[1] + shown[2], axis=0, keepdims=True)
+    return jnp.concatenate([part * inverse for part in shown], axis=0)
+
+
+def staged(items, first, second):
+    waiting = []
+    for item in items:
+        waiting.append((item, first(item)))
+        if len(waiting) > DEPTH:
+            second(*waiting.pop(0))
+    for entry in waiting:
+        second(*entry)
 
 
 def forward_attention(s, env):
     diff = env["diff"][...]
-
-    def step(g, carry):
-        expand(s["q"][g], env["heads"], env["qx"])
-        keys, values = s["k"][g], s["v"][g]
-        count = env["count"][pl.ds(g, 1), :]
-        tiles = []
-        for start, n in TILES:
-            scores = dot(keys, env["qx"][start : start + n, :], 1, 1)
-            own = diff[:, 0:n]
-            kept = collect(scores, own)
-            limit = count[:, 0:n]
-            slot = own.astype(F32)
-            shown = [
-                jnp.where(slot <= limit, kept[0] * SCALE, -1e9),
-                jnp.where(slot + 8.0 <= limit, kept[1] * SCALE, -1e9),
-                jnp.where(
-                    own == 0, jnp.where(limit >= 16.0, kept[2] * SCALE, -1e9), -3e38
-                ),
-            ]
-            top = jnp.max(
-                jnp.maximum(jnp.maximum(shown[0], shown[1]), shown[2]), axis=0, keepdims=True
-            )
-            shown = [jnp.exp(part - top) for part in shown]
-            total = jnp.sum(shown[0] + shown[1] + shown[2], axis=0, keepdims=True)
-            inverse = 1.0 / total
-            attention = jnp.concatenate([part * inverse for part in shown], axis=0)
-            s["att"][g, :, start : start + n] = attention
-            tiles.append(dot(values, spread(attention, env["masks"]), 0, 0))
-        main, last = heads_joined(tiles)
-        s["mixed"][g, 0:LANES, :] = main.astype(BF16)
-        s["mixed"][g, LANES:GT, :] = last.astype(BF16)
+    bits = [(diff & (1 << i)) != 0 for i in range(3)]
+    halves = [env["halves"][i] for i in range(2)]
+
+    def step(i, carry):
+        state = {}
+
+        def load(u):
+            g = i * UNROLL + u
+            queries, values = s["q"][g], s["v"][g]
+            state[u] = {
+                "g": g,
+                "queries": queries,
+                "keys": s["k"][g],
+                "turned": jnp.transpose(queries)[:, 0:LANES],
+                "values": jnp.transpose(values),
+                "count": env["count"][pl.ds(g, 1), :],
+                "tiles": [],
+            }
+
+        def scores(item):
+            u, t = item
+            if t == 0:
+                load(u)
+            at = state[u]
+            if t < 4:
+                right = padded(blocks_of(at["turned"], t, halves), t)
+            else:
+                right = tail_of(at["queries"][LANES:GT], env["heads"])
+            return dot(at["keys"], right, 1, 0)
+
+        def mix(item, products):
+            u, t = item
+            at = state[u]
+            attention = softmax(collect(products, bits), diff, at["count"])
+            s["att"][at["g"], :, t * CHUNK : min((t + 1) * CHUNK, QL)] = attention
+            low = spread(attention, env["masks"])
+            left = at["values"][48 * t : 48 * t + 48] if t < 4 else at["values"]
+            at["tiles"].append(dot(left, low, 1, 0))
+            if t == 4:
+                main, last = heads_joined(at["tiles"][0:4], at["tiles"][4], env["heads"])
+                s["mixed"][at["g"], 0:LANES, :] = main
+                s["mixed"][at["g"], LANES:GT, :] = last
+
+        staged([(u, t) for u in range(UNROLL) for t in range(5)], scores, mix)
         return carry
 
-    lax.fori_loop(0, GROUPS, step, 0)
+    lax.fori_loop(0, GROUPS // UNROLL, step, 0)
 
 
 def forward_rest(s, w, done):
     gain, bias = wide(w["cols"][3]), wide(w["cols"][4])
     bias_out, bias_down = wide(w["cols"][2]), wide(w["cols"][5])
 
-    def step(c, carry):
+    def attended(c, _):
+        mixed = from_groups(s["mixed"][:, group_rows(c), :].astype(F32)).astype(BF16)
+        return dot(w["out_t"][...], mixed, 1, 1)
+
+    def normed(c, product):
         lanes = lanes_of(c)
-        mixed = from_groups(s["mixed"][:, group_rows(c), :].astype(F32)).astype(BF16)
-        middle = s["x"][:, lanes] + (dot(w["out_t"][...], mixed, 1, 1) + bias_out)
-        xhat, rstd, normed = norm(middle, gain, bias)
+        middle = s["x"][:, lanes] + (product + bias_out)
+        xhat, rstd, low = norm(middle, gain, bias)
+        s["middle"][:, lanes] = middle
         s["xhat2"][:, lanes] = xhat
         s["rstd2"][:, lanes] = rstd
-        s["h2"][0:D, lanes] = normed
-        gate_up = dot(w["gu_t"][...], s["h2"][:, lanes], 1, 0)
+        s["h2"][0:D, lanes] = low
+        return dot(w["gu_t"][...], s["h2"][:, lanes], 1, 0)
+
+    def gated(c, gate_up):
+        lanes = lanes_of(c)
         gate, up = gate_up[0:FF], gate_up[FF:]
         cdf, slope = gelu_parts(gate)
         gelu = gate * cdf
@@ -426,11 +503,13 @@
         s["act"][0:FF, lanes] = act
         s["gelu"][:, lanes] = gelu
         s["slope"][:, lanes] = slope * up
-        result = middle + (dot(w["down_t"][...], act, 1, 0) + bias_down)
-        done(c, lanes, result)
-        return carry
-
-    lax.fori_loop(0, CHUNKS, step, 0)
+        return dot(w["down_t"][...], act, 1, 0)
+
+    def finish(c, product):
+        lanes = lanes_of(c)
+        done(c, lanes, s["middle"][:, lanes] + (product + bias_down))
+
+    skewed((attended, normed, gated, finish))
 
 
 def add_tiles(ref, value):
@@ -446,87 +525,138 @@
 def backward_rest(s, w, acc, sums):
     gain = wide(w["cols"][3])
 
-    def step(c, carry):
+    def down(c, _):
         lanes = lanes_of(c)
-        grad = s["g"][:, lanes]
-        branch = grad.astype(BF16)
-        add_narrow(acc["down"], dot(s["act"][:, lanes], branch, 1, 1))
-        d_act = dot(w["down"][...], branch, 1, 0)
+        branch = s["g"][:, lanes].astype(BF16)
+        return dot(s["act"][:, lanes], branch, 1, 1), dot(w["down"][...], branch, 1, 0)
+
+    def gate_up(c, held):
+        lanes = lanes_of(c)
+        grad_down, d_act = held
+        add_narrow(acc["down"], grad_down)
         d_gate_up = jnp.concatenate(
             [d_act * s["slope"][:, lanes], d_act * s["gelu"][:, lanes]], axis=0
         ).astype(BF16)
-        add_tiles(acc["gu"], dot(s["h2"][:, lanes], d_gate_up, 1, 1))
-        d_normed = dot(w["gu"][...], d_gate_up, 1, 0)
+        return dot(s["h2"][:, lanes], d_gate_up, 1, 1), dot(w["gu"][...], d_gate_up, 1, 0)
+
+    def normed(c, held):
+        lanes = lanes_of(c)
+        grad_gu, d_normed = held
+        add_tiles(acc["gu"], grad_gu)
         xhat = s["xhat2"][:, lanes]
         sums[2] += fold(d_normed * xhat)
         sums[3] += fold(d_normed)
-        d_middle = grad + norm_back(d_normed, xhat, s["rstd2"][:, lanes], gain)
+        d_middle = s["g"][:, lanes] + norm_back(d_normed, xhat, s["rstd2"][:, lanes], gain)
         s["g"][:, lanes] = d_middle
         d_attended = d_middle.astype(BF16)
         sums[4] += fold(d_attended.astype(F32))
-        place = group_rows(c)
-        s["dm"][:, place, :] = to_groups(dot(d_attended, w["out_t"][...], 0, 0)).astype(BF16)
-        mixed = from_groups(s["mixed"][:, place, :].astype(F32)).astype(BF16)
-        acc["out_t"][...] += dot(d_attended, mixed, 1, 0)
-        return carry
-
-    lax.fori_loop(0, CHUNKS, step, 0)
+        mixed = from_groups(s["mixed"][:, group_rows(c), :].astype(F32)).astype(BF16)
+        return dot(d_attended, w["out_t"][...], 0, 0), dot(d_attended, mixed, 1, 0)
+
+    def finish(c, held):
+        d_mixed, grad_out = held
+        s["dm"][:, group_rows(c), :] = to_groups(d_mixed).astype(BF16)
+        acc["out_t"][...] += grad_out
+
+    skewed((down, gate_up, normed, finish))
 
 
 def backward_attention(s, env):
     diff = env["diff"][...]
-
-    def step(g, carry):
-        expand(s["q"][g], env["heads"], env["qx"])
-        expand(s["dm"][g], env["heads"], env["dx"])
-        keys, values = s["k"][g], s["v"][g]
-        tiles = []
-        d_values = jnp.zeros((GT, D), F32)
-        d_keys = jnp.zeros((GT, D), F32)
-        for start, n in TILES:
-            d_mixed = env["dx"][start : start + n, :]
-            kept = jnp.concatenate(collect(dot(values, d_mixed, 1, 1), diff[:, 0:n]), axis=0)
-            attention = s["att"][g, :, start : start + n]
-            weighted = attention * kept
+    bits = [(diff & (1 << i)) != 0 for i in range(3)]
+    halves = [env["halves"][i] for i in range(2)]
+
+    def step(i, carry):
+        state = {}
+
+        def load(u):
+            g = i * UNROLL + u
+            queries, keys, grads = s["q"][g], s["k"][g], s["dm"][g]
+            state[u] = {
+                "g": g,
+                "queries": queries,
+                "grads": grads,
+                "values": s["v"][g],
+                "turned": jnp.transpose(queries)[:, 0:LANES],
+                "turned_grads": jnp.transpose(grads)[:, 0:LANES],
+                "turned_keys": jnp.transpose(keys),
+                "dq": [],
+                "dk": [],
+                "dv": [],
+            }
+
+        def products(item):
+            u, t = item
+            if t == 0:
+                load(u)
+            at = state[u]
+            if t < 4:
+                block = blocks_of(at["turned_grads"], t, halves)
+                right = padded(block, t)
+            else:
+                block = right = tail_of(at["grads"][LANES:GT], env["heads"])
+            return block, dot(at["values"], right, 1, 0)
+
+        def back(item, result):
+            u, t = item
+            at = state[u]
+            grad_block, product = result
+            attention = s["att"][at["g"], :, t * CHUNK : min((t + 1) * CHUNK, QL)]
+            weighted = attention * jnp.concatenate(collect(product, bits), axis=0)
             total = jnp.sum(weighted, axis=0, keepdims=True)
             d_score = spread(weighted - attention * total, env["masks"])
-            d_values += dot(spread(attention, env["masks"]), d_mixed, 1, 0)
-            d_keys += dot(d_score, env["qx"][start : start + n, :], 1, 0)
-            tiles.append(dot(keys, d_score, 0, 0))
-        main, last = heads_joined(tiles)
-        s["dqkv"][g, 0:LANES, 0:D] = (main * SCALE).astype(BF16)
-        s["dqkv"][g, LANES:GT, 0:D] = (last * SCALE).astype(BF16)
-        for value, start, scale in ((d_keys, 256, SCALE), (d_values, 512, 1.0)):
-            slots = value.reshape(SLOTS, GROUP, D)
-            turned = [
-                slots[k] if k % GROUP == 0 else pltpu.roll(slots[k], GROUP - k % GROUP, 0)
-                for k in range(SLOTS)
-            ]
-            s["dqkv"][g, :, start : start + D] = (jnp.concatenate(turned, axis=0) * scale).astype(
-                BF16
-            )
+            at["dv"].append(dot(grad_block, spread(attention, env["masks"]), 1, 1))
+            if t < 4:
+                block = blocks_of(at["turned"], t, halves)
+                left = at["turned_keys"][48 * t : 48 * t + 48]
+            else:
+                block = tail_of(at["queries"][LANES:GT], env["heads"])
+                left = at["turned_keys"]
+            at["dk"].append(dot(block, d_score, 1, 1))
+            at["dq"].append(dot(left, d_score, 1, 0))
+            if t == 4:
+                finish(at)
+
+        def finish(at):
+            g = at["g"]
+            main, last = heads_joined(at["dq"][0:4], at["dq"][4], env["heads"], SCALE)
+            s["dqkv"][g, 0:LANES, 0:D] = main
+            s["dqkv"][g, LANES:GT, 0:D] = last
+            d_keys = (jnp.concatenate(at["dk"][0:4], axis=0) + at["dk"][4]) * SCALE
+            d_values = jnp.concatenate(at["dv"][0:4], axis=0) + at["dv"][4]
+            for value, start in ((d_keys, 256), (d_values, 512)):
+                slots = jnp.transpose(value.astype(BF16)).astype(F32).reshape(SLOTS, GROUP, D)
+                turned = [
+                    slots[k] if k % GROUP == 0 else pltpu.roll(slots[k], GROUP - k % GROUP, 0)
+                    for k in range(SLOTS)
+                ]
+                s["dqkv"][g, :, start : start + D] = jnp.concatenate(turned, axis=0).astype(BF16)
+
+        staged([(u, t) for u in range(UNROLL) for t in range(5)], products, back)
         return carry
 
-    lax.fori_loop(0, GROUPS, step, 0)
+    lax.fori_loop(0, GROUPS // UNROLL, step, 0)
 
 
 def backward_qkv(s, w, acc, sums, done):
     gain = wide(w["cols"][0])
 
-    def step(c, carry):
+    def products(c, _):
+        d_qkv = from_groups(s["dqkv"][:, group_rows(c), :].astype(F32)).astype(BF16)
+        return dot(s["h1"][:, lanes_of(c)], d_qkv, 1, 0), dot(w["qkv"][0:D, :], d_qkv, 1, 1)
+
+    def finish(c, held):
         lanes = lanes_of(c)
-        d_qkv = from_groups(s["dqkv"][:, group_rows(c), :].astype(F32)).astype(BF16)
-        add_tiles(acc["qkv"], dot(s["h1"][:, lanes], d_qkv, 1, 0))
-        d_normed = dot(w["qkv"][0:D, :], d_qkv, 1, 1)
+        grad_qkv, d_normed = held
+        add_tiles(acc["qkv"], grad_qkv)
         xhat = s["xhat1"][:, lanes]
         sums[0] += fold(d_normed * xhat)
         sums[1] += fold(d_normed)
         done(
             c, lanes, s["g"][:, lanes] + norm_back(d_normed, xhat, s["rstd1"][:, lanes], gain)
         )
-        return carry
-
-    lax.fori_loop(0, CHUNKS, step, 0)
+
+    skewed((products, finish))
 
 
 def per_layer():
@@ -572,13 +702,13 @@
 
 def common():
     return {
-        "qx": ((QL, D), BF16),
-        "dx": ((QL, D), BF16),
+        "halves": ((2, 16, LANES), BF16),
         "heads": ((HEADS, 16, D), BF16),
         "masks": ((5, 16, CHUNK), BF16),
         "diff": ((GROUP, CHUNK), jnp.int32),
         "count": ((GROUPS, CHUNK), F32),
         "dm": ((GROUPS, GT, D), BF16),
+        "middle": ((D, TOKENS), F32),
         "dqkv": ((GROUPS, GT, 6 * LANES), BF16),
         "g": ((D, TOKENS), F32),
         "sums": ((5, D, LANES), F32),
@@ -612,6 +742,9 @@
         first = jnp.where(diff == (2 * m) % 8, 1.0, 0.0)
         second = jnp.where(diff == 2 * m + 1, 1.0, 0.0)
         env["masks"][m] = jnp.concatenate([first, second], axis=0).astype(BF16)
+    sub = lax.broadcasted_iota(jnp.int32, (16, LANES), 0)
+    env["halves"][0] = jnp.where(sub < 8, 1.0, 0.0).astype(BF16)
+    env["halves"][1] = jnp.where(sub < 8, 0.0, 1.0).astype(BF16)
     feature = lax.broadcasted_iota(jnp.int32, (16, D), 1) // HEAD_DIM
     for h in range(HEADS):
         env["heads"][h] = jnp.where(feature == h, 1.0, 0.0).astype(BF16)
@@ -677,7 +810,7 @@
         forward_qkv(s[layer], w[layer])
         forward_attention(s[layer], env)
         last = layer == LAYERS - 1
-        forward_rest(s[layer], w[layer], put(out) if last else keep(s[layer + 1]["x"]))
+        forward_rest(dict(s[layer], middle=env["middle"]), w[layer], put(out) if last else keep(s[layer + 1]["x"]))
     for layer in reversed(range(LAYERS)):
         sums[...] = jnp.zeros_like(sums)
         for ref in acc.values():

time: 254 us -> 171 us (0.67)
  Pallas kernels: 141 us -> 57.8 us
    pallas_call x1, Pallas kernels: 141 us -> 57.8 us  [run_kernel(): pl.pallas_call(body, out_shape=(full, full, jax.ShapeDtypeStruct(blocks.s...]
  transfers between devices with their start and end apart: 1 -> 1, of which waited for: 1 -> 1; matrix products, arithmetic and copies ran while one was open for 2% -> 3% of each run, Pallas kernels for 0% -> 0%
where the time goes in v2:
time: 171 us
  Pallas kernels  57.8 us (34%)
  waiting for transfers between devices  54.6 us (32%)
  blocking collectives  36.8 us (22%)
  between operations  14.7 us (9%)
  other arithmetic  6.36 us (4%)
    pallas_call x1, Pallas kernels, run_kernel(): pl.pallas_call(body, out_shape=(full, full, jax.ShapeDtypeStruct(blocks.s...  57.8 us
    all_gather x1, waiting for transfers between devices, gather_params(): return lax.all_gather(padded, AXES, axis=0, tiled=False)  54.6 us
    all_to_all x1, blocking collectives, reduce_grads(): got = lax.all_to_all(grads, AXES, 0, 0, tiled=True)  36.8 us
  transfers between devices with their start and end apart: 1, of which 1 were waited for; matrix products, arithmetic and copies ran while one was open for 3% of the time, Pallas kernels for 0%

profile of v2, /device:TPU:0, one launch (start us, length us, event | category | flops | bytes accessed | tf_op | source)
XLA Modules:
  0.0 171.0 jit_solution(2949921406152685550)
XLA Ops:
  7.2 0.0 all-gather.2.cloned.1.call-start
  7.2 1.0 fusion
  8.2 0.6 copy.14
  8.8 0.0 all-gather.2.cloned.1.call-update
  8.8 0.7 convert_element_type.14
  9.5 1.3 convert_reduce_fusion.1
  11.4 0.7 select_reduce_fusion
  12.2 1.2 convert_bitcast_fusion.refs_4_
  13.4 0.5 sqrt_bitcast_fusion.refs_3_
  13.9 54.6 %all-gather.2.cloned.1.call-done.refs_2_ = bf16[32,2,80,128]{3,2,1,0:T(8,128)(2,1)} async-done(((bf16[1,2,80,128]{3,2,1,0:T(8,128)(2,1)}), bf16[32,2,80,128]{3,2,1,0:T(8,128)(2,1)}) %all-gather.2.cloned.1.call-update) | async-done | bytes 1310736 | tf_op jit(solution)/shard_map/all_gather | solution.py:874
  68.5 57.8 %shard_map.85 = (f32[17,192,128]{2,1,0:T(8,128)}, f32[17,192,128]{2,1,0:T(8,128)}, bf16[32,2,80,128]{3,2,1,0:T(8,128)(2,1)}) custom-call(bf16[17,192,128]{2,1,0:T(8,128)(2,1)} %bitcast.18, bf16[17,192,128]{2,1,0:T(8,128)(2,1)} %bitcast.19, bf16[32,2,80,128]{3,2,1,0:T(8,128)(2,1)} %all-gather.2.cloned.1.call-done.refs_2_, f32[1,128]{1,0:T(1,128)} %sqrt_bitcast_fusion.refs_3_, ...), custom_call_target="tpu_custom_call" | custom-call | tf_op jit(solution)/shard_map/pallas_call | solution.py:835
  126.4 36.8 %all_to_all.5 = bf16[32,2,80,128]{3,2,1,0:T(8,128)(2,1)S(1)} all-to-all(bf16[32,2,80,128]{3,2,1,0:T(8,128)(2,1)} %get-tuple-element.8), channel_id=1, replica_groups=mesh['dp'=8,'fsdp'=4] {'dp','fsdp'}, dimensions={0} | all-to-all | bytes 2621440 | tf_op jit(solution)/shard_map/all_to_all | solution.py:883
  163.2 0.2 convert_reduce_fusion
  163.4 0.8 slice_select_fusion
  (1 shorter events, 0.0 us)
Async XLA Ops:
  7.2 61.4 %all-gather.2.cloned.1.call-start = ((), (), s32[]{:S(2)}) async-start(), calls=%async_computation.1 | async-start | bytes 1351680 | tf_op jit(solution)/shard_map/all_gather | solution.py:874
Sparse Core Ops, SparseCore 0:
  11.4 57.0 all-gather.1

commit v3 on v2

--- a/solution.py
+++ b/solution.py
@@ -1,3 +1,4 @@
+import functools
 import math
 
 import jax
@@ -28,7 +29,6 @@
 CHUNK = 2 * ROWS
 CHUNKS = TOKENS // CHUNK
 FLAT = PSIZE // LANES
-PARTS = 32
 BLOCK = 80
 EPS = 1e-05
 SCALE = 1.0 / math.sqrt(HEAD_DIM)
@@ -64,11 +64,16 @@
     return jnp.concatenate([column, column], axis=1)
 
 
-def gather_flat(blocks, layer, flat):
-    for pair in range(blocks.shape[0] // 2):
-        base = 145 * pair
-        first = blocks[2 * pair, layer].astype(F32)
-        second = blocks[2 * pair + 1, layer].astype(F32)
+def gather_flat(own, other, place, layer, flat):
+    z, core = place[0], place[1]
+    for chip in range(FLAT // 145):
+        turn = z ^ (chip // 4)
+        at = (turn & 1) * 2 + turn // 2
+        mine = own[chip % 4, at, layer].astype(F32)
+        theirs = other[chip % 4, at, layer].astype(F32)
+        first = jnp.where(core == 0, mine, theirs)
+        second = jnp.where(core == 0, theirs, mine)
+        base = 145 * chip
         flat[pl.ds(base, BLOCK), :] = first
         flat[pl.ds(base + 72, BLOCK), :] = second
         flat[pl.ds(base + 72, 1), :] = jnp.where(
@@ -233,10 +238,13 @@
     put_row(2319, splice(acc["down"][0, FF : FF + 1, :], acc["down"][1, FF : FF + 1, :]))
 
 
-def scatter_blocks(flat, layer, blocks):
-    for part in range(blocks.shape[0]):
-        start = (145 * part) // 2
-        blocks[part, layer] = flat[pl.ds(start, BLOCK), :].astype(BF16)
+def scatter_blocks(flat, place, layer, keep, give):
+    core = place[1]
+    for chip in range(FLAT // 145):
+        first = flat[pl.ds(145 * chip, BLOCK), :]
+        second = flat[pl.ds(145 * chip + 72, BLOCK), :]
+        keep[chip % 4, chip // 4, layer] = jnp.where(core == 0, first, second).astype(BF16)
+        give[chip % 4, chip // 4, layer] = jnp.where(core == 0, second, first).astype(BF16)
 
 
 def norm(x, gain, bias):
@@ -661,7 +669,6 @@
 
 def per_layer():
     return {
-        "x": ((D, TOKENS), F32),
         "xhat1": ((D, TOKENS), F32),
         "rstd1": ((1, TOKENS), F32),
         "h1": ((D + 16, TOKENS), BF16),
@@ -708,6 +715,7 @@
         "diff": ((GROUP, CHUNK), jnp.int32),
         "count": ((GROUPS, CHUNK), F32),
         "dm": ((GROUPS, GT, D), BF16),
+        "x": ((D, TOKENS), F32),
         "middle": ((D, TOKENS), F32),
         "dqkv": ((GROUPS, GT, 6 * LANES), BF16),
         "g": ((D, TOKENS), F32),
@@ -763,7 +771,9 @@
     ref[rows:, :] = jnp.where(mark, 1.0, 0.0).astype(BF16)
 
 
-def kernel(names, tokens, out_grad, blocks, row_scale, count, out, in_grad, grads, *scratch):
+def kernel(
+    names, place, tokens, out_grad, own, other, row_scale, count, out, in_grad, keep_out, give_out, *scratch
+):
     table = {}
     for (prefix, name), ref in zip(names, scratch):
         table.setdefault(prefix, {})[name] = ref
@@ -778,16 +788,16 @@
         ones_below(s[layer]["h1"], D)
         ones_below(s[layer]["h2"], D)
         ones_below(s[layer]["act"], FF)
-        gather_flat(blocks, layer, env["flat"])
+        gather_flat(own, other, place, layer, env["flat"])
         unpack(env["flat"], w[layer], env["tmp"])
     for slot in range(SLOTS):
         lanes = slice(slot * ROWS, (slot + 1) * ROWS)
         if slot < SEQ:
-            s[0]["x"][:, lanes] = tokens[slot].astype(F32)
+            env["x"][:, lanes] = tokens[slot].astype(F32)
             keep = jnp.where(valid_slots >= float(slot), row_scale[...], 0.0)
             env["g"][:, lanes] = out_grad[slot].astype(F32) * keep
         else:
-            s[0]["x"][:, lanes] = jnp.zeros((D, ROWS), F32)
+            env["x"][:, lanes] = jnp.zeros((D, ROWS), F32)
             env["g"][:, lanes] = jnp.zeros((D, ROWS), F32)
 
     def put(target):
@@ -807,10 +817,11 @@
         return done
 
     for layer in range(LAYERS):
-        forward_qkv(s[layer], w[layer])
-        forward_attention(s[layer], env)
+        state = dict(s[layer], x=env["x"], middle=env["middle"])
+        forward_qkv(state, w[layer])
+        forward_attention(state, env)
         last = layer == LAYERS - 1
-        forward_rest(dict(s[layer], middle=env["middle"]), w[layer], put(out) if last else keep(s[layer + 1]["x"]))
+        forward_rest(state, w[layer], put(out) if last else keep(env["x"]))
     for layer in reversed(range(LAYERS)):
         sums[...] = jnp.zeros_like(sums)
         for ref in acc.values():
@@ -822,110 +833,138 @@
             state, w[layer], acc, sums, put(in_grad) if layer == 0 else keep(env["g"])
         )
         pack(env["flat"], acc, sums, env["tmp"])
-        scatter_blocks(env["flat"], layer, grads)
-
-
-def run_kernel(tokens, out_grad, blocks, row_scale, count):
+        scatter_blocks(env["flat"], place, layer, keep_out, give_out)
+
+
+def run_kernel(place, tokens, out_grad, own, other, row_scale, count):
     names, scratch = make_scratch()
     full = jax.ShapeDtypeStruct((SEQ, D, ROWS), F32)
+    blocks = jax.ShapeDtypeStruct(own.shape, BF16)
 
     def body(*refs):
         kernel(names, *refs)
 
+    vmem = pl.BlockSpec(memory_space=pltpu.VMEM)
     return pl.pallas_call(
         body,
-        out_shape=(full, full, jax.ShapeDtypeStruct(blocks.shape, BF16)),
-        in_specs=[pl.BlockSpec(memory_space=pltpu.VMEM)] * 5,
-        out_specs=[pl.BlockSpec(memory_space=pltpu.VMEM)] * 3,
+        out_shape=(full, full, blocks, blocks),
+        in_specs=[pl.BlockSpec(memory_space=pltpu.SMEM)] + [vmem] * 6,
+        out_specs=[vmem] * 4,
         scratch_shapes=scratch,
         compiler_params=pltpu.CompilerParams(vmem_limit_bytes=64 * 1024 * 1024 - 256 * 1024),
-    )(tokens, out_grad, blocks, row_scale, count)
-
-
-AXES = ("dp", "fsdp")
-
-
-def flat_to_blocks(flat):
+    )(place, tokens, out_grad, own, other, row_scale, count)
+
+
+def halves_of_pairs(flat):
     rows = jnp.pad(flat.reshape(LAYERS, FLAT, LANES), ((0, 0), (0, BLOCK), (0, 0)))
-    starts = [(145 * part) // 2 for part in range(PARTS)]
-    return jnp.stack([rows[:, start : start + BLOCK] for start in starts])
-
-
-def blocks_to_flat(blocks):
+
+    def blocks(skip):
+        parts = [rows[:, 145 * chip + skip : 145 * chip + skip + BLOCK] for chip in range(16)]
+        return jnp.stack([jnp.stack(parts[at::4]) for at in range(4)])
+
+    return blocks(0), blocks(72)
+
+
+def pairs_joined(even, odd):
     joined = []
-    for pair in range(PARTS // 2):
-        first, second = blocks[2 * pair], blocks[2 * pair + 1]
+    for chip in range(16):
+        first, second = even[chip % 4, chip // 4], odd[chip % 4, chip // 4]
         seam = jnp.concatenate([first[:, 72:73, 0:64], second[:, 0:1, 64:]], axis=2)
         joined += [first[:, 0:72], seam, second[:, 1:73]]
     return jnp.concatenate(joined, axis=1).reshape(LAYERS, PSIZE)
 
 
-def gather_params(flat_params):
-    parts = lax.axis_size(AXES)
-    if parts != PARTS:
-        return flat_to_blocks(lax.all_gather(flat_params, AXES, axis=1, tiled=True))
+def swap_along(x, axis, bit):
+    pairs = [(i, i ^ bit) for i in range(lax.axis_size(axis))]
+    return lax.ppermute(x, axis, pairs)
+
+
+def gather_pairs(flat_params):
     size = flat_params.shape[1]
     room = BLOCK * LANES - size
-    padded = jnp.where(
-        lax.axis_index("fsdp") % 2 == 0,
+    part = jnp.where(
+        lax.axis_index("core") == 0,
         jnp.pad(flat_params, ((0, 0), (0, room))),
         jnp.pad(flat_params, ((0, 0), (64, room - 64))),
-    ).reshape(LAYERS, BLOCK, LANES)
-    return lax.all_gather(padded, AXES, axis=0, tiled=False)
-
-
-def reduce_grads(grads, size):
-    parts = lax.axis_size(AXES)
-    if parts != PARTS:
-        return lax.psum_scatter(
-            blocks_to_flat(grads.astype(F32)), AXES, scatter_dimension=1, tiled=True
-        )
-    got = lax.all_to_all(grads, AXES, 0, 0, tiled=True)
-    total = jnp.sum(got.astype(F32), axis=0).reshape(LAYERS, BLOCK * LANES)
+    ).reshape(1, LAYERS, BLOCK, LANES)
+    for bit in (2, 1):
+        part = jnp.concatenate([part, swap_along(part, "z", bit)], axis=0)
+    own = lax.all_gather(part, ("x", "y"), axis=0, tiled=False)
+    return own, swap_along(own, "core", 1)
+
+
+def reduce_pairs(keep, give, size):
+    got = swap_along(give, "core", 1)
+    part = (keep.astype(F32) + got.astype(F32)).astype(BF16)
+    part = lax.all_to_all(part, ("x", "y"), 0, 0, tiled=True)
+    part = jnp.sum(part.astype(F32), axis=0)
+    z = lax.axis_index("z")
+    for bit in (2, 1):
+        high = (z // bit) % 2
+        stay = lax.dynamic_slice_in_dim(part, high * bit, bit, 0)
+        go = lax.dynamic_slice_in_dim(part, (1 - high) * bit, bit, 0).astype(BF16)
+        part = stay + swap_along(go, "z", bit).astype(F32)
+    total = part.reshape(LAYERS, BLOCK * LANES)
     return jnp.where(
-        lax.axis_index("fsdp") % 2 == 0, total[:, 0:size], total[:, 64 : 64 + size]
-    )
-
-
-def body(tokens, out_grad, flat_params, feat_count, table_ids, table_counts):
+        lax.axis_index("core") == 0, total[:, 0:size], total[:, 64 : 64 + size]
+    )
+
+
+def body(axes, tokens, out_grad, flat_params, feat_count, table_ids, table_counts):
+    four = "core" in axes
     counts_float = table_counts.astype(F32)
     table_index = jnp.arange(table_counts.shape[0], dtype=jnp.int32)
     match = (table_ids[None, :] == table_index[:, None]).astype(F32)
     row_count = jnp.sum(match * counts_float[:, None], axis=0)
     row_scale = jnp.sqrt(jnp.mean(counts_float) / row_count)[None, :]
     count = feat_count.astype(F32)[None, :]
-    blocks = gather_params(flat_params)
+    if four:
+        place = jnp.stack([lax.axis_index("z"), lax.axis_index("core")]).astype(jnp.int32)
+        own, other = gather_pairs(flat_params)
+    else:
+        place = jnp.zeros((2,), jnp.int32)
+        own, other = halves_of_pairs(lax.all_gather(flat_params, axes, axis=1, tiled=True))
+        turn = jnp.array([0, 2, 1, 3])
+        own, other = own[:, turn], other[:, turn]
     turned = jnp.transpose(tokens, (1, 2, 0))
     turned_grad = jnp.transpose(out_grad, (1, 2, 0))
     results = [
         run_kernel(
+            place,
             turned[:, :, at : at + ROWS],
             turned_grad[:, :, at : at + ROWS],
-            blocks,
+            own,
+            other,
             row_scale[:, at : at + ROWS],
             count[:, at : at + ROWS],
         )
         for at in range(0, tokens.shape[0], ROWS)
     ]
-    out, in_grad, grads = results[0]
+    out, in_grad, keep, give = results[0]
     if len(results) > 1:
         out = jnp.concatenate([r[0] for r in results], axis=2)
         in_grad = jnp.concatenate([r[1] for r in results], axis=2)
-        grads = sum(r[2].astype(F32) for r in results).astype(BF16)
-    return (
-        jnp.transpose(out, (2, 0, 1)),
-        jnp.transpose(in_grad, (2, 0, 1)),
-        reduce_grads(grads, flat_params.shape[1]),
-    )
+        keep = sum(r[2].astype(F32) for r in results)
+        give = sum(r[3].astype(F32) for r in results)
+    if four:
+        grads = reduce_pairs(keep, give, flat_params.shape[1])
+    else:
+        flat = pairs_joined(keep.astype(F32), give.astype(F32))
+        grads = lax.psum_scatter(flat, axes, scatter_dimension=1, tiled=True)
+    return jnp.transpose(out, (2, 0, 1)), jnp.transpose(in_grad, (2, 0, 1)), grads
 
 
 def solution(mesh):
-    rows = P(AXES, None, None)
-    placed = (rows, rows, P(None, AXES), P(AXES), P(AXES), P())
+    axes = mesh.axis_names
+    if tuple(mesh.devices.shape) == (8, 4):
+        axes = ("z", "x", "y", "core")
+        mesh = jax.sharding.Mesh(mesh.devices.reshape(4, 2, 2, 2), axes)
+    rows = P(axes, None, None)
+    placed = (rows, rows, P(None, axes), P(axes), P(axes), P())
     return jax.shard_map(
-        body,
+        functools.partial(body, axes),
         mesh=mesh,
         in_specs=placed,
-        out_specs=(rows, rows, P(None, AXES)),
+        out_specs=(rows, rows, P(None, axes)),
         check_vma=False,
     )

time: 171 us -> 116 us (0.68)
  waiting for transfers between devices: 54.6 us -> 23 us
  blocking collectives: 36.8 us -> 11.6 us
  between operations: 14.7 us -> 1.42 us
  starting transfers between devices: 0.04 us -> 12.3 us
    all_gather x1 -> x0, waiting for transfers between devices: 54.6 us -> none  [gather_params(): return lax.all_gather(padded, AXES, axis=0, tiled=False)]
    all_to_all x1 -> x0, blocking collectives: 36.8 us -> none  [reduce_grads(): got = lax.all_to_all(grads, AXES, 0, 0, tiled=True)]
    ppermute x0 -> x6, waiting for transfers between devices: none -> 12.9 us  [swap_along(): return lax.ppermute(x, axis, pairs)]
    all_gather x0 -> x1, blocking collectives: none -> 11.6 us  [gather_pairs(): own = lax.all_gather(part, ('x', 'y'), axis=0, tiled=False)]
    all_to_all x0 -> x1, waiting for transfers between devices: none -> 10.1 us  [reduce_pairs(): part = lax.all_to_all(part, ('x', 'y'), 0, 0, tiled=True)]
    ppermute x0 -> x6, starting transfers between devices: none -> 8.79 us  [swap_along(): return lax.ppermute(x, axis, pairs)]
    all_to_all x0 -> x1, starting transfers between devices: none -> 3.48 us  [reduce_pairs(): part = lax.all_to_all(part, ('x', 'y'), 0, 0, tiled=True)]
    convert_element_type x0 -> x1, other arithmetic: none -> 2.09 us  [reduce_pairs(): part = (keep.astype(F32) + got.astype(F32)).astype(BF16)]
  transfers between devices with their start and end apart: 1 -> 7, of which waited for: 1 -> 7; matrix products, arithmetic and copies ran while one was open for 3% -> 3% of each run, Pallas kernels for 0% -> 0%
where the time goes in v3:
time: 116 us
  Pallas kernels  58 us (50%)
  waiting for transfers between devices  23 us (20%)
  starting transfers between devices  12.3 us (11%)
  blocking collectives  11.6 us (10%)
  other arithmetic  7.76 us (7%)
  local copies, waits for them, and re-layouts  1.79 us (2%)
  between operations  1.42 us (1%)
    pallas_call x1, Pallas kernels, run_kernel(): pl.pallas_call(body, out_shape=(full, full, blocks, blocks), in_specs=[pl...  58 us
    ppermute x6, waiting for transfers between devices, swap_along(): return lax.ppermute(x, axis, pairs)  12.9 us
    all_gather x1, blocking collectives, gather_pairs(): own = lax.all_gather(part, ('x', 'y'), axis=0, tiled=False)  11.6 us
    all_to_all x1, waiting for transfers between devices, reduce_pairs(): part = lax.all_to_all(part, ('x', 'y'), 0, 0, tiled=True)  10.1 us
    ppermute x6, starting transfers between devices, swap_along(): return lax.ppermute(x, axis, pairs)  8.79 us
    all_to_all x1, starting transfers between devices, reduce_pairs(): part = lax.all_to_all(part, ('x', 'y'), 0, 0, tiled=True)  3.48 us
  transfers between devices with their start and end apart: 7, of which 7 were waited for; matrix products, arithmetic and copies ran while one was open for 3% of the time, Pallas kernels for 0%

profile of v3, /device:TPU:0, one launch (start us, length us, event | category | flops | bytes accessed | tf_op | source)
XLA Modules:
  0.0 115.8 jit_solution(13097260818400173368)
XLA Ops:
  0.6 0.0 copy-start.2
  0.6 0.0 copy-start.3
  0.7 1.0 fusion
  1.6 4.1 %collective-permute-start = (bf16[1,2,80,128]{3,2,1,0:T(8,128)(2,1)S(1)}, bf16[1,2,80,128]{3,2,1,0:T(8,128)(2,1)S(1)}, u32[]{:S(2)}, u32[]{:S(2)}) collective-permute-start(bf16[1,2,80,128]{3,2,1,0:T(8,128)(2,1)S(1)} %copy.14), channel_id=1, source_target_pairs={{0,16},{8,24},{16,0},{24,8},{1,17},{9,25},{17,1},{25,9},{2,18},{10... | collective-permute-start | bytes 122888 | tf_op jit(solution)/shard_map/ppermute | solution.py:879
  5.7 0.7 convert_element_type.35
  6.4 1.8 %collective-permute-done = bf16[1,2,80,128]{3,2,1,0:T(8,128)(2,1)S(1)} collective-permute-done((bf16[1,2,80,128]{3,2,1,0:T(8,128)(2,1)S(1)}, bf16[1,2,80,128]{3,2,1,0:T(8,128)(2,1)S(1)}, u32[]{:S(2)}, u32[]{:S(2)}) %collective-permute-start) | collective-permute-done | bytes 40992 | tf_op jit(solution)/shard_map/ppermute | solution.py:879
  8.2 1.5 %collective-permute-start.1 = (bf16[2,2,80,128]{3,2,1,0:T(8,128)(2,1)S(1)}, bf16[2,2,80,128]{3,2,1,0:T(8,128)(2,1)S(1)}, u32[]{:S(2)}, u32[]{:S(2)}) collective-permute-start(bf16[2,2,80,128]{3,2,1,0:T(8,128)(2,1)S(1)} %pad_maximum_fusion.1), channel_id=1, source_target_pairs={{0,8},{8,0},{16,24},{24,16},{1,9},{9,1},{17,25},{25,17},{2,10},{10... | collective-permute-start | bytes 245768 | tf_op jit(solution)/shard_map/ppermute | solution.py:879
  9.7 1.3 %convert_reduce_fusion.1 = f32[]{:T(128)} fusion(s32[52]{0:T(128)} %param.11), kind=kLoop, calls=%fused_computation.18 | loop fusion | flops 103 | bytes 212 | tf_op jit(solution)/shard_map/reduce_sum | solution.py:919
  11.6 1.1 collective-permute-done.1
  12.7 11.6 %all-gather = bf16[16,2,80,128]{3,2,1,0:T(8,128)(2,1)S(1)} all-gather(bf16[4,2,80,128]{3,2,1,0:T(8,128)(2,1)S(1)} %pad_maximum_fusion), channel_id=2, replica_groups=mesh['z'=4,'x'=2,'y'=2,'core'=2] {'x','y'}, dimensions={0}, use_global_device_ids=true | all-gather | bytes 819200 | tf_op jit(solution)/shard_map/all_gather | solution.py:892
  24.3 0.0 copy-start
  24.3 0.8 copy-done
  25.2 0.0 collective-permute-start.2
  25.2 0.6 pad_add_fusion.refs_0_
  25.8 0.0 copy-done.2
  25.8 0.1 select_reduce_fusion
  25.9 0.0 copy-done.3
  25.9 0.6 convert_bitcast_fusion.refs_6_
  26.5 0.5 sqrt_bitcast_fusion.refs_5_
  27.0 0.2 collective-permute-done.2.refs_4_
  27.3 0.0 copy-start.1
  27.3 0.9 copy-done.1
  28.1 58.0 %shard_map.85 = (f32[17,192,128]{2,1,0:T(8,128)}, f32[17,192,128]{2,1,0:T(8,128)}, bf16[4,4,2,80,128]{4,3,2,1,0:T(8,128)(2,1)}, bf16[4,4,2,80,128]{4,3,2,1,0:T(8,128)(2,1)}) custom-call(s32[2]{0:T(128)} %pad_add_fusion.refs_0_, bf16[17,192,128]{2,1,0:T(8,128)(2,1)} %bitcast.25, bf16[17,192,128]{2,1,0:T(8,128)(2,1)} %bitcast.26, ...), custom_call_target="tpu_custom_call" | custom-call | tf_op jit(solution)/shard_map/pallas_call | solution.py:848
  86.1 0.3 collective-permute-start.3
  86.4 2.0 %collective-permute-done.3 = bf16[4,4,2,80,128]{4,3,2,1,0:T(8,128)(2,1)S(1)} collective-permute-done((bf16[4,4,2,80,128]{4,3,2,1,0:T(8,128)(2,1)}, bf16[4,4,2,80,128]{4,3,2,1,0:T(8,128)(2,1)S(1)}, u32[]{:S(2)}, u32[]{:S(2)}) %collective-permute-start.3) | collective-permute-done | bytes 655392 | tf_op jit(solution)/shard_map/ppermute | solution.py:879
  88.4 2.1 %add_convert_fusion = bf16[4,4,2,80,128]{4,3,2,1,0:T(8,128)(2,1)} fusion(bf16[4,4,2,80,128]{4,3,2,1,0:T(8,128)(2,1)S(1)} %collective-permute-done.3, bf16[4,4,2,80,128]{4,3,2,1,0:T(8,128)(2,1)} %get-tuple-element.9), kind=kLoop, calls=%fused_computation.1 | loop fusion | flops 1310720 | bytes 1966080 | tf_op jit(solution)/shard_map/convert_element_type | solution.py:898
  90.5 3.5 %all-to-all-start = ((bf16[4,4,2,80,128]{4,3,2,1,0:T(8,128)(2,1)}), bf16[4,4,2,80,128]{4,3,2,1,0:T(8,128)(2,1)S(1)}, u32[]{:S(2)}, u32[]{:S(2)}) async-start(bf16[4,4,2,80,128]{4,3,2,1,0:T(8,128)(2,1)} %add_convert_fusion), calls=%async_computation | async-start | bytes 1310720 | tf_op jit(solution)/shard_map/all_to_all | solution.py:899
  94.0 10.1 %all-to-all-done = bf16[4,4,2,80,128]{4,3,2,1,0:T(8,128)(2,1)S(1)} async-done(((bf16[4,4,2,80,128]{4,3,2,1,0:T(8,128)(2,1)}), bf16[4,4,2,80,128]{4,3,2,1,0:T(8,128)(2,1)S(1)}, u32[]{:S(2)}, u32[]{:S(2)}) %all-to-all-start) | async-done | bytes 655392 | tf_op jit(solution)/shard_map/all_to_all | solution.py:899
  104.1 0.1 convert_reduce_fusion
  104.3 2.4 %collective-permute-start.4 = (bf16[2,2,80,128]{3,2,1,0:T(8,128)(2,1)S(1)}, bf16[2,2,80,128]{3,2,1,0:T(8,128)(2,1)S(1)}, u32[]{:S(2)}, u32[]{:S(2)}) collective-permute-start(bf16[2,2,80,128]{3,2,1,0:T(8,128)(2,1)S(1)} %dynamic-slice_convert_fusion), channel_id=1, source_target_pairs={{0,16},{8,24},{16,0},{24,8},{1,17},{9,25},{17,1},{25,9},{2,18},{10... | collective-permute-start | bytes 245768 | tf_op jit(solution)/shard_map/ppermute | solution.py:879
  106.7 4.2 %collective-permute-done.4 = bf16[2,2,80,128]{3,2,1,0:T(8,128)(2,1)S(1)} collective-permute-done((bf16[2,2,80,128]{3,2,1,0:T(8,128)(2,1)S(1)}, bf16[2,2,80,128]{3,2,1,0:T(8,128)(2,1)S(1)}, u32[]{:S(2)}, u32[]{:S(2)}) %collective-permute-start.4) | collective-permute-done | bytes 81952 | tf_op jit(solution)/shard_map/ppermute | solution.py:879
  110.9 0.4 collective-permute-start.5
  111.3 3.6 %collective-permute-done.5 = bf16[1,2,80,128]{3,2,1,0:T(8,128)(2,1)S(1)} collective-permute-done((bf16[1,2,80,128]{3,2,1,0:T(8,128)(2,1)S(1)}, bf16[1,2,80,128]{3,2,1,0:T(8,128)(2,1)S(1)}, u32[]{:S(2)}, u32[]{:S(2)}) %collective-permute-start.5) | collective-permute-done | bytes 40992 | tf_op jit(solution)/shard_map/ppermute | solution.py:879
  115.0 0.8 slice_select_fusion
  (8 shorter events, 0.1 us)
Async XLA Ops:
  0.6 25.2 %copy-start.2 = (s32[128]{0:T(128)S(1)}, s32[128]{0:T(128)}, u32[]{:S(2)}) copy-start(s32[128]{0:T(128)} %param.10) | copy-start | bytes 1540
  0.6 25.3 %copy-start.3 = (s32[128]{0:T(128)S(1)}, s32[128]{0:T(128)}, u32[]{:S(2)}) copy-start(s32[128]{0:T(128)} %param.9) | copy-start | bytes 1540
  1.6 6.5 %collective-permute-start = (bf16[1,2,80,128]{3,2,1,0:T(8,128)(2,1)S(1)}, bf16[1,2,80,128]{3,2,1,0:T(8,128)(2,1)S(1)}, u32[]{:S(2)}, u32[]{:S(2)}) collective-permute-start(bf16[1,2,80,128]{3,2,1,0:T(8,128)(2,1)S(1)} %copy.14), channel_id=1, source_target_pairs={{0,16},{8,24},{16,0},{24,8},{1,17},{9,25},{17,1},{25,9},{2,18},{10... | collective-permute-start | bytes 122888 | tf_op jit(solution)/shard_map/ppermute | solution.py:879
  8.2 4.5 %collective-permute-start.1 = (bf16[2,2,80,128]{3,2,1,0:T(8,128)(2,1)S(1)}, bf16[2,2,80,128]{3,2,1,0:T(8,128)(2,1)S(1)}, u32[]{:S(2)}, u32[]{:S(2)}) collective-permute-start(bf16[2,2,80,128]{3,2,1,0:T(8,128)(2,1)S(1)} %pad_maximum_fusion.1), channel_id=1, source_target_pairs={{0,8},{8,0},{16,24},{24,16},{1,9},{9,1},{17,25},{25,17},{2,10},{10... | collective-permute-start | bytes 245768 | tf_op jit(solution)/shard_map/ppermute | solution.py:879
  24.3 0.8 copy-start
  25.2 2.1 %collective-permute-start.2 = (bf16[4,4,2,80,128]{4,3,2,1,0:T(8,128)(2,1)S(1)}, bf16[4,4,2,80,128]{4,3,2,1,0:T(8,128)(2,1)S(1)}, u32[]{:S(2)}, u32[]{:S(2)}) collective-permute-start(bf16[4,4,2,80,128]{4,3,2,1,0:T(8,128)(2,1)S(1)} %bitcast.23), channel_id=1, source_target_pairs={{0,1},{1,0},{2,3},{3,2},{4,5},{5,4},{6,7},{7,6},{8,9},{9,8},{10,11... | collective-permute-start | bytes 1966088 | tf_op jit(solution)/shard_map/ppermute | solution.py:879
  27.3 0.9 copy-start.1
  86.1 2.3 %collective-permute-start.3 = (bf16[4,4,2,80,128]{4,3,2,1,0:T(8,128)(2,1)}, bf16[4,4,2,80,128]{4,3,2,1,0:T(8,128)(2,1)S(1)}, u32[]{:S(2)}, u32[]{:S(2)}) collective-permute-start(bf16[4,4,2,80,128]{4,3,2,1,0:T(8,128)(2,1)} %get-tuple-element.10), channel_id=1, source_target_pairs={{0,1},{1,0},{2,3},{3,2},{4,5},{5,4},{6,7},{7,6},{8,9},{9,8},{10,11... | collective-permute-start | bytes 1966088 | tf_op jit(solution)/shard_map/ppermute | solution.py:879
  90.5 13.6 %all-to-all-start = ((bf16[4,4,2,80,128]{4,3,2,1,0:T(8,128)(2,1)}), bf16[4,4,2,80,128]{4,3,2,1,0:T(8,128)(2,1)S(1)}, u32[]{:S(2)}, u32[]{:S(2)}) async-start(bf16[4,4,2,80,128]{4,3,2,1,0:T(8,128)(2,1)} %add_convert_fusion), calls=%async_computation | async-start | bytes 1310720 | tf_op jit(solution)/shard_map/all_to_all | solution.py:899
  104.3 6.6 %collective-permute-start.4 = (bf16[2,2,80,128]{3,2,1,0:T(8,128)(2,1)S(1)}, bf16[2,2,80,128]{3,2,1,0:T(8,128)(2,1)S(1)}, u32[]{:S(2)}, u32[]{:S(2)}) collective-permute-start(bf16[2,2,80,128]{3,2,1,0:T(8,128)(2,1)S(1)} %dynamic-slice_convert_fusion), channel_id=1, source_target_pairs={{0,16},{8,24},{16,0},{24,8},{1,17},{9,25},{17,1},{25,9},{2,18},{10... | collective-permute-start | bytes 245768 | tf_op jit(solution)/shard_map/ppermute | solution.py:879
  110.9 4.1 %collective-permute-start.5 = (bf16[1,2,80,128]{3,2,1,0:T(8,128)(2,1)S(1)}, bf16[1,2,80,128]{3,2,1,0:T(8,128)(2,1)S(1)}, u32[]{:S(2)}, u32[]{:S(2)}) collective-permute-start(bf16[1,2,80,128]{3,2,1,0:T(8,128)(2,1)S(1)} %dynamic-slice_convert_fusion.1), channel_id=1, source_target_pairs={{0,8},{8,0},{16,24},{24,16},{1,9},{9,1},{17,25},{25,17},{2,10},{10... | collective-permute-start | bytes 122888 | tf_op jit(solution)/shard_map/ppermute | solution.py:879

commit v4 on v3

--- a/solution.py
+++ b/solution.py
@@ -20,6 +20,7 @@
 LANES = 128
 UNROLL = 4
 DEPTH = 6
+BAND = 32
 STEPS = 3
 GROUP = 8
 GROUPS = ROWS // GROUP
@@ -28,6 +29,7 @@
 TOKENS = SLOTS * ROWS
 CHUNK = 2 * ROWS
 CHUNKS = TOKENS // CHUNK
+HALVES = (slice(0, ROWS), slice(ROWS, CHUNK))
 FLAT = PSIZE // LANES
 BLOCK = 80
 EPS = 1e-05
@@ -53,7 +55,7 @@
 
 
 def splice(a, b):
-    return jnp.where(lane_half(a.shape), swap(a), swap(b))
+    return swap(jnp.where(lane_half(a.shape), b, a))
 
 
 def after(a, b):
@@ -81,10 +83,6 @@
         )
 
 
-def column_of(row):
-    return jnp.transpose(jnp.broadcast_to(row, (LANES, 2 * LANES)))[0:D]
-
-
 def unpack(flat, w, tmp):
     def rows(start, count, stride):
         return flat[pl.ds(start, count, stride=stride), :]
@@ -95,12 +93,22 @@
     def pair_row(a, b):
         return jnp.concatenate([a, b], axis=1)
 
-    w["cols"][0] = column_of(pair_row(row(0), low_half(row(1))))
-    w["cols"][1] = column_of(pair_row(splice(row(1), row(2)), low_half(swap(row(2)))))
-    w["cols"][2] = column_of(pair_row(row(1158), low_half(row(1159))))
-    w["cols"][3] = column_of(pair_row(splice(row(1159), row(1160)), low_half(swap(row(1160)))))
-    w["cols"][4] = column_of(pair_row(row(1161), low_half(row(1162))))
-    w["cols"][5] = column_of(pair_row(splice(row(2318), row(2319)), low_half(swap(row(2319)))))
+    vectors = [
+        pair_row(row(0), low_half(row(1))),
+        pair_row(splice(row(1), row(2)), low_half(swap(row(2)))),
+        pair_row(row(1158), low_half(row(1159))),
+        pair_row(splice(row(1159), row(1160)), low_half(swap(row(1160)))),
+        pair_row(row(1161), low_half(row(1162))),
+        pair_row(splice(row(2318), row(2319)), low_half(swap(row(2319)))),
+    ]
+    index = lax.broadcasted_iota(jnp.int32, (16, 2 * LANES), 0)
+    stacked = jnp.zeros((16, 2 * LANES), F32)
+    for i, vector in enumerate(vectors):
+        stacked = jnp.where(index == i, vector, stacked)
+    stacked = stacked.astype(BF16)
+    for i in range(6):
+        pick = jnp.where(index[:, 0:LANES] == i, 1.0, 0.0).astype(BF16)
+        w["cols"][i] = dot(stacked, pick, 0, 0)[0:D]
 
     e = [rows(3 + j, 96, 9) for j in range(9)]
     even = (e[0], low_half(e[1]), splice(e[1], e[2]), low_half(swap(e[2])), e[3], low_half(e[4]))
@@ -123,9 +131,9 @@
     )
     first_row = lax.broadcasted_iota(jnp.int32, (16, LANES), 0) == 0
     for j in range(6):
-        tmp[j, pl.ds(0, 96, stride=2), :] = even[j]
-        tmp[j, pl.ds(1, 96, stride=2), :] = odd[j]
-        w["qkv"][0:D, j * LANES : (j + 1) * LANES] = tmp[j, 0:D, :].astype(BF16)
+        tmp[j % 2, pl.ds(0, 96, stride=2), :] = even[j]
+        tmp[j % 2, pl.ds(1, 96, stride=2), :] = odd[j]
+        w["qkv"][0:D, j * LANES : (j + 1) * LANES] = tmp[j % 2, 0:D, :].astype(BF16)
         w["qkv"][D : D + 16, j * LANES : (j + 1) * LANES] = jnp.where(
             first_row, jnp.broadcast_to(bias[j], (16, LANES)), 0.0
         ).astype(BF16)
@@ -136,7 +144,7 @@
     tmp[0, pl.ds(1, 96, stride=2), :] = splice(e[1], e[2])
     tmp[1, pl.ds(1, 96, stride=2), :] = low_half(swap(e[2]))
     w_out = jnp.concatenate([tmp[0, 0:D, :], tmp[1, 0:D, :]], axis=1)
-    w["out_t"][...] = jnp.transpose(w_out)[0:D].astype(BF16)
+    w["out_t"][...] = jnp.transpose(w_out.astype(BF16))[0:D]
 
     g = [rows(1162 + j, 192, 4) for j in range(5)]
     tiles = [splice(g[j], g[j + 1]) for j in range(4)]
@@ -150,9 +158,9 @@
         jnp.broadcast_to(bias_row, (64, 2 * FF)),
         0.0,
     )
-    w["gu_t"][...] = jnp.transpose(jnp.concatenate([gate_up, bias_rows], axis=0))[
+    w["gu_t"][...] = jnp.transpose(jnp.concatenate([gate_up, bias_rows], axis=0).astype(BF16))[
         :, 0 : D + 16
-    ].astype(BF16)
+    ]
 
     e = [rows(1934 + j, 128, 3) for j in range(4)]
     tmp[0, pl.ds(0, 128, stride=2), :] = splice(e[0], e[1])
@@ -161,7 +169,7 @@
     tmp[1, pl.ds(1, 128, stride=2), :] = low_half(e[3])
     w_down = jnp.concatenate([tmp[0, 0:FF, :], tmp[1, 0:FF, :]], axis=1)
     w["down"][...] = w_down[:, 0:D].astype(BF16)
-    w["down_t"][...] = jnp.transpose(w_down)[0:D].astype(BF16)
+    w["down_t"][...] = jnp.transpose(w_down.astype(BF16))[0:D]
 
 
 def row_of(columns):
@@ -302,24 +310,31 @@
             for j, stage in enumerate(stages):
                 u = tick - j
                 if 0 <= u < STEPS:
-                    held[u] = stage(i * STEPS + u, held.get(u))
+                    held[u] = stage(i * STEPS + u, u, held.get(u))
         return carry
 
     lax.fori_loop(0, CHUNKS // STEPS, steps, 0)
 
 
-def forward_qkv(s, w):
-    gain, bias = wide(w["cols"][0]), wide(w["cols"][1])
-
-    def project(c, _):
-        lanes = lanes_of(c)
-        xhat, rstd, normed = norm(s["x"][:, lanes], gain, bias)
-        s["xhat1"][:, lanes] = xhat
-        s["rstd1"][:, lanes] = rstd
-        s["h1"][0:D, lanes] = normed
-        return dot(s["h1"][:, lanes], w["qkv"][...], 0, 0)
-
-    def keep(c, qkv):
+def view(ref, c, u, rows=None):
+    lanes = lanes_of(c) if ref.shape[1] == TOKENS else pl.ds(u * CHUNK, CHUNK)
+    return ref.at[slice(0, ref.shape[0] if rows is None else rows), lanes]
+
+
+def project_stages(s, w):
+    def project(c, u, _):
+        lows = []
+        for half in HALVES:
+            xhat, rstd, low = norm(
+                view(s["x"], c, u).at[:, half][...], w["cols"][0], w["cols"][1]
+            )
+            view(s["xhat1"], c, u).at[:, half][...] = xhat
+            view(s["rstd1"], c, u).at[:, half][...] = rstd
+            lows.append(low)
+        view(s["h1"], c, u, D)[...] = jnp.concatenate(lows, axis=1)
+        return dot(view(s["h1"], c, u)[...], w["qkv"][...], 0, 0)
+
+    def keep(c, u, qkv):
         place = group_rows(c)
         s["q"][:, place, :] = to_groups(qkv[:, 0:D]).astype(BF16)
         for name, start in (("k", 256), ("v", 512)):
@@ -333,7 +348,7 @@
             )
             s[name][:, place, :] = turned.reshape(GROUPS, 2 * GROUP, D).astype(BF16)
 
-    skewed((project, keep))
+    return project, keep
 
 
 def spread(values, masks):
@@ -387,9 +402,7 @@
 
 
 def tail_of(rows, heads):
-    return jnp.transpose(
-        jnp.concatenate([rows * heads[h, 0:1, :] for h in range(HEADS)], axis=0)
-    )
+    return jnp.concatenate([rows * heads[h, 0:1, :] for h in range(HEADS)], axis=0)
 
 
 def heads_joined(tiles, tail, heads, scale=None):
@@ -400,7 +413,7 @@
     if scale is not None:
         main, tail = main * scale, tail * scale
     main = jnp.transpose(main.astype(BF16))
-    tail = jnp.transpose(tail.astype(BF16))
+    tail = tail.astype(BF16)
     last = tail[0:16] * heads[0, 0:1, :]
     for h in range(1, HEADS):
         last += tail[16 * h : 16 * h + 16] * heads[h, 0:1, :]
@@ -449,7 +462,8 @@
                 "queries": queries,
                 "keys": s["k"][g],
                 "turned": jnp.transpose(queries)[:, 0:LANES],
-                "values": jnp.transpose(values),
+                "values": values,
+                "turned_values": jnp.transpose(values),
                 "count": env["count"][pl.ds(g, 1), :],
                 "tiles": [],
             }
@@ -460,10 +474,8 @@
                 load(u)
             at = state[u]
             if t < 4:
-                right = padded(blocks_of(at["turned"], t, halves), t)
-            else:
-                right = tail_of(at["queries"][LANES:GT], env["heads"])
-            return dot(at["keys"], right, 1, 0)
+                return dot(at["keys"], padded(blocks_of(at["turned"], t, halves), t), 1, 0)
+            return dot(at["keys"], tail_of(at["queries"][LANES:GT], env["heads"]), 1, 1)
 
         def mix(item, products):
             u, t = item
@@ -471,12 +483,13 @@
             attention = softmax(collect(products, bits), diff, at["count"])
             s["att"][at["g"], :, t * CHUNK : min((t + 1) * CHUNK, QL)] = attention
             low = spread(attention, env["masks"])
-            left = at["values"][48 * t : 48 * t + 48] if t < 4 else at["values"]
-            at["tiles"].append(dot(left, low, 1, 0))
-            if t == 4:
-                main, last = heads_joined(at["tiles"][0:4], at["tiles"][4], env["heads"])
-                s["mixed"][at["g"], 0:LANES, :] = main
-                s["mixed"][at["g"], LANES:GT, :] = last
+            if t < 4:
+                at["tiles"].append(dot(at["turned_values"][48 * t : 48 * t + 48], low, 1, 0))
+                return
+            tail = dot(low, at["values"], 0, 0)
+            main, last = heads_joined(at["tiles"], tail, env["heads"])
+            s["mixed"][at["g"], 0:LANES, :] = main
+            s["mixed"][at["g"], LANES:GT, :] = last
 
         staged([(u, t) for u in range(UNROLL) for t in range(5)], scores, mix)
         return carry
@@ -484,40 +497,43 @@
     lax.fori_loop(0, GROUPS // UNROLL, step, 0)
 
 
-def forward_rest(s, w, done):
-    gain, bias = wide(w["cols"][3]), wide(w["cols"][4])
-    bias_out, bias_down = wide(w["cols"][2]), wide(w["cols"][5])
-
-    def attended(c, _):
+def rest_stages(s, w, done):
+    def attended(c, u, _):
         mixed = from_groups(s["mixed"][:, group_rows(c), :].astype(F32)).astype(BF16)
         return dot(w["out_t"][...], mixed, 1, 1)
 
-    def normed(c, product):
-        lanes = lanes_of(c)
-        middle = s["x"][:, lanes] + (product + bias_out)
-        xhat, rstd, low = norm(middle, gain, bias)
-        s["middle"][:, lanes] = middle
-        s["xhat2"][:, lanes] = xhat
-        s["rstd2"][:, lanes] = rstd
-        s["h2"][0:D, lanes] = low
-        return dot(w["gu_t"][...], s["h2"][:, lanes], 1, 0)
-
-    def gated(c, gate_up):
-        lanes = lanes_of(c)
-        gate, up = gate_up[0:FF], gate_up[FF:]
-        cdf, slope = gelu_parts(gate)
-        gelu = gate * cdf
-        act = (gelu * up).astype(BF16)
-        s["act"][0:FF, lanes] = act
-        s["gelu"][:, lanes] = gelu
-        s["slope"][:, lanes] = slope * up
+    def normed(c, u, product):
+        lows = []
+        for half in HALVES:
+            middle = view(s["x"], c, u).at[:, half][...] + (product[:, half] + w["cols"][2])
+            view(s["middle"], c, u).at[:, half][...] = middle
+            xhat, rstd, low = norm(middle, w["cols"][3], w["cols"][4])
+            view(s["xhat2"], c, u).at[:, half][...] = xhat
+            view(s["rstd2"], c, u).at[:, half][...] = rstd
+            lows.append(low)
+        view(s["h2"], c, u, D)[...] = jnp.concatenate(lows, axis=1)
+        return dot(w["gu_t"][...], view(s["h2"], c, u)[...], 1, 0)
+
+    def gated(c, u, gate_up):
+        acts = []
+        for r in range(0, FF, BAND):
+            band = pl.ds(r, BAND)
+            gate, up = gate_up[r : r + BAND], gate_up[FF + r : FF + r + BAND]
+            cdf, slope = gelu_parts(gate)
+            gelu = gate * cdf
+            view(s["gelu"], c, u).at[band][...] = gelu
+            view(s["slope"], c, u).at[band][...] = slope * up
+            acts.append((gelu * up).astype(BF16))
+        act = jnp.concatenate(acts, axis=0)
+        view(s["act"], c, u, FF)[...] = act
         return dot(w["down_t"][...], act, 1, 0)
 
-    def finish(c, product):
-        lanes = lanes_of(c)
-        done(c, lanes, s["middle"][:, lanes] + (product + bias_down))
-
-    skewed((attended, normed, gated, finish))
+    def finish(c, u, product):
+        for i, half in enumerate(HALVES):
+            value = view(s["middle"], c, u).at[:, half][...]
+            done(c, u, i, value + (product[:, half] + w["cols"][5]))
+
+    return attended, normed, gated, finish
 
 
 def add_tiles(ref, value):
@@ -530,43 +546,50 @@
     ref[1, :, 0 : D - LANES] += value[:, LANES:D]
 
 
-def backward_rest(s, w, acc, sums):
-    gain = wide(w["cols"][3])
-
-    def down(c, _):
-        lanes = lanes_of(c)
-        branch = s["g"][:, lanes].astype(BF16)
-        return dot(s["act"][:, lanes], branch, 1, 1), dot(w["down"][...], branch, 1, 0)
-
-    def gate_up(c, held):
-        lanes = lanes_of(c)
+def rest_back_stages(s, w, acc, sums):
+    def down(c, u, _):
+        branch = view(s["g"], c, u)[...].astype(BF16)
+        return dot(view(s["act"], c, u)[...], branch, 1, 1), dot(w["down"][...], branch, 1, 0)
+
+    def gate_up(c, u, held):
         grad_down, d_act = held
         add_narrow(acc["down"], grad_down)
-        d_gate_up = jnp.concatenate(
-            [d_act * s["slope"][:, lanes], d_act * s["gelu"][:, lanes]], axis=0
-        ).astype(BF16)
-        return dot(s["h2"][:, lanes], d_gate_up, 1, 1), dot(w["gu"][...], d_gate_up, 1, 0)
-
-    def normed(c, held):
-        lanes = lanes_of(c)
+        gates, ups = [], []
+        for r in range(0, FF, BAND):
+            band = pl.ds(r, BAND)
+            part = d_act[r : r + BAND]
+            gates.append((part * view(s["slope"], c, u).at[band][...]).astype(BF16))
+            ups.append((part * view(s["gelu"], c, u).at[band][...]).astype(BF16))
+        d_gate_up = jnp.concatenate(gates + ups, axis=0)
+        return dot(view(s["h2"], c, u)[...], d_gate_up, 1, 1), dot(w["gu"][...], d_gate_up, 1, 0)
+
+    def normed(c, u, held):
         grad_gu, d_normed = held
         add_tiles(acc["gu"], grad_gu)
-        xhat = s["xhat2"][:, lanes]
-        sums[2] += fold(d_normed * xhat)
-        sums[3] += fold(d_normed)
-        d_middle = s["g"][:, lanes] + norm_back(d_normed, xhat, s["rstd2"][:, lanes], gain)
-        s["g"][:, lanes] = d_middle
-        d_attended = d_middle.astype(BF16)
-        sums[4] += fold(d_attended.astype(F32))
+        lows = []
+        for half in HALVES:
+            xhat = view(s["xhat2"], c, u).at[:, half][...]
+            part = d_normed[:, half]
+            sums[2] += part * xhat
+            sums[3] += part
+            g = view(s["g"], c, u).at[:, half]
+            d_middle = g[...] + norm_back(
+                part, xhat, view(s["rstd2"], c, u).at[:, half][...], w["cols"][3]
+            )
+            g[...] = d_middle
+            low = d_middle.astype(BF16)
+            sums[4] += low.astype(F32)
+            lows.append(low)
+        d_attended = jnp.concatenate(lows, axis=1)
         mixed = from_groups(s["mixed"][:, group_rows(c), :].astype(F32)).astype(BF16)
         return dot(d_attended, w["out_t"][...], 0, 0), dot(d_attended, mixed, 1, 0)
 
-    def finish(c, held):
+    def finish(c, u, held):
         d_mixed, grad_out = held
         s["dm"][:, group_rows(c), :] = to_groups(d_mixed).astype(BF16)
         acc["out_t"][...] += grad_out
 
-    skewed((down, gate_up, normed, finish))
+    return down, gate_up, normed, finish
 
 
 def backward_attention(s, env):
@@ -584,6 +607,7 @@
                 "g": g,
                 "queries": queries,
                 "grads": grads,
+                "keys": keys,
                 "values": s["v"][g],
                 "turned": jnp.transpose(queries)[:, 0:LANES],
                 "turned_grads": jnp.transpose(grads)[:, 0:LANES],
@@ -600,10 +624,9 @@
             at = state[u]
             if t < 4:
                 block = blocks_of(at["turned_grads"], t, halves)
-                right = padded(block, t)
-            else:
-                block = right = tail_of(at["grads"][LANES:GT], env["heads"])
-            return block, dot(at["values"], right, 1, 0)
+                return block, dot(at["values"], padded(block, t), 1, 0)
+            block = tail_of(at["grads"][LANES:GT], env["heads"])
+            return block, dot(at["values"], block, 1, 1)
 
         def back(item, result):
             u, t = item
@@ -613,27 +636,27 @@
             weighted = attention * jnp.concatenate(collect(product, bits), axis=0)
             total = jnp.sum(weighted, axis=0, keepdims=True)
             d_score = spread(weighted - attention * total, env["masks"])
-            at["dv"].append(dot(grad_block, spread(attention, env["masks"]), 1, 1))
+            low = spread(attention, env["masks"])
             if t < 4:
-                block = blocks_of(at["turned"], t, halves)
-                left = at["turned_keys"][48 * t : 48 * t + 48]
-            else:
-                block = tail_of(at["queries"][LANES:GT], env["heads"])
-                left = at["turned_keys"]
-            at["dk"].append(dot(block, d_score, 1, 1))
-            at["dq"].append(dot(left, d_score, 1, 0))
-            if t == 4:
-                finish(at)
-
-        def finish(at):
+                at["dv"].append(dot(grad_block, low, 1, 1))
+                at["dk"].append(dot(blocks_of(at["turned"], t, halves), d_score, 1, 1))
+                at["dq"].append(dot(at["turned_keys"][48 * t : 48 * t + 48], d_score, 1, 0))
+                return
+            d_values = dot(low, grad_block, 1, 0)
+            d_keys = dot(d_score, tail_of(at["queries"][LANES:GT], env["heads"]), 1, 0)
+            finish(at, d_values, d_keys, dot(d_score, at["keys"], 0, 0))
+
+        def finish(at, d_values, d_keys, tail):
             g = at["g"]
-            main, last = heads_joined(at["dq"][0:4], at["dq"][4], env["heads"], SCALE)
+            main, last = heads_joined(at["dq"], tail, env["heads"], SCALE)
             s["dqkv"][g, 0:LANES, 0:D] = main
             s["dqkv"][g, LANES:GT, 0:D] = last
-            d_keys = (jnp.concatenate(at["dk"][0:4], axis=0) + at["dk"][4]) * SCALE
-            d_values = jnp.concatenate(at["dv"][0:4], axis=0) + at["dv"][4]
-            for value, start in ((d_keys, 256), (d_values, 512)):
-                slots = jnp.transpose(value.astype(BF16)).astype(F32).reshape(SLOTS, GROUP, D)
+            for parts, own, start, scale in (
+                (at["dk"], d_keys, 256, SCALE),
+                (at["dv"], d_values, 512, 1.0),
+            ):
+                value = jnp.transpose(jnp.concatenate(parts, axis=0)) + own
+                slots = (value * scale).reshape(SLOTS, GROUP, D)
                 turned = [
                     slots[k] if k % GROUP == 0 else pltpu.roll(slots[k], GROUP - k % GROUP, 0)
                     for k in range(SLOTS)
@@ -646,28 +669,27 @@
     lax.fori_loop(0, GROUPS // UNROLL, step, 0)
 
 
-def backward_qkv(s, w, acc, sums, done):
-    gain = wide(w["cols"][0])
-
-    def products(c, _):
+def project_back_stages(s, w, acc, sums, done):
+    def products(c, u, _):
         d_qkv = from_groups(s["dqkv"][:, group_rows(c), :].astype(F32)).astype(BF16)
-        return dot(s["h1"][:, lanes_of(c)], d_qkv, 1, 0), dot(w["qkv"][0:D, :], d_qkv, 1, 1)
-
-    def finish(c, held):
-        lanes = lanes_of(c)
+        return dot(view(s["h1"], c, u)[...], d_qkv, 1, 0), dot(w["qkv"][0:D, :], d_qkv, 1, 1)
+
+    def finish(c, u, held):
         grad_qkv, d_normed = held
         add_tiles(acc["qkv"], grad_qkv)
-        xhat = s["xhat1"][:, lanes]
-        sums[0] += fold(d_normed * xhat)
-        sums[1] += fold(d_normed)
-        done(
-            c, lanes, s["g"][:, lanes] + norm_back(d_normed, xhat, s["rstd1"][:, lanes], gain)
-        )
-
-    skewed((products, finish))
-
-
-def per_layer():
+        for i, half in enumerate(HALVES):
+            xhat = view(s["xhat1"], c, u).at[:, half][...]
+            part = d_normed[:, half]
+            sums[0] += part * xhat
+            sums[1] += part
+            back = norm_back(part, xhat, view(s["rstd1"], c, u).at[:, half][...], w["cols"][0])
+            done(c, u, i, view(s["g"], c, u).at[:, half][...] + back)
+
+    return products, finish
+
+
+def per_layer(layer):
+    room = TOKENS if layer < LAYERS - 1 else STEPS * CHUNK
     return {
         "xhat1": ((D, TOKENS), F32),
         "rstd1": ((1, TOKENS), F32),
@@ -677,12 +699,12 @@
         "v": ((GROUPS, GT, D), BF16),
         "att": ((GROUPS, 24, QL), F32),
         "mixed": ((GROUPS, GT, D), BF16),
-        "xhat2": ((D, TOKENS), F32),
-        "rstd2": ((1, TOKENS), F32),
-        "h2": ((D + 16, TOKENS), BF16),
-        "act": ((FF + 16, TOKENS), BF16),
-        "gelu": ((FF, TOKENS), F32),
-        "slope": ((FF, TOKENS), F32),
+        "xhat2": ((D, room), F32),
+        "rstd2": ((1, room), F32),
+        "h2": ((D + 16, room), BF16),
+        "act": ((FF + 16, room), BF16),
+        "gelu": ((FF, room), F32),
+        "slope": ((FF, room), F32),
     }
 
 
@@ -704,10 +726,13 @@
         "out_t": ((D, D), F32),
         "gu": ((4, D + 16, LANES), F32),
         "down": ((2, FF + 16, LANES), F32),
+        "sums": ((5, D, LANES), F32),
     }
 
 
 def common():
+    full = (SEQ, D, ROWS)
+    blocks = (4, 4, LAYERS, BLOCK, LANES)
     return {
         "halves": ((2, 16, LANES), BF16),
         "heads": ((HEADS, 16, D), BF16),
@@ -715,13 +740,20 @@
         "diff": ((GROUP, CHUNK), jnp.int32),
         "count": ((GROUPS, CHUNK), F32),
         "dm": ((GROUPS, GT, D), BF16),
+        "dqkv": ((GROUPS, GT, 6 * LANES), BF16),
         "x": ((D, TOKENS), F32),
-        "middle": ((D, TOKENS), F32),
-        "dqkv": ((GROUPS, GT, 6 * LANES), BF16),
+        "middle": ((D, STEPS * CHUNK), F32),
         "g": ((D, TOKENS), F32),
-        "sums": ((5, D, LANES), F32),
         "flat": ((FLAT + 8, LANES), F32),
-        "tmp": ((6, FF, LANES), F32),
+        "tmp": ((2, FF, LANES), F32),
+        "tokens": (full, BF16),
+        "out_grad": (full, BF16),
+        "own": (blocks, BF16),
+        "other": (blocks, BF16),
+        "out": ((SLOTS, D, ROWS), F32),
+        "in_grad": ((SLOTS, D, ROWS), F32),
+        "keep": (blocks, BF16),
+        "give": (blocks, BF16),
     }
 
 
@@ -729,16 +761,17 @@
     shapes, names = [], []
     for prefix, table in (
         ("common", common()),
-        ("acc", accumulators()),
-        ("s0", per_layer()),
-        ("s1", per_layer()),
+        ("acc0", accumulators()),
+        ("acc1", accumulators()),
+        ("s0", per_layer(0)),
+        ("s1", per_layer(1)),
         ("w0", weights()),
         ("w1", weights()),
     ):
         for name, (shape, kind) in table.items():
             names.append((prefix, name))
             shapes.append(pltpu.VMEM(shape, kind))
-    return names, shapes
+    return names, shapes + [pltpu.SemaphoreType.DMA((10,))]
 
 
 def init_env(env, count):
@@ -771,88 +804,161 @@
     ref[rows:, :] = jnp.where(mark, 1.0, 0.0).astype(BF16)
 
 
-def kernel(
-    names, place, tokens, out_grad, own, other, row_scale, count, out, in_grad, keep_out, give_out, *scratch
-):
+def scales(ids, table_counts):
+    counts = table_counts.astype(F32)
+    tables = counts.shape[1]
+    high = jnp.floor(counts * (1.0 / 32.0))
+    table = lax.broadcasted_iota(jnp.int32, (tables, ROWS), 0)
+    match = jnp.where(table == ids, 1.0, 0.0).astype(BF16)
+
+    def pick(values):
+        return dot(jnp.broadcast_to(values, (8, tables)).astype(BF16), match, 1, 0)[0:1]
+
+    mine = 32.0 * pick(high) + pick(counts - 32.0 * high)
+    return jnp.sqrt(jnp.sum(counts, axis=1, keepdims=True) * (1.0 / tables) / mine)
+
+
+def kernel(names, four, *refs):
+    inputs, outputs, scratch, sems = refs[0:7], refs[7:11], refs[11:-1], refs[-1]
+    tokens, out_grad, own, other, feat_count, table_ids, table_counts = inputs
+    out, in_grad, keep_out, give_out = outputs
     table = {}
     for (prefix, name), ref in zip(names, scratch):
         table.setdefault(prefix, {})[name] = ref
-    env, acc = table["common"], table["acc"]
+    env = table["common"]
+    acc = [table["acc0"], table["acc1"]]
     s, w = [table["s0"], table["s1"]], [table["w0"], table["w1"]]
-    sums = env["sums"]
-
-    init_env(env, count[...])
-    valid_slots = count[...]
-    env["dqkv"][...] = jnp.zeros_like(env["dqkv"])
+    sums = [part["sums"] for part in acc]
+    place = (lax.axis_index("z"), lax.axis_index("core")) if four else (0, 0)
+
+    copies = [
+        pltpu.make_async_copy(source, env[name], sems.at[i])
+        for i, (source, name) in enumerate(
+            ((own, "own"), (other, "other"), (tokens, "tokens"), (out_grad, "out_grad"))
+        )
+    ]
+    for copy in copies:
+        copy.start()
+
+    count = feat_count[...].astype(F32)
+    init_env(env, count)
+    pad = jnp.zeros((GROUPS, GT, 2 * LANES - D), BF16)
+    for part in range(3):
+        env["dqkv"][:, :, 2 * LANES * part + D : 2 * LANES * (part + 1)] = pad
     for layer in range(LAYERS):
         ones_below(s[layer]["h1"], D)
         ones_below(s[layer]["h2"], D)
         ones_below(s[layer]["act"], FF)
-        gather_flat(own, other, place, layer, env["flat"])
+        for ref in acc[layer].values():
+            ref[...] = jnp.zeros_like(ref)
+    env["x"][:, SEQ * ROWS :] = jnp.zeros((D, ROWS), F32)
+    env["g"][:, SEQ * ROWS :] = jnp.zeros((D, ROWS), F32)
+    row_scale = scales(table_ids[...], table_counts[...])
+    copies[0].wait()
+    copies[1].wait()
+    for layer in range(LAYERS):
+        gather_flat(env["own"], env["other"], place, layer, env["flat"])
         unpack(env["flat"], w[layer], env["tmp"])
-    for slot in range(SLOTS):
+    copies[2].wait()
+    copies[3].wait()
+    for slot in range(SEQ):
         lanes = slice(slot * ROWS, (slot + 1) * ROWS)
-        if slot < SEQ:
-            env["x"][:, lanes] = tokens[slot].astype(F32)
-            keep = jnp.where(valid_slots >= float(slot), row_scale[...], 0.0)
-            env["g"][:, lanes] = out_grad[slot].astype(F32) * keep
-        else:
-            env["x"][:, lanes] = jnp.zeros((D, ROWS), F32)
-            env["g"][:, lanes] = jnp.zeros((D, ROWS), F32)
+        env["x"][:, lanes] = env["tokens"][slot].astype(F32)
+        keep = jnp.where(count >= float(slot), row_scale, 0.0)
+        env["g"][:, lanes] = env["out_grad"][slot].astype(F32) * keep
 
     def put(target):
-        def done(c, lanes, value):
-            target[2 * c] = value[:, 0:ROWS]
-
-            @pl.when(c < CHUNKS - 1)
-            def _():
-                target[2 * c + 1] = value[:, ROWS:]
+        def done(c, u, i, value):
+            target[2 * c + i] = value
 
         return done
 
-    def keep(target):
-        def done(c, lanes, value):
-            target[:, lanes] = value
+    def set_to(target):
+        def done(c, u, i, value):
+            view(target, c, u).at[:, HALVES[i]][...] = value
 
         return done
 
-    for layer in range(LAYERS):
-        state = dict(s[layer], x=env["x"], middle=env["middle"])
-        forward_qkv(state, w[layer])
-        forward_attention(state, env)
-        last = layer == LAYERS - 1
-        forward_rest(state, w[layer], put(out) if last else keep(env["x"]))
-    for layer in reversed(range(LAYERS)):
-        sums[...] = jnp.zeros_like(sums)
-        for ref in acc.values():
-            ref[...] = jnp.zeros_like(ref)
-        state = dict(s[layer], g=env["g"], dm=env["dm"], dqkv=env["dqkv"])
-        backward_rest(state, w[layer], acc, sums)
-        backward_attention(state, env)
-        backward_qkv(
-            state, w[layer], acc, sums, put(in_grad) if layer == 0 else keep(env["g"])
-        )
-        pack(env["flat"], acc, sums, env["tmp"])
-        scatter_blocks(env["flat"], place, layer, keep_out, give_out)
-
-
-def run_kernel(place, tokens, out_grad, own, other, row_scale, count):
+    shared = {name: env[name] for name in ("x", "middle", "g", "dm", "dqkv")}
+    s = [dict(part, **shared) for part in s]
+
+    skewed(project_stages(s[0], w[0]))
+    forward_attention(s[0], env)
+    attended, normed, gated, finish = rest_stages(s[0], w[0], set_to(env["x"]))
+    project, hold = project_stages(s[1], w[1])
+
+    def finish_project(c, u, held):
+        finish(c, u, held)
+        return project(c, u, None)
+
+    skewed((attended, normed, gated, finish_project, hold))
+    forward_attention(s[1], env)
+    attended, normed, gated, finish_out = rest_stages(s[1], w[1], put(env["out"]))
+    down, gate_up, normed_back, finish_back = rest_back_stages(s[1], w[1], acc[1], sums[1])
+
+    def gated_down(c, u, held):
+        return gated(c, u, held), down(c, u, None)
+
+    def finish_gate_up(c, u, held):
+        finish_out(c, u, held[0])
+        return gate_up(c, u, held[1])
+
+    skewed((attended, normed, gated_down, finish_gate_up, normed_back, finish_back))
+    out_copy = pltpu.make_async_copy(env["out"].at[0:SEQ], out, sems.at[4])
+    out_copy.start()
+    backward_attention(s[1], env)
+    products, finish_project_back = project_back_stages(
+        s[1], w[1], acc[1], sums[1], set_to(env["g"])
+    )
+    down, gate_up, normed_back, finish_back = rest_back_stages(s[0], w[0], acc[0], sums[0])
+
+    def finish_down(c, u, held):
+        finish_project_back(c, u, held)
+        return down(c, u, None)
+
+    skewed((products, finish_down, gate_up, normed_back, finish_back))
+
+    def send(layer):
+        pack(env["flat"], acc[layer], sums[layer], env["tmp"])
+        scatter_blocks(env["flat"], place, layer, env["keep"], env["give"])
+        started = []
+        for i, (name, target) in enumerate((("keep", keep_out), ("give", give_out))):
+            started.append(
+                pltpu.make_async_copy(
+                    env[name].at[:, :, layer], target.at[:, :, layer], sems.at[5 + 2 * layer + i]
+                )
+            )
+            started[-1].start()
+        return started
+
+    started = [out_copy] + send(1)
+    backward_attention(s[0], env)
+    skewed(project_back_stages(s[0], w[0], acc[0], sums[0], put(env["in_grad"])))
+    last = pltpu.make_async_copy(env["in_grad"].at[0:SEQ], in_grad, sems.at[9])
+    last.start()
+    started += send(0) + [last]
+    for copy in started:
+        copy.wait()
+
+
+def run_kernel(four, tokens, out_grad, own, other, count, ids, table_counts):
     names, scratch = make_scratch()
     full = jax.ShapeDtypeStruct((SEQ, D, ROWS), F32)
     blocks = jax.ShapeDtypeStruct(own.shape, BF16)
 
     def body(*refs):
-        kernel(names, *refs)
+        kernel(names, four, *refs)
 
     vmem = pl.BlockSpec(memory_space=pltpu.VMEM)
+    anywhere = pl.BlockSpec(memory_space=pl.ANY)
     return pl.pallas_call(
         body,
         out_shape=(full, full, blocks, blocks),
-        in_specs=[pl.BlockSpec(memory_space=pltpu.SMEM)] + [vmem] * 6,
-        out_specs=[vmem] * 4,
+        in_specs=[anywhere] * 4 + [vmem] * 3,
+        out_specs=[anywhere] * 4,
         scratch_shapes=scratch,
         compiler_params=pltpu.CompilerParams(vmem_limit_bytes=64 * 1024 * 1024 - 256 * 1024),
-    )(place, tokens, out_grad, own, other, row_scale, count)
+    )(tokens, out_grad, own, other, count, ids, table_counts)
 
 
 def halves_of_pairs(flat):
@@ -912,17 +1018,10 @@
 
 def body(axes, tokens, out_grad, flat_params, feat_count, table_ids, table_counts):
     four = "core" in axes
-    counts_float = table_counts.astype(F32)
-    table_index = jnp.arange(table_counts.shape[0], dtype=jnp.int32)
-    match = (table_ids[None, :] == table_index[:, None]).astype(F32)
-    row_count = jnp.sum(match * counts_float[:, None], axis=0)
-    row_scale = jnp.sqrt(jnp.mean(counts_float) / row_count)[None, :]
-    count = feat_count.astype(F32)[None, :]
+    count, ids = feat_count[None, :], table_ids[None, :]
     if four:
-        place = jnp.stack([lax.axis_index("z"), lax.axis_index("core")]).astype(jnp.int32)
         own, other = gather_pairs(flat_params)
     else:
-        place = jnp.zeros((2,), jnp.int32)
         own, other = halves_of_pairs(lax.all_gather(flat_params, axes, axis=1, tiled=True))
         turn = jnp.array([0, 2, 1, 3])
         own, other = own[:, turn], other[:, turn]
@@ -930,13 +1029,14 @@
     turned_grad = jnp.transpose(out_grad, (1, 2, 0))
     results = [
         run_kernel(
-            place,
+            four,
             turned[:, :, at : at + ROWS],
             turned_grad[:, :, at : at + ROWS],
             own,
             other,
-            row_scale[:, at : at + ROWS],
             count[:, at : at + ROWS],
+            ids[:, at : at + ROWS],
+            table_counts[None, :],
         )
         for at in range(0, tokens.shape[0], ROWS)
     ]

time: 116 us -> 111 us (0.957)
  Pallas kernels: 58 us -> 53 us
  waiting for transfers between devices: 23 us -> 27.3 us
  other arithmetic: 7.76 us -> 3.99 us
    pallas_call x1, Pallas kernels: 58 us -> 53 us  [run_kernel(): pl.pallas_call(body, out_shape=(full, full, blocks, blocks), in_specs=[an...]
    ppermute x6, waiting for transfers between devices: 12.9 us -> 17.3 us  [swap_along(): return lax.ppermute(x, axis, pairs)]
    reduce_sum x2 -> x0, other arithmetic: 1.35 us -> none  [the longest x1 1.26 us: body(): row_scale = jnp.sqrt(jnp.mean(counts_float) / row_count)[None, :]]
  transfers between devices with their start and end apart: 7 -> 7, of which waited for: 7 -> 7; matrix products, arithmetic and copies ran while one was open for 3% -> 0% of each run, Pallas kernels for 0% -> 0%
where the time goes in v4:
time: 111 us
  Pallas kernels  53 us (48%)
  waiting for transfers between devices  27.3 us (25%)
  starting transfers between devices  12.2 us (11%)
  blocking collectives  11.6 us (10%)
  other arithmetic  3.99 us (4%)
  local copies, waits for them, and re-layouts  1.8 us (2%)
    pallas_call x1, Pallas kernels, run_kernel(): pl.pallas_call(body, out_shape=(full, full, blocks, blocks), in_specs=[an...  53 us
    ppermute x6, waiting for transfers between devices, swap_along(): return lax.ppermute(x, axis, pairs)  17.3 us
    all_gather x1, blocking collectives, gather_pairs(): own = lax.all_gather(part, ('x', 'y'), axis=0, tiled=False)  11.6 us
    all_to_all x1, waiting for transfers between devices, reduce_pairs(): part = lax.all_to_all(part, ('x', 'y'), 0, 0, tiled=True)  9.93 us
    ppermute x6, starting transfers between devices, swap_along(): return lax.ppermute(x, axis, pairs)  8.68 us
    all_to_all x1, starting transfers between devices, reduce_pairs(): part = lax.all_to_all(part, ('x', 'y'), 0, 0, tiled=True)  3.48 us
  transfers between devices with their start and end apart: 7, of which 7 were waited for; matrix products, arithmetic and copies ran while one was open for 0% of the time, Pallas kernels for 0%

profile of v4, /device:TPU:0, one launch (start us, length us, event | category | flops | bytes accessed | tf_op | source)
XLA Modules:
  0.0 110.6 jit_solution(14428348035975610396)
XLA Ops:
  0.6 1.0 fusion
  1.6 4.1 %collective-permute-start = (bf16[1,2,80,128]{3,2,1,0:T(8,128)(2,1)S(1)}, bf16[1,2,80,128]{3,2,1,0:T(8,128)(2,1)S(1)}, u32[]{:S(2)}, u32[]{:S(2)}) collective-permute-start(bf16[1,2,80,128]{3,2,1,0:T(8,128)(2,1)S(1)} %copy.14), channel_id=1, source_target_pairs={{0,16},{8,24},{16,0},{24,8},{1,17},{9,25},{17,1},{25,9},{2,18},{10... | collective-permute-start | bytes 122888 | tf_op jit(solution)/shard_map/ppermute | solution.py:985
  5.7 2.4 %collective-permute-done = bf16[1,2,80,128]{3,2,1,0:T(8,128)(2,1)S(1)} collective-permute-done((bf16[1,2,80,128]{3,2,1,0:T(8,128)(2,1)S(1)}, bf16[1,2,80,128]{3,2,1,0:T(8,128)(2,1)S(1)}, u32[]{:S(2)}, u32[]{:S(2)}) %collective-permute-start) | collective-permute-done | bytes 40992 | tf_op jit(solution)/shard_map/ppermute | solution.py:985
  8.2 1.5 %collective-permute-start.1 = (bf16[2,2,80,128]{3,2,1,0:T(8,128)(2,1)S(1)}, bf16[2,2,80,128]{3,2,1,0:T(8,128)(2,1)S(1)}, u32[]{:S(2)}, u32[]{:S(2)}) collective-permute-start(bf16[2,2,80,128]{3,2,1,0:T(8,128)(2,1)S(1)} %pad_maximum_fusion.1), channel_id=1, source_target_pairs={{0,8},{8,0},{16,24},{24,16},{1,9},{9,1},{17,25},{25,17},{2,10},{10... | collective-permute-start | bytes 245768 | tf_op jit(solution)/shard_map/ppermute | solution.py:985
  9.7 3.0 %collective-permute-done.1 = bf16[2,2,80,128]{3,2,1,0:T(8,128)(2,1)S(1)} collective-permute-done((bf16[2,2,80,128]{3,2,1,0:T(8,128)(2,1)S(1)}, bf16[2,2,80,128]{3,2,1,0:T(8,128)(2,1)S(1)}, u32[]{:S(2)}, u32[]{:S(2)}) %collective-permute-start.1) | collective-permute-done | bytes 81952 | tf_op jit(solution)/shard_map/ppermute | solution.py:985
  12.7 11.6 %all-gather = bf16[16,2,80,128]{3,2,1,0:T(8,128)(2,1)S(1)} all-gather(bf16[4,2,80,128]{3,2,1,0:T(8,128)(2,1)S(1)} %pad_maximum_fusion), channel_id=2, replica_groups=mesh['z'=4,'x'=2,'y'=2,'core'=2] {'x','y'}, dimensions={0}, use_global_device_ids=true | all-gather | bytes 819200 | tf_op jit(solution)/shard_map/all_gather | solution.py:998
  24.3 0.0 copy-start
  24.3 0.8 copy-done
  25.1 0.0 collective-permute-start.2
  25.1 2.1 %collective-permute-done.2.refs_3_ = bf16[4,4,2,80,128]{4,3,2,1,0:T(8,128)(2,1)S(1)} collective-permute-done((bf16[4,4,2,80,128]{4,3,2,1,0:T(8,128)(2,1)S(1)}, bf16[4,4,2,80,128]{4,3,2,1,0:T(8,128)(2,1)S(1)}, u32[]{:S(2)}, u32[]{:S(2)}) %collective-permute-start.2) | collective-permute-done | bytes 655392 | tf_op jit(solution)/shard_map/ppermute | solution.py:985
  27.2 0.0 copy-start.1
  27.2 0.9 copy-done.1
  28.1 53.0 %shard_map.85 = (f32[17,192,128]{2,1,0:T(8,128)}, f32[17,192,128]{2,1,0:T(8,128)}, bf16[4,4,2,80,128]{4,3,2,1,0:T(8,128)(2,1)}, bf16[4,4,2,80,128]{4,3,2,1,0:T(8,128)(2,1)}) custom-call(bf16[17,192,128]{2,1,0:T(8,128)(2,1)} %bitcast.22, bf16[17,192,128]{2,1,0:T(8,128)(2,1)} %bitcast.23, bf16[4,4,2,80,128]{4,3,2,1,0:T(8,128)(2,1)} %bitcast.21, ...), custom_call_target="tpu_custom_call" | custom-call | tf_op jit(solution)/shard_map/pallas_call | solution.py:954
  81.2 0.2 collective-permute-start.3
  81.3 2.2 %collective-permute-done.3 = bf16[4,4,2,80,128]{4,3,2,1,0:T(8,128)(2,1)S(1)} collective-permute-done((bf16[4,4,2,80,128]{4,3,2,1,0:T(8,128)(2,1)}, bf16[4,4,2,80,128]{4,3,2,1,0:T(8,128)(2,1)S(1)}, u32[]{:S(2)}, u32[]{:S(2)}) %collective-permute-start.3) | collective-permute-done | bytes 655392 | tf_op jit(solution)/shard_map/ppermute | solution.py:985
  83.5 2.1 %add_convert_fusion = bf16[4,4,2,80,128]{4,3,2,1,0:T(8,128)(2,1)} fusion(bf16[4,4,2,80,128]{4,3,2,1,0:T(8,128)(2,1)S(1)} %collective-permute-done.3, bf16[4,4,2,80,128]{4,3,2,1,0:T(8,128)(2,1)} %get-tuple-element.9), kind=kLoop, calls=%fused_computation.1 | loop fusion | flops 1310720 | bytes 1966080 | tf_op jit(solution)/shard_map/convert_element_type | solution.py:1004
  85.6 3.5 %all-to-all-start = ((bf16[4,4,2,80,128]{4,3,2,1,0:T(8,128)(2,1)}), bf16[4,4,2,80,128]{4,3,2,1,0:T(8,128)(2,1)S(1)}, u32[]{:S(2)}, u32[]{:S(2)}) async-start(bf16[4,4,2,80,128]{4,3,2,1,0:T(8,128)(2,1)} %add_convert_fusion), calls=%async_computation | async-start | bytes 1310720 | tf_op jit(solution)/shard_map/all_to_all | solution.py:1005
  89.2 9.9 %all-to-all-done = bf16[4,4,2,80,128]{4,3,2,1,0:T(8,128)(2,1)S(1)} async-done(((bf16[4,4,2,80,128]{4,3,2,1,0:T(8,128)(2,1)}), bf16[4,4,2,80,128]{4,3,2,1,0:T(8,128)(2,1)S(1)}, u32[]{:S(2)}, u32[]{:S(2)}) %all-to-all-start) | async-done | bytes 655392 | tf_op jit(solution)/shard_map/all_to_all | solution.py:1005
  99.1 0.1 convert_reduce_fusion
  99.2 2.4 %collective-permute-start.4 = (bf16[2,2,80,128]{3,2,1,0:T(8,128)(2,1)S(1)}, bf16[2,2,80,128]{3,2,1,0:T(8,128)(2,1)S(1)}, u32[]{:S(2)}, u32[]{:S(2)}) collective-permute-start(bf16[2,2,80,128]{3,2,1,0:T(8,128)(2,1)S(1)} %dynamic-slice_convert_fusion), channel_id=1, source_target_pairs={{0,16},{8,24},{16,0},{24,8},{1,17},{9,25},{17,1},{25,9},{2,18},{10... | collective-permute-start | bytes 245768 | tf_op jit(solution)/shard_map/ppermute | solution.py:985
  101.6 4.0 %collective-permute-done.4 = bf16[2,2,80,128]{3,2,1,0:T(8,128)(2,1)S(1)} collective-permute-done((bf16[2,2,80,128]{3,2,1,0:T(8,128)(2,1)S(1)}, bf16[2,2,80,128]{3,2,1,0:T(8,128)(2,1)S(1)}, u32[]{:S(2)}, u32[]{:S(2)}) %collective-permute-start.4) | collective-permute-done | bytes 81952 | tf_op jit(solution)/shard_map/ppermute | solution.py:985
  105.7 0.4 collective-permute-start.5
  106.1 3.6 %collective-permute-done.5 = bf16[1,2,80,128]{3,2,1,0:T(8,128)(2,1)S(1)} collective-permute-done((bf16[1,2,80,128]{3,2,1,0:T(8,128)(2,1)S(1)}, bf16[1,2,80,128]{3,2,1,0:T(8,128)(2,1)S(1)}, u32[]{:S(2)}, u32[]{:S(2)}) %collective-permute-start.5) | collective-permute-done | bytes 40992 | tf_op jit(solution)/shard_map/ppermute | solution.py:985
  109.8 0.8 slice_select_fusion
  (8 shorter events, 0.1 us)
Async XLA Ops:
  1.6 6.5 %collective-permute-start = (bf16[1,2,80,128]{3,2,1,0:T(8,128)(2,1)S(1)}, bf16[1,2,80,128]{3,2,1,0:T(8,128)(2,1)S(1)}, u32[]{:S(2)}, u32[]{:S(2)}) collective-permute-start(bf16[1,2,80,128]{3,2,1,0:T(8,128)(2,1)S(1)} %copy.14), channel_id=1, source_target_pairs={{0,16},{8,24},{16,0},{24,8},{1,17},{9,25},{17,1},{25,9},{2,18},{10... | collective-permute-start | bytes 122888 | tf_op jit(solution)/shard_map/ppermute | solution.py:985
  8.2 4.5 %collective-permute-start.1 = (bf16[2,2,80,128]{3,2,1,0:T(8,128)(2,1)S(1)}, bf16[2,2,80,128]{3,2,1,0:T(8,128)(2,1)S(1)}, u32[]{:S(2)}, u32[]{:S(2)}) collective-permute-start(bf16[2,2,80,128]{3,2,1,0:T(8,128)(2,1)S(1)} %pad_maximum_fusion.1), channel_id=1, source_target_pairs={{0,8},{8,0},{16,24},{24,16},{1,9},{9,1},{17,25},{25,17},{2,10},{10... | collective-permute-start | bytes 245768 | tf_op jit(solution)/shard_map/ppermute | solution.py:985
  24.3 0.8 copy-start
  25.1 2.1 %collective-permute-start.2 = (bf16[4,4,2,80,128]{4,3,2,1,0:T(8,128)(2,1)S(1)}, bf16[4,4,2,80,128]{4,3,2,1,0:T(8,128)(2,1)S(1)}, u32[]{:S(2)}, u32[]{:S(2)}) collective-permute-start(bf16[4,4,2,80,128]{4,3,2,1,0:T(8,128)(2,1)S(1)} %bitcast.20), channel_id=1, source_target_pairs={{0,1},{1,0},{2,3},{3,2},{4,5},{5,4},{6,7},{7,6},{8,9},{9,8},{10,11... | collective-permute-start | bytes 1966088 | tf_op jit(solution)/shard_map/ppermute | solution.py:985
  27.2 0.9 copy-start.1
  81.2 2.4 %collective-permute-start.3 = (bf16[4,4,2,80,128]{4,3,2,1,0:T(8,128)(2,1)}, bf16[4,4,2,80,128]{4,3,2,1,0:T(8,128)(2,1)S(1)}, u32[]{:S(2)}, u32[]{:S(2)}) collective-permute-start(bf16[4,4,2,80,128]{4,3,2,1,0:T(8,128)(2,1)} %get-tuple-element.10), channel_id=1, source_target_pairs={{0,1},{1,0},{2,3},{3,2},{4,5},{5,4},{6,7},{7,6},{8,9},{9,8},{10,11... | collective-permute-start | bytes 1966088 | tf_op jit(solution)/shard_map/ppermute | solution.py:985
  85.6 13.5 %all-to-all-start = ((bf16[4,4,2,80,128]{4,3,2,1,0:T(8,128)(2,1)}), bf16[4,4,2,80,128]{4,3,2,1,0:T(8,128)(2,1)S(1)}, u32[]{:S(2)}, u32[]{:S(2)}) async-start(bf16[4,4,2,80,128]{4,3,2,1,0:T(8,128)(2,1)} %add_convert_fusion), calls=%async_computation | async-start | bytes 1310720 | tf_op jit(solution)/shard_map/all_to_all | solution.py:1005
  99.2 6.4 %collective-permute-start.4 = (bf16[2,2,80,128]{3,2,1,0:T(8,128)(2,1)S(1)}, bf16[2,2,80,128]{3,2,1,0:T(8,128)(2,1)S(1)}, u32[]{:S(2)}, u32[]{:S(2)}) collective-permute-start(bf16[2,2,80,128]{3,2,1,0:T(8,128)(2,1)S(1)} %dynamic-slice_convert_fusion), channel_id=1, source_target_pairs={{0,16},{8,24},{16,0},{24,8},{1,17},{9,25},{17,1},{25,9},{2,18},{10... | collective-permute-start | bytes 245768 | tf_op jit(solution)/shard_map/ppermute | solution.py:985
  105.7 4.1 %collective-permute-start.5 = (bf16[1,2,80,128]{3,2,1,0:T(8,128)(2,1)S(1)}, bf16[1,2,80,128]{3,2,1,0:T(8,128)(2,1)S(1)}, u32[]{:S(2)}, u32[]{:S(2)}) collective-permute-start(bf16[1,2,80,128]{3,2,1,0:T(8,128)(2,1)S(1)} %dynamic-slice_convert_fusion.1), channel_id=1, source_target_pairs={{0,8},{8,0},{16,24},{24,16},{1,9},{9,1},{17,25},{25,17},{2,10},{10... | collective-permute-start | bytes 122888 | tf_op jit(solution)/shard_map/ppermute | solution.py:985

commit v5 on v4

--- a/solution.py
+++ b/solution.py
@@ -18,10 +18,10 @@
 ROWS = 128
 SLOTS = 18
 LANES = 128
-UNROLL = 4
-DEPTH = 6
+FORWARD_GROUPS = 8
+BACKWARD_GROUPS = 16
+DEPTH = 8
 BAND = 32
-STEPS = 3
 GROUP = 8
 GROUPS = ROWS // GROUP
 GT = SLOTS * GROUP
@@ -33,6 +33,7 @@
 FLAT = PSIZE // LANES
 BLOCK = 80
 EPS = 1e-05
+VMEM_BYTES = 60 * 1024 * 1024
 SCALE = 1.0 / math.sqrt(HEAD_DIM)
 F32 = jnp.float32
 BF16 = jnp.bfloat16
@@ -295,53 +296,44 @@
     return jnp.concatenate([x[:, 0], x[:, 1]], axis=0).reshape(CHUNK, n)
 
 
-def lanes_of(c):
-    return pl.ds(pl.multiple_of(c * CHUNK, CHUNK), CHUNK)
-
-
 def group_rows(c):
-    return pl.ds(pl.multiple_of(c * 2 * GROUP, 2 * GROUP), 2 * GROUP)
+    return slice(2 * GROUP * c, 2 * GROUP * (c + 1))
 
 
 def skewed(stages):
-    def steps(i, carry):
-        held = {}
-        for tick in range(STEPS + len(stages) - 1):
-            for j, stage in enumerate(stages):
-                u = tick - j
-                if 0 <= u < STEPS:
-                    held[u] = stage(i * STEPS + u, u, held.get(u))
-        return carry
-
-    lax.fori_loop(0, CHUNKS // STEPS, steps, 0)
-
-
-def view(ref, c, u, rows=None):
-    lanes = lanes_of(c) if ref.shape[1] == TOKENS else pl.ds(u * CHUNK, CHUNK)
-    return ref.at[slice(0, ref.shape[0] if rows is None else rows), lanes]
+    held = {}
+    for tick in range(CHUNKS + len(stages) - 1):
+        for j, stage in enumerate(stages):
+            c = tick - j
+            if 0 <= c < CHUNKS:
+                held[c] = stage(c, held.get(c))
+
+
+def view(ref, c, rows=None):
+    return ref.at[0 : ref.shape[0] if rows is None else rows, c * CHUNK : (c + 1) * CHUNK]
 
 
 def project_stages(s, w):
-    def project(c, u, _):
+    def project(c, _):
         lows = []
         for half in HALVES:
             xhat, rstd, low = norm(
-                view(s["x"], c, u).at[:, half][...], w["cols"][0], w["cols"][1]
+                view(s["x"], c).at[:, half][...], w["cols"][0], w["cols"][1]
             )
-            view(s["xhat1"], c, u).at[:, half][...] = xhat
-            view(s["rstd1"], c, u).at[:, half][...] = rstd
+            view(s["xhat1"], c).at[:, half][...] = xhat
+            view(s["rstd1"], c).at[:, half][...] = rstd
             lows.append(low)
-        view(s["h1"], c, u, D)[...] = jnp.concatenate(lows, axis=1)
-        return dot(view(s["h1"], c, u)[...], w["qkv"][...], 0, 0)
-
-    def keep(c, u, qkv):
+        view(s["h1"], c, D)[...] = jnp.concatenate(lows, axis=1)
+        return dot(view(s["h1"], c)[...], w["qkv"][...], 0, 0)
+
+    def keep(c, qkv):
         place = group_rows(c)
         s["q"][:, place, :] = to_groups(qkv[:, 0:D]).astype(BF16)
         for name, start in (("k", 256), ("v", 512)):
             part = qkv[:, start : start + D].reshape(2, GROUPS, GROUP, D)
             turned = jnp.concatenate(
                 [
-                    pltpu.roll(part[t], lax.rem(2 * c + t, GROUP), 1)[:, None]
+                    pltpu.roll(part[t], (2 * c + t) % GROUP, 1)[:, None]
                     for t in range(2)
                 ],
                 axis=1,
@@ -446,16 +438,28 @@
         second(*entry)
 
 
+def batches(size, run):
+    if size == GROUPS:
+        run(0)
+        return
+
+    def step(i, carry):
+        run(i * size)
+        return carry
+
+    lax.fori_loop(0, GROUPS // size, step, 0)
+
+
 def forward_attention(s, env):
     diff = env["diff"][...]
     bits = [(diff & (1 << i)) != 0 for i in range(3)]
     halves = [env["halves"][i] for i in range(2)]
 
-    def step(i, carry):
+    def run(base):
         state = {}
 
         def load(u):
-            g = i * UNROLL + u
+            g = base + u
             queries, values = s["q"][g], s["v"][g]
             state[u] = {
                 "g": g,
@@ -491,47 +495,46 @@
             s["mixed"][at["g"], 0:LANES, :] = main
             s["mixed"][at["g"], LANES:GT, :] = last
 
-        staged([(u, t) for u in range(UNROLL) for t in range(5)], scores, mix)
-        return carry
-
-    lax.fori_loop(0, GROUPS // UNROLL, step, 0)
+        staged([(u, t) for u in range(FORWARD_GROUPS) for t in range(5)], scores, mix)
+
+    batches(FORWARD_GROUPS, run)
 
 
 def rest_stages(s, w, done):
-    def attended(c, u, _):
+    def attended(c, _):
         mixed = from_groups(s["mixed"][:, group_rows(c), :].astype(F32)).astype(BF16)
         return dot(w["out_t"][...], mixed, 1, 1)
 
-    def normed(c, u, product):
+    def normed(c, product):
         lows = []
         for half in HALVES:
-            middle = view(s["x"], c, u).at[:, half][...] + (product[:, half] + w["cols"][2])
-            view(s["middle"], c, u).at[:, half][...] = middle
+            middle = view(s["x"], c).at[:, half][...] + (product[:, half] + w["cols"][2])
+            view(s["middle"], c).at[:, half][...] = middle
             xhat, rstd, low = norm(middle, w["cols"][3], w["cols"][4])
-            view(s["xhat2"], c, u).at[:, half][...] = xhat
-            view(s["rstd2"], c, u).at[:, half][...] = rstd
+            view(s["xhat2"], c).at[:, half][...] = xhat
+            view(s["rstd2"], c).at[:, half][...] = rstd
             lows.append(low)
-        view(s["h2"], c, u, D)[...] = jnp.concatenate(lows, axis=1)
-        return dot(w["gu_t"][...], view(s["h2"], c, u)[...], 1, 0)
-
-    def gated(c, u, gate_up):
+        view(s["h2"], c, D)[...] = jnp.concatenate(lows, axis=1)
+        return dot(w["gu_t"][...], view(s["h2"], c)[...], 1, 0)
+
+    def gated(c, gate_up):
         acts = []
         for r in range(0, FF, BAND):
             band = pl.ds(r, BAND)
             gate, up = gate_up[r : r + BAND], gate_up[FF + r : FF + r + BAND]
             cdf, slope = gelu_parts(gate)
             gelu = gate * cdf
-            view(s["gelu"], c, u).at[band][...] = gelu
-            view(s["slope"], c, u).at[band][...] = slope * up
+            view(s["gelu"], c).at[band][...] = gelu
+            view(s["slope"], c).at[band][...] = slope * up
             acts.append((gelu * up).astype(BF16))
         act = jnp.concatenate(acts, axis=0)
-        view(s["act"], c, u, FF)[...] = act
+        view(s["act"], c, FF)[...] = act
         return dot(w["down_t"][...], act, 1, 0)
 
-    def finish(c, u, product):
+    def finish(c, product):
         for i, half in enumerate(HALVES):
-            value = view(s["middle"], c, u).at[:, half][...]
-            done(c, u, i, value + (product[:, half] + w["cols"][5]))
+            value = view(s["middle"], c).at[:, half][...]
+            done(c, i, value + (product[:, half] + w["cols"][5]))
 
     return attended, normed, gated, finish
 
@@ -547,34 +550,34 @@
 
 
 def rest_back_stages(s, w, acc, sums):
-    def down(c, u, _):
-        branch = view(s["g"], c, u)[...].astype(BF16)
-        return dot(view(s["act"], c, u)[...], branch, 1, 1), dot(w["down"][...], branch, 1, 0)
-
-    def gate_up(c, u, held):
+    def down(c, _):
+        branch = view(s["g"], c)[...].astype(BF16)
+        return dot(view(s["act"], c)[...], branch, 1, 1), dot(w["down"][...], branch, 1, 0)
+
+    def gate_up(c, held):
         grad_down, d_act = held
         add_narrow(acc["down"], grad_down)
         gates, ups = [], []
         for r in range(0, FF, BAND):
             band = pl.ds(r, BAND)
             part = d_act[r : r + BAND]
-            gates.append((part * view(s["slope"], c, u).at[band][...]).astype(BF16))
-            ups.append((part * view(s["gelu"], c, u).at[band][...]).astype(BF16))
+            gates.append((part * view(s["slope"], c).at[band][...]).astype(BF16))
+            ups.append((part * view(s["gelu"], c).at[band][...]).astype(BF16))
         d_gate_up = jnp.concatenate(gates + ups, axis=0)
-        return dot(view(s["h2"], c, u)[...], d_gate_up, 1, 1), dot(w["gu"][...], d_gate_up, 1, 0)
-
-    def normed(c, u, held):
+        return dot(view(s["h2"], c)[...], d_gate_up, 1, 1), dot(w["gu"][...], d_gate_up, 1, 0)
+
+    def normed(c, held):
         grad_gu, d_normed = held
         add_tiles(acc["gu"], grad_gu)
         lows = []
         for half in HALVES:
-            xhat = view(s["xhat2"], c, u).at[:, half][...]
+            xhat = view(s["xhat2"], c).at[:, half][...]
             part = d_normed[:, half]
             sums[2] += part * xhat
             sums[3] += part
-            g = view(s["g"], c, u).at[:, half]
+            g = view(s["g"], c).at[:, half]
             d_middle = g[...] + norm_back(
-                part, xhat, view(s["rstd2"], c, u).at[:, half][...], w["cols"][3]
+                part, xhat, view(s["rstd2"], c).at[:, half][...], w["cols"][3]
             )
             g[...] = d_middle
             low = d_middle.astype(BF16)
@@ -584,9 +587,9 @@
         mixed = from_groups(s["mixed"][:, group_rows(c), :].astype(F32)).astype(BF16)
         return dot(d_attended, w["out_t"][...], 0, 0), dot(d_attended, mixed, 1, 0)
 
-    def finish(c, u, held):
+    def finish(c, held):
         d_mixed, grad_out = held
-        s["dm"][:, group_rows(c), :] = to_groups(d_mixed).astype(BF16)
+        s["dqkv"][:, group_rows(c), 0:D] = to_groups(d_mixed).astype(BF16)
         acc["out_t"][...] += grad_out
 
     return down, gate_up, normed, finish
@@ -597,12 +600,12 @@
     bits = [(diff & (1 << i)) != 0 for i in range(3)]
     halves = [env["halves"][i] for i in range(2)]
 
-    def step(i, carry):
+    def run(base):
         state = {}
 
         def load(u):
-            g = i * UNROLL + u
-            queries, keys, grads = s["q"][g], s["k"][g], s["dm"][g]
+            g = base + u
+            queries, keys, grads = s["q"][g], s["k"][g], s["dqkv"][g, :, 0:D]
             state[u] = {
                 "g": g,
                 "queries": queries,
@@ -663,33 +666,31 @@
                 ]
                 s["dqkv"][g, :, start : start + D] = jnp.concatenate(turned, axis=0).astype(BF16)
 
-        staged([(u, t) for u in range(UNROLL) for t in range(5)], products, back)
-        return carry
-
-    lax.fori_loop(0, GROUPS // UNROLL, step, 0)
+        staged([(u, t) for u in range(BACKWARD_GROUPS) for t in range(5)], products, back)
+
+    batches(BACKWARD_GROUPS, run)
 
 
 def project_back_stages(s, w, acc, sums, done):
-    def products(c, u, _):
+    def products(c, _):
         d_qkv = from_groups(s["dqkv"][:, group_rows(c), :].astype(F32)).astype(BF16)
-        return dot(view(s["h1"], c, u)[...], d_qkv, 1, 0), dot(w["qkv"][0:D, :], d_qkv, 1, 1)
-
-    def finish(c, u, held):
+        return dot(view(s["h1"], c)[...], d_qkv, 1, 0), dot(w["qkv"][0:D, :], d_qkv, 1, 1)
+
+    def finish(c, held):
         grad_qkv, d_normed = held
         add_tiles(acc["qkv"], grad_qkv)
         for i, half in enumerate(HALVES):
-            xhat = view(s["xhat1"], c, u).at[:, half][...]
+            xhat = view(s["xhat1"], c).at[:, half][...]
             part = d_normed[:, half]
             sums[0] += part * xhat
             sums[1] += part
-            back = norm_back(part, xhat, view(s["rstd1"], c, u).at[:, half][...], w["cols"][0])
-            done(c, u, i, view(s["g"], c, u).at[:, half][...] + back)
+            back = norm_back(part, xhat, view(s["rstd1"], c).at[:, half][...], w["cols"][0])
+            done(c, i, view(s["g"], c).at[:, half][...] + back)
 
     return products, finish
 
 
-def per_layer(layer):
-    room = TOKENS if layer < LAYERS - 1 else STEPS * CHUNK
+def per_layer():
     return {
         "xhat1": ((D, TOKENS), F32),
         "rstd1": ((1, TOKENS), F32),
@@ -699,12 +700,12 @@
         "v": ((GROUPS, GT, D), BF16),
         "att": ((GROUPS, 24, QL), F32),
         "mixed": ((GROUPS, GT, D), BF16),
-        "xhat2": ((D, room), F32),
-        "rstd2": ((1, room), F32),
-        "h2": ((D + 16, room), BF16),
-        "act": ((FF + 16, room), BF16),
-        "gelu": ((FF, room), F32),
-        "slope": ((FF, room), F32),
+        "xhat2": ((D, TOKENS), F32),
+        "rstd2": ((1, TOKENS), F32),
+        "h2": ((D + 16, TOKENS), BF16),
+        "act": ((FF + 16, TOKENS), BF16),
+        "gelu": ((FF, TOKENS), F32),
+        "slope": ((FF, TOKENS), F32),
     }
 
 
@@ -732,28 +733,21 @@
 
 def common():
     full = (SEQ, D, ROWS)
-    blocks = (4, 4, LAYERS, BLOCK, LANES)
     return {
         "halves": ((2, 16, LANES), BF16),
         "heads": ((HEADS, 16, D), BF16),
         "masks": ((5, 16, CHUNK), BF16),
         "diff": ((GROUP, CHUNK), jnp.int32),
         "count": ((GROUPS, CHUNK), F32),
-        "dm": ((GROUPS, GT, D), BF16),
         "dqkv": ((GROUPS, GT, 6 * LANES), BF16),
         "x": ((D, TOKENS), F32),
-        "middle": ((D, STEPS * CHUNK), F32),
+        "middle": ((D, TOKENS), F32),
         "g": ((D, TOKENS), F32),
         "flat": ((FLAT + 8, LANES), F32),
         "tmp": ((2, FF, LANES), F32),
         "tokens": (full, BF16),
         "out_grad": (full, BF16),
-        "own": (blocks, BF16),
-        "other": (blocks, BF16),
         "out": ((SLOTS, D, ROWS), F32),
-        "in_grad": ((SLOTS, D, ROWS), F32),
-        "keep": (blocks, BF16),
-        "give": (blocks, BF16),
     }
 
 
@@ -763,15 +757,15 @@
         ("common", common()),
         ("acc0", accumulators()),
         ("acc1", accumulators()),
-        ("s0", per_layer(0)),
-        ("s1", per_layer(1)),
+        ("s0", per_layer()),
+        ("s1", per_layer()),
         ("w0", weights()),
         ("w1", weights()),
     ):
         for name, (shape, kind) in table.items():
             names.append((prefix, name))
             shapes.append(pltpu.VMEM(shape, kind))
-    return names, shapes + [pltpu.SemaphoreType.DMA((10,))]
+    return names, shapes + [pltpu.SemaphoreType.DMA((6,))]
 
 
 def init_env(env, count):
@@ -834,7 +828,7 @@
     copies = [
         pltpu.make_async_copy(source, env[name], sems.at[i])
         for i, (source, name) in enumerate(
-            ((own, "own"), (other, "other"), (tokens, "tokens"), (out_grad, "out_grad"))
+            ((tokens, "tokens"), (out_grad, "out_grad"))
         )
     ]
     for copy in copies:
@@ -854,13 +848,11 @@
     env["x"][:, SEQ * ROWS :] = jnp.zeros((D, ROWS), F32)
     env["g"][:, SEQ * ROWS :] = jnp.zeros((D, ROWS), F32)
     row_scale = scales(table_ids[...], table_counts[...])
+    for layer in range(LAYERS):
+        gather_flat(own, other, place, layer, env["flat"])
+        unpack(env["flat"], w[layer], env["tmp"])
     copies[0].wait()
     copies[1].wait()
-    for layer in range(LAYERS):
-        gather_flat(env["own"], env["other"], place, layer, env["flat"])
-        unpack(env["flat"], w[layer], env["tmp"])
-    copies[2].wait()
-    copies[3].wait()
     for slot in range(SEQ):
         lanes = slice(slot * ROWS, (slot + 1) * ROWS)
         env["x"][:, lanes] = env["tokens"][slot].astype(F32)
@@ -868,18 +860,18 @@
         env["g"][:, lanes] = env["out_grad"][slot].astype(F32) * keep
 
     def put(target):
-        def done(c, u, i, value):
+        def done(c, i, value):
             target[2 * c + i] = value
 
         return done
 
     def set_to(target):
-        def done(c, u, i, value):
-            view(target, c, u).at[:, HALVES[i]][...] = value
+        def done(c, i, value):
+            view(target, c).at[:, HALVES[i]][...] = value
 
         return done
 
-    shared = {name: env[name] for name in ("x", "middle", "g", "dm", "dqkv")}
+    shared = {name: env[name] for name in ("x", "middle", "g", "dqkv")}
     s = [dict(part, **shared) for part in s]
 
     skewed(project_stages(s[0], w[0]))
@@ -887,21 +879,21 @@
     attended, normed, gated, finish = rest_stages(s[0], w[0], set_to(env["x"]))
     project, hold = project_stages(s[1], w[1])
 
-    def finish_project(c, u, held):
-        finish(c, u, held)
-        return project(c, u, None)
+    def finish_project(c, held):
+        finish(c, held)
+        return project(c, None)
 
     skewed((attended, normed, gated, finish_project, hold))
     forward_attention(s[1], env)
     attended, normed, gated, finish_out = rest_stages(s[1], w[1], put(env["out"]))
     down, gate_up, normed_back, finish_back = rest_back_stages(s[1], w[1], acc[1], sums[1])
 
-    def gated_down(c, u, held):
-        return gated(c, u, held), down(c, u, None)
-
-    def finish_gate_up(c, u, held):
-        finish_out(c, u, held[0])
-        return gate_up(c, u, held[1])
+    def gated_down(c, held):
+        return gated(c, held), down(c, None)
+
+    def finish_gate_up(c, held):
+        finish_out(c, held[0])
+        return gate_up(c, held[1])
 
     skewed((attended, normed, gated_down, finish_gate_up, normed_back, finish_back))
     out_copy = pltpu.make_async_copy(env["out"].at[0:SEQ], out, sems.at[4])
@@ -912,39 +904,31 @@
     )
     down, gate_up, normed_back, finish_back = rest_back_stages(s[0], w[0], acc[0], sums[0])
 
-    def finish_down(c, u, held):
-        finish_project_back(c, u, held)
-        return down(c, u, None)
+    def finish_down(c, held):
+        finish_project_back(c, held)
+        return down(c, None)
 
     skewed((products, finish_down, gate_up, normed_back, finish_back))
 
     def send(layer):
         pack(env["flat"], acc[layer], sums[layer], env["tmp"])
-        scatter_blocks(env["flat"], place, layer, env["keep"], env["give"])
-        started = []
-        for i, (name, target) in enumerate((("keep", keep_out), ("give", give_out))):
-            started.append(
-                pltpu.make_async_copy(
-                    env[name].at[:, :, layer], target.at[:, :, layer], sems.at[5 + 2 * layer + i]
-                )
-            )
-            started[-1].start()
-        return started
-
-    started = [out_copy] + send(1)
+        scatter_blocks(env["flat"], place, layer, keep_out, give_out)
+
+    send(1)
     backward_attention(s[0], env)
-    skewed(project_back_stages(s[0], w[0], acc[0], sums[0], put(env["in_grad"])))
-    last = pltpu.make_async_copy(env["in_grad"].at[0:SEQ], in_grad, sems.at[9])
+    out_copy.wait()
+    skewed(project_back_stages(s[0], w[0], acc[0], sums[0], put(env["out"])))
+    last = pltpu.make_async_copy(env["out"].at[0:SEQ], in_grad, sems.at[5])
     last.start()
-    started += send(0) + [last]
-    for copy in started:
-        copy.wait()
+    send(0)
+    last.wait()
 
 
 def run_kernel(four, tokens, out_grad, own, other, count, ids, table_counts):
     names, scratch = make_scratch()
     full = jax.ShapeDtypeStruct((SEQ, D, ROWS), F32)
-    blocks = jax.ShapeDtypeStruct(own.shape, BF16)
+    blocks = pltpu.VMEM(own.shape, BF16)
+    own, other = (pltpu.with_memory_space_constraint(part, pltpu.VMEM) for part in (own, other))
 
     def body(*refs):
         kernel(names, four, *refs)
@@ -954,10 +938,10 @@
     return pl.pallas_call(
         body,
         out_shape=(full, full, blocks, blocks),
-        in_specs=[anywhere] * 4 + [vmem] * 3,
-        out_specs=[anywhere] * 4,
+        in_specs=[anywhere] * 2 + [vmem] * 5,
+        out_specs=[anywhere] * 2 + [vmem] * 2,
         scratch_shapes=scratch,
-        compiler_params=pltpu.CompilerParams(vmem_limit_bytes=64 * 1024 * 1024 - 256 * 1024),
+        compiler_params=pltpu.CompilerParams(vmem_limit_bytes=VMEM_BYTES),
     )(tokens, out_grad, own, other, count, ids, table_counts)
 
 

time: 111 us -> 96.1 us (0.87)
  Pallas kernels: 53 us -> 41.2 us
  local copies, waits for them, and re-layouts: 1.8 us -> 0.09 us
    pallas_call x1, Pallas kernels: 53 us -> 41.2 us  [run_kernel(): pl.pallas_call(body, out_shape=(full, full, blocks, blocks), in_specs=[an...]
    unnamed x6 -> x2, local copies, waits for them, and re-layouts: 1.76 us -> 0.05 us
where the time goes in v5:
time: 96.1 us; the launch traced here: 95.8 us
  Pallas kernels  41.2 us (43%)
  waiting for transfers between devices  27 us (28%)
  starting transfers between devices  12.2 us (13%)
  blocking collectives  11.6 us (12%)
  other arithmetic  2.9 us (3%)
    pallas_call x1, Pallas kernels, run_kernel(): pl.pallas_call(body, out_shape=(full, full, blocks, blocks), in_specs=[an...  41.2 us
    ppermute x6, waiting for transfers between devices, swap_along(): return lax.ppermute(x, axis, pairs)  17.1 us
    all_gather x1, blocking collectives, gather_pairs(): own = lax.all_gather(part, ('x', 'y'), axis=0, tiled=False)  11.6 us
    all_to_all x1, waiting for transfers between devices, reduce_pairs(): part = lax.all_to_all(part, ('x', 'y'), 0, 0, tiled=True)  9.94 us
    ppermute x6, starting transfers between devices, swap_along(): return lax.ppermute(x, axis, pairs)  8.69 us
    all_to_all x1, starting transfers between devices, reduce_pairs(): part = lax.all_to_all(part, ('x', 'y'), 0, 0, tiled=True)  3.48 us
  transfers between devices with their start and end apart: 7, of which 7 were waited for; matrix products, arithmetic and copies ran while one was open for 0% of the time, Pallas kernels for 0%

profile of v5, /device:TPU:0, one launch (start us, length us, event | category | flops | bytes accessed | tf_op | source)
XLA Modules:
  0.0 95.8 jit_solution(14378241785281403519)
XLA Ops:
  0.6 1.0 %fusion = bf16[1,2,80,128]{3,1,2,0:T(2,128)(2,1)S(1)} fusion(pred[]{:T(512)S(6)} %eq.7, bf16[2,9280]{1,0:T(2,128)(2,1)} %param.8), kind=kLoop, calls=%fused_computation.11 | loop fusion | flops 20480 | bytes 78081
  1.6 4.1 %collective-permute-start = (bf16[1,2,80,128]{3,2,1,0:T(8,128)(2,1)S(1)}, bf16[1,2,80,128]{3,2,1,0:T(8,128)(2,1)S(1)}, u32[]{:S(2)}, u32[]{:S(2)}) collective-permute-start(bf16[1,2,80,128]{3,2,1,0:T(8,128)(2,1)S(1)} %copy.14), channel_id=1, source_target_pairs={{0,16},{8,24},{16,0},{24,8},{1,17},{9,25},{17,1},{25,9},{2,18},{10... | collective-permute-start | bytes 122888 | tf_op jit(solution)/shard_map/ppermute | solution.py:969
  5.7 2.4 %collective-permute-done = bf16[1,2,80,128]{3,2,1,0:T(8,128)(2,1)S(1)} collective-permute-done((bf16[1,2,80,128]{3,2,1,0:T(8,128)(2,1)S(1)}, bf16[1,2,80,128]{3,2,1,0:T(8,128)(2,1)S(1)}, u32[]{:S(2)}, u32[]{:S(2)}) %collective-permute-start) | collective-permute-done | bytes 40992 | tf_op jit(solution)/shard_map/ppermute | solution.py:969
  8.2 1.5 %collective-permute-start.1 = (bf16[2,2,80,128]{3,2,1,0:T(8,128)(2,1)S(1)}, bf16[2,2,80,128]{3,2,1,0:T(8,128)(2,1)S(1)}, u32[]{:S(2)}, u32[]{:S(2)}) collective-permute-start(bf16[2,2,80,128]{3,2,1,0:T(8,128)(2,1)S(1)} %pad_maximum_fusion.1), channel_id=1, source_target_pairs={{0,8},{8,0},{16,24},{24,16},{1,9},{9,1},{17,25},{25,17},{2,10},{10... | collective-permute-start | bytes 245768 | tf_op jit(solution)/shard_map/ppermute | solution.py:969
  9.7 3.0 %collective-permute-done.1 = bf16[2,2,80,128]{3,2,1,0:T(8,128)(2,1)S(1)} collective-permute-done((bf16[2,2,80,128]{3,2,1,0:T(8,128)(2,1)S(1)}, bf16[2,2,80,128]{3,2,1,0:T(8,128)(2,1)S(1)}, u32[]{:S(2)}, u32[]{:S(2)}) %collective-permute-start.1) | collective-permute-done | bytes 81952 | tf_op jit(solution)/shard_map/ppermute | solution.py:969
  12.7 11.6 %all-gather = bf16[16,2,80,128]{3,2,1,0:T(8,128)(2,1)S(1)} all-gather(bf16[4,2,80,128]{3,2,1,0:T(8,128)(2,1)S(1)} %pad_maximum_fusion), channel_id=2, replica_groups=mesh['z'=4,'x'=2,'y'=2,'core'=2] {'x','y'}, dimensions={0}, use_global_device_ids=true | all-gather | bytes 819200 | tf_op jit(solution)/shard_map/all_gather | solution.py:982
  24.3 0.0 collective-permute-start.2
  24.3 2.1 %collective-permute-done.2.refs_3_ = bf16[4,4,2,80,128]{4,3,2,1,0:T(8,128)(2,1)S(1)} collective-permute-done((bf16[4,4,2,80,128]{4,3,2,1,0:T(8,128)(2,1)S(1)}, bf16[4,4,2,80,128]{4,3,2,1,0:T(8,128)(2,1)S(1)}, u32[]{:S(2)}, u32[]{:S(2)}) %collective-permute-start.2) | collective-permute-done | bytes 655392 | tf_op jit(solution)/shard_map/ppermute | solution.py:969
  26.4 41.2 %shard_map.85 = (f32[17,192,128]{2,1,0:T(8,128)}, f32[17,192,128]{2,1,0:T(8,128)}, bf16[4,4,2,80,128]{4,3,2,1,0:T(8,128)(2,1)S(1)}, bf16[4,4,2,80,128]{4,3,2,1,0:T(8,128)(2,1)S(1)}) custom-call(bf16[17,192,128]{2,1,0:T(8,128)(2,1)} %bitcast.22, bf16[17,192,128]{2,1,0:T(8,128)(2,1)} %bitcast.23, bf16[4,4,2,80,128]{4,3,2,1,0:T(8,128)(2,1)S(1)} %bitcast.21, ...), custom_call_target="tpu_custom_call" | custom-call | tf_op jit(solution)/shard_map/pallas_call | solution.py:938
  67.6 0.2 collective-permute-start.3
  67.8 2.0 %collective-permute-done.3 = bf16[4,4,2,80,128]{4,3,2,1,0:T(8,128)(2,1)S(1)} collective-permute-done((bf16[4,4,2,80,128]{4,3,2,1,0:T(8,128)(2,1)S(1)}, bf16[4,4,2,80,128]{4,3,2,1,0:T(8,128)(2,1)S(1)}, u32[]{:S(2)}, u32[]{:S(2)}) %collective-permute-start.3) | collective-permute-done | bytes 655392 | tf_op jit(solution)/shard_map/ppermute | solution.py:969
  69.8 1.0 %add_convert_fusion = bf16[4,4,2,80,128]{4,3,2,1,0:T(8,128)(2,1)} fusion(bf16[4,4,2,80,128]{4,3,2,1,0:T(8,128)(2,1)S(1)} %collective-permute-done.3, bf16[4,4,2,80,128]{4,3,2,1,0:T(8,128)(2,1)S(1)} %get-tuple-element.9), kind=kLoop, calls=%fused_computation.1 | loop fusion | flops 1310720 | bytes 1966080 | tf_op jit(solution)/shard_map/convert_element_type | solution.py:988
  70.8 3.5 %all-to-all-start = ((bf16[4,4,2,80,128]{4,3,2,1,0:T(8,128)(2,1)}), bf16[4,4,2,80,128]{4,3,2,1,0:T(8,128)(2,1)S(1)}, u32[]{:S(2)}, u32[]{:S(2)}) async-start(bf16[4,4,2,80,128]{4,3,2,1,0:T(8,128)(2,1)} %add_convert_fusion), calls=%async_computation | async-start | bytes 1310720 | tf_op jit(solution)/shard_map/all_to_all | solution.py:989
  74.3 9.9 %all-to-all-done = bf16[4,4,2,80,128]{4,3,2,1,0:T(8,128)(2,1)S(1)} async-done(((bf16[4,4,2,80,128]{4,3,2,1,0:T(8,128)(2,1)}), bf16[4,4,2,80,128]{4,3,2,1,0:T(8,128)(2,1)S(1)}, u32[]{:S(2)}, u32[]{:S(2)}) %all-to-all-start) | async-done | bytes 655392 | tf_op jit(solution)/shard_map/all_to_all | solution.py:989
  84.3 0.1 convert_reduce_fusion
  84.4 2.4 %collective-permute-start.4 = (bf16[2,2,80,128]{3,2,1,0:T(8,128)(2,1)S(1)}, bf16[2,2,80,128]{3,2,1,0:T(8,128)(2,1)S(1)}, u32[]{:S(2)}, u32[]{:S(2)}) collective-permute-start(bf16[2,2,80,128]{3,2,1,0:T(8,128)(2,1)S(1)} %dynamic-slice_convert_fusion), channel_id=1, source_target_pairs={{0,16},{8,24},{16,0},{24,8},{1,17},{9,25},{17,1},{25,9},{2,18},{10... | collective-permute-start | bytes 245768 | tf_op jit(solution)/shard_map/ppermute | solution.py:969
  86.8 4.0 %collective-permute-done.4 = bf16[2,2,80,128]{3,2,1,0:T(8,128)(2,1)S(1)} collective-permute-done((bf16[2,2,80,128]{3,2,1,0:T(8,128)(2,1)S(1)}, bf16[2,2,80,128]{3,2,1,0:T(8,128)(2,1)S(1)}, u32[]{:S(2)}, u32[]{:S(2)}) %collective-permute-start.4) | collective-permute-done | bytes 81952 | tf_op jit(solution)/shard_map/ppermute | solution.py:969
  90.9 0.4 collective-permute-start.5
  91.3 3.6 %collective-permute-done.5 = bf16[1,2,80,128]{3,2,1,0:T(8,128)(2,1)S(1)} collective-permute-done((bf16[1,2,80,128]{3,2,1,0:T(8,128)(2,1)S(1)}, bf16[1,2,80,128]{3,2,1,0:T(8,128)(2,1)S(1)}, u32[]{:S(2)}, u32[]{:S(2)}) %collective-permute-start.5) | collective-permute-done | bytes 40992 | tf_op jit(solution)/shard_map/ppermute | solution.py:969
  95.0 0.8 slice_select_fusion
  (8 shorter events, 0.1 us)
Async XLA Ops:
  1.6 6.5 %collective-permute-start = (bf16[1,2,80,128]{3,2,1,0:T(8,128)(2,1)S(1)}, bf16[1,2,80,128]{3,2,1,0:T(8,128)(2,1)S(1)}, u32[]{:S(2)}, u32[]{:S(2)}) collective-permute-start(bf16[1,2,80,128]{3,2,1,0:T(8,128)(2,1)S(1)} %copy.14), channel_id=1, source_target_pairs={{0,16},{8,24},{16,0},{24,8},{1,17},{9,25},{17,1},{25,9},{2,18},{10... | collective-permute-start | bytes 122888 | tf_op jit(solution)/shard_map/ppermute | solution.py:969
  8.2 4.5 %collective-permute-start.1 = (bf16[2,2,80,128]{3,2,1,0:T(8,128)(2,1)S(1)}, bf16[2,2,80,128]{3,2,1,0:T(8,128)(2,1)S(1)}, u32[]{:S(2)}, u32[]{:S(2)}) collective-permute-start(bf16[2,2,80,128]{3,2,1,0:T(8,128)(2,1)S(1)} %pad_maximum_fusion.1), channel_id=1, source_target_pairs={{0,8},{8,0},{16,24},{24,16},{1,9},{9,1},{17,25},{25,17},{2,10},{10... | collective-permute-start | bytes 245768 | tf_op jit(solution)/shard_map/ppermute | solution.py:969
  24.3 2.1 %collective-permute-start.2 = (bf16[4,4,2,80,128]{4,3,2,1,0:T(8,128)(2,1)S(1)}, bf16[4,4,2,80,128]{4,3,2,1,0:T(8,128)(2,1)S(1)}, u32[]{:S(2)}, u32[]{:S(2)}) collective-permute-start(bf16[4,4,2,80,128]{4,3,2,1,0:T(8,128)(2,1)S(1)} %bitcast.20), channel_id=1, source_target_pairs={{0,1},{1,0},{2,3},{3,2},{4,5},{5,4},{6,7},{7,6},{8,9},{9,8},{10,11... | collective-permute-start | bytes 1966088 | tf_op jit(solution)/shard_map/ppermute | solution.py:969
  67.6 2.2 %collective-permute-start.3 = (bf16[4,4,2,80,128]{4,3,2,1,0:T(8,128)(2,1)S(1)}, bf16[4,4,2,80,128]{4,3,2,1,0:T(8,128)(2,1)S(1)}, u32[]{:S(2)}, u32[]{:S(2)}) collective-permute-start(bf16[4,4,2,80,128]{4,3,2,1,0:T(8,128)(2,1)S(1)} %get-tuple-element.10), channel_id=1, source_target_pairs={{0,1},{1,0},{2,3},{3,2},{4,5},{5,4},{6,7},{7,6},{8,9},{9,8},{10,11... | collective-permute-start | bytes 1966088 | tf_op jit(solution)/shard_map/ppermute | solution.py:969
  70.8 13.5 %all-to-all-start = ((bf16[4,4,2,80,128]{4,3,2,1,0:T(8,128)(2,1)}), bf16[4,4,2,80,128]{4,3,2,1,0:T(8,128)(2,1)S(1)}, u32[]{:S(2)}, u32[]{:S(2)}) async-start(bf16[4,4,2,80,128]{4,3,2,1,0:T(8,128)(2,1)} %add_convert_fusion), calls=%async_computation | async-start | bytes 1310720 | tf_op jit(solution)/shard_map/all_to_all | solution.py:989
  84.4 6.4 %collective-permute-start.4 = (bf16[2,2,80,128]{3,2,1,0:T(8,128)(2,1)S(1)}, bf16[2,2,80,128]{3,2,1,0:T(8,128)(2,1)S(1)}, u32[]{:S(2)}, u32[]{:S(2)}) collective-permute-start(bf16[2,2,80,128]{3,2,1,0:T(8,128)(2,1)S(1)} %dynamic-slice_convert_fusion), channel_id=1, source_target_pairs={{0,16},{8,24},{16,0},{24,8},{1,17},{9,25},{17,1},{25,9},{2,18},{10... | collective-permute-start | bytes 245768 | tf_op jit(solution)/shard_map/ppermute | solution.py:969
  90.9 4.1 %collective-permute-start.5 = (bf16[1,2,80,128]{3,2,1,0:T(8,128)(2,1)S(1)}, bf16[1,2,80,128]{3,2,1,0:T(8,128)(2,1)S(1)}, u32[]{:S(2)}, u32[]{:S(2)}) collective-permute-start(bf16[1,2,80,128]{3,2,1,0:T(8,128)(2,1)S(1)} %dynamic-slice_convert_fusion.1), channel_id=1, source_target_pairs={{0,8},{8,0},{16,24},{24,16},{1,9},{9,1},{17,25},{25,17},{2,10},{10... | collective-permute-start | bytes 122888 | tf_op jit(solution)/shard_map/ppermute | solution.py:969

commit v6 on v5

--- a/solution.py
+++ b/solution.py
@@ -252,8 +252,10 @@
     for chip in range(FLAT // 145):
         first = flat[pl.ds(145 * chip, BLOCK), :]
         second = flat[pl.ds(145 * chip + 72, BLOCK), :]
-        keep[chip % 4, chip // 4, layer] = jnp.where(core == 0, first, second).astype(BF16)
-        give[chip % 4, chip // 4, layer] = jnp.where(core == 0, second, first).astype(BF16)
+        z = chip // 4
+        at = (z & 1) * 2 + z // 2
+        keep[chip % 4, at, layer] = jnp.where(core == 0, first, second).astype(BF16)
+        give[chip % 4, at, layer] = jnp.where(core == 0, second, first).astype(BF16)
 
 
 def norm(x, gain, bias):
@@ -417,13 +419,15 @@
     own = diff[:, 0:n]
     limit = limit[:, 0:n]
     slot = own.astype(F32)
+    scale = SCALE / math.log(2.0)
+    low = -1e9 / math.log(2.0)
     shown = [
-        jnp.where(slot <= limit, kept[0] * SCALE, -1e9),
-        jnp.where(slot + 8.0 <= limit, kept[1] * SCALE, -1e9),
-        jnp.where(own == 0, jnp.where(limit >= 16.0, kept[2] * SCALE, -1e9), -3e38),
+        jnp.where(slot <= limit, kept[0] * scale, low),
+        jnp.where(slot + 8.0 <= limit, kept[1] * scale, low),
+        jnp.where(own == 0, jnp.where(limit >= 16.0, kept[2] * scale, low), -3e38),
     ]
     top = jnp.max(jnp.maximum(jnp.maximum(shown[0], shown[1]), shown[2]), axis=0, keepdims=True)
-    shown = [jnp.exp(part - top) for part in shown]
+    shown = [jnp.exp2(part - top) for part in shown]
     inverse = 1.0 / jnp.sum(shown[0] + shown[1] + shown[2], axis=0, keepdims=True)
     return jnp.concatenate([part * inverse for part in shown], axis=0)
 
@@ -958,7 +962,8 @@
 def pairs_joined(even, odd):
     joined = []
     for chip in range(16):
-        first, second = even[chip % 4, chip // 4], odd[chip % 4, chip // 4]
+        at = (chip // 4 % 2) * 2 + chip // 8
+        first, second = even[chip % 4, at], odd[chip % 4, at]
         seam = jnp.concatenate([first[:, 72:73, 0:64], second[:, 0:1, 64:]], axis=2)
         joined += [first[:, 0:72], seam, second[:, 1:73]]
     return jnp.concatenate(joined, axis=1).reshape(LAYERS, PSIZE)
@@ -986,13 +991,18 @@
 def reduce_pairs(keep, give, size):
     got = swap_along(give, "core", 1)
     part = (keep.astype(F32) + got.astype(F32)).astype(BF16)
-    part = lax.all_to_all(part, ("x", "y"), 0, 0, tiled=True)
-    part = jnp.sum(part.astype(F32), axis=0)
+    me = 2 * lax.axis_index("x") + lax.axis_index("y")
+    total = lax.dynamic_index_in_dim(part, me, 0, False).astype(F32)
+    for away in (3, 2, 1):
+        pairs = [(i, i ^ away) for i in range(4)]
+        theirs = lax.dynamic_index_in_dim(part, me ^ away, 0, False)
+        total += lax.ppermute(theirs, ("x", "y"), pairs).astype(F32)
+    part = total
     z = lax.axis_index("z")
-    for bit in (2, 1):
+    for bit, count in ((1, 2), (2, 1)):
         high = (z // bit) % 2
-        stay = lax.dynamic_slice_in_dim(part, high * bit, bit, 0)
-        go = lax.dynamic_slice_in_dim(part, (1 - high) * bit, bit, 0).astype(BF16)
+        stay = lax.dynamic_slice_in_dim(part, high * count, count, 0)
+        go = lax.dynamic_slice_in_dim(part, (1 - high) * count, count, 0).astype(BF16)
         part = stay + swap_along(go, "z", bit).astype(F32)
     total = part.reshape(LAYERS, BLOCK * LANES)
     return jnp.where(

time: 96.1 us -> 91.5 us (0.952)
  waiting for transfers between devices: 27 us -> 22.4 us
    all_to_all x1 -> x0, waiting for transfers between devices: 9.94 us -> none  [reduce_pairs(): part = lax.all_to_all(part, ('x', 'y'), 0, 0, tiled=True)]
    ppermute x0 -> x3, waiting for transfers between devices: none -> 7.16 us  [reduce_pairs(): total += lax.ppermute(theirs, ('x', 'y'), pairs).astype(F32)]
    ppermute x0 -> x3, starting transfers between devices: none -> 3.55 us  [reduce_pairs(): total += lax.ppermute(theirs, ('x', 'y'), pairs).astype(F32)]
    all_to_all x1 -> x0, starting transfers between devices: 3.48 us -> none  [reduce_pairs(): part = lax.all_to_all(part, ('x', 'y'), 0, 0, tiled=True)]
    ppermute x6, waiting for transfers between devices: 17.1 us -> 15.3 us  [swap_along(): return lax.ppermute(x, axis, pairs)]
  transfers between devices with their start and end apart: 7 -> 9, of which waited for: 7 -> 9; matrix products, arithmetic and copies ran while one was open for 0% -> 0% of each run, Pallas kernels for 0% -> 0%
where the time goes in v6:
time: 91.5 us; the launch traced here: 91.3 us
  Pallas kernels  41.3 us (45%)
  waiting for transfers between devices  22.4 us (24%)
  starting transfers between devices  13.1 us (14%)
  blocking collectives  11.6 us (13%)
  other arithmetic  2.05 us (2%)
    pallas_call x1, Pallas kernels, run_kernel(): pl.pallas_call(body, out_shape=(full, full, blocks, blocks), in_specs=[an...  41.3 us
    ppermute x6, waiting for transfers between devices, swap_along(): return lax.ppermute(x, axis, pairs)  15.3 us
    all_gather x1, blocking collectives, gather_pairs(): own = lax.all_gather(part, ('x', 'y'), axis=0, tiled=False)  11.6 us
    ppermute x6, starting transfers between devices, swap_along(): return lax.ppermute(x, axis, pairs)  9.5 us
    ppermute x3, waiting for transfers between devices, reduce_pairs(): total += lax.ppermute(theirs, ('x', 'y'), pairs).astype(F32)  7.16 us
    ppermute x3, starting transfers between devices, reduce_pairs(): total += lax.ppermute(theirs, ('x', 'y'), pairs).astype(F32)  3.55 us
  transfers between devices with their start and end apart: 9, of which 9 were waited for; matrix products, arithmetic and copies ran while one was open for 0% of the time, Pallas kernels for 0%

profile of v6, /device:TPU:0, one launch (start us, length us, event | category | flops | bytes accessed | tf_op | source)
XLA Modules:
  0.0 91.3 jit_solution(13241729264604271960)
XLA Ops:
  0.6 1.0 %fusion.2 = bf16[1,2,80,128]{3,1,2,0:T(2,128)(2,1)S(1)} fusion(pred[]{:T(512)S(6)} %eq.7, bf16[2,9280]{1,0:T(2,128)(2,1)} %param.8), kind=kLoop, calls=%fused_computation.16 | loop fusion | flops 20480 | bytes 78081
  1.6 4.1 %collective-permute-start = (bf16[1,2,80,128]{3,2,1,0:T(8,128)(2,1)S(1)}, bf16[1,2,80,128]{3,2,1,0:T(8,128)(2,1)S(1)}, u32[]{:S(2)}, u32[]{:S(2)}) collective-permute-start(bf16[1,2,80,128]{3,2,1,0:T(8,128)(2,1)S(1)} %copy.14), channel_id=1, source_target_pairs={{0,16},{8,24},{16,0},{24,8},{1,17},{9,25},{17,1},{25,9},{2,18},{10... | collective-permute-start | bytes 122888 | tf_op jit(solution)/shard_map/ppermute | solution.py:974
  5.7 2.4 %collective-permute-done = bf16[1,2,80,128]{3,2,1,0:T(8,128)(2,1)S(1)} collective-permute-done((bf16[1,2,80,128]{3,2,1,0:T(8,128)(2,1)S(1)}, bf16[1,2,80,128]{3,2,1,0:T(8,128)(2,1)S(1)}, u32[]{:S(2)}, u32[]{:S(2)}) %collective-permute-start) | collective-permute-done | bytes 40992 | tf_op jit(solution)/shard_map/ppermute | solution.py:974
  8.2 1.5 %collective-permute-start.1 = (bf16[2,2,80,128]{3,2,1,0:T(8,128)(2,1)S(1)}, bf16[2,2,80,128]{3,2,1,0:T(8,128)(2,1)S(1)}, u32[]{:S(2)}, u32[]{:S(2)}) collective-permute-start(bf16[2,2,80,128]{3,2,1,0:T(8,128)(2,1)S(1)} %pad_maximum_fusion.1), channel_id=1, source_target_pairs={{0,8},{8,0},{16,24},{24,16},{1,9},{9,1},{17,25},{25,17},{2,10},{10... | collective-permute-start | bytes 245768 | tf_op jit(solution)/shard_map/ppermute | solution.py:974
  9.7 3.0 %collective-permute-done.1 = bf16[2,2,80,128]{3,2,1,0:T(8,128)(2,1)S(1)} collective-permute-done((bf16[2,2,80,128]{3,2,1,0:T(8,128)(2,1)S(1)}, bf16[2,2,80,128]{3,2,1,0:T(8,128)(2,1)S(1)}, u32[]{:S(2)}, u32[]{:S(2)}) %collective-permute-start.1) | collective-permute-done | bytes 81952 | tf_op jit(solution)/shard_map/ppermute | solution.py:974
  12.7 11.6 %all-gather = bf16[16,2,80,128]{3,2,1,0:T(8,128)(2,1)S(1)} all-gather(bf16[4,2,80,128]{3,2,1,0:T(8,128)(2,1)S(1)} %pad_maximum_fusion), channel_id=2, replica_groups=mesh['z'=4,'x'=2,'y'=2,'core'=2] {'x','y'}, dimensions={0}, use_global_device_ids=true | all-gather | bytes 819200 | tf_op jit(solution)/shard_map/all_gather | solution.py:987
  24.3 0.0 collective-permute-start.2
  24.3 2.1 %collective-permute-done.2.refs_3_ = bf16[4,4,2,80,128]{4,3,2,1,0:T(8,128)(2,1)S(1)} collective-permute-done((bf16[4,4,2,80,128]{4,3,2,1,0:T(8,128)(2,1)S(1)}, bf16[4,4,2,80,128]{4,3,2,1,0:T(8,128)(2,1)S(1)}, u32[]{:S(2)}, u32[]{:S(2)}) %collective-permute-start.2) | collective-permute-done | bytes 655392 | tf_op jit(solution)/shard_map/ppermute | solution.py:974
  26.4 41.3 %shard_map.85 = (f32[17,192,128]{2,1,0:T(8,128)}, f32[17,192,128]{2,1,0:T(8,128)}, bf16[4,4,2,80,128]{4,3,2,1,0:T(8,128)(2,1)S(1)}, bf16[4,4,2,80,128]{4,3,2,1,0:T(8,128)(2,1)S(1)}) custom-call(bf16[17,192,128]{2,1,0:T(8,128)(2,1)} %bitcast.31, bf16[17,192,128]{2,1,0:T(8,128)(2,1)} %bitcast.32, bf16[4,4,2,80,128]{4,3,2,1,0:T(8,128)(2,1)S(1)} %bitcast.30, ...), custom_call_target="tpu_custom_call" | custom-call | tf_op jit(solution)/shard_map/pallas_call | solution.py:942
  67.7 0.2 collective-permute-start.3
  67.9 2.0 %collective-permute-done.3 = bf16[4,4,2,80,128]{4,3,2,1,0:T(8,128)(2,1)S(1)} collective-permute-done((bf16[4,4,2,80,128]{4,3,2,1,0:T(8,128)(2,1)S(1)}, bf16[4,4,2,80,128]{4,3,2,1,0:T(8,128)(2,1)S(1)}, u32[]{:S(2)}, u32[]{:S(2)}) %collective-permute-start.3) | collective-permute-done | bytes 655392 | tf_op jit(solution)/shard_map/ppermute | solution.py:974
  69.9 0.2 add_convert_fusion
  70.1 1.5 %collective-permute-start.4 = (bf16[4,2,80,128]{3,2,1,0:T(8,128)(2,1)S(1)}, bf16[4,2,80,128]{3,2,1,0:T(8,128)(2,1)S(1)}, u32[]{:S(2)}, u32[]{:S(2)}) collective-permute-start(bf16[4,2,80,128]{3,2,1,0:T(8,128)(2,1)S(1)} %get-tuple-element.11), channel_id=1, source_target_pairs={{0,6},{2,4},{4,2},{6,0},{1,7},{3,5},{5,3},{7,1},{8,14},{10,12},{12... | collective-permute-start | bytes 491528 | tf_op jit(solution)/shard_map/ppermute | solution.py:999
  71.6 0.7 collective-permute-start.5
  72.4 1.3 %collective-permute-start.6 = (bf16[4,2,80,128]{3,2,1,0:T(8,128)(2,1)S(1)}, bf16[4,2,80,128]{3,2,1,0:T(8,128)(2,1)S(1)}, u32[]{:S(2)}, u32[]{:S(2)}) collective-permute-start(bf16[4,2,80,128]{3,2,1,0:T(8,128)(2,1)S(1)} %get-tuple-element.12), channel_id=1, source_target_pairs={{0,2},{2,0},{4,6},{6,4},{1,3},{3,1},{5,7},{7,5},{8,10},{10,8},{12,... | collective-permute-start | bytes 491528 | tf_op jit(solution)/shard_map/ppermute | solution.py:999
  73.6 4.5 %collective-permute-done.4 = bf16[4,2,80,128]{3,2,1,0:T(8,128)(2,1)S(1)} collective-permute-done((bf16[4,2,80,128]{3,2,1,0:T(8,128)(2,1)S(1)}, bf16[4,2,80,128]{3,2,1,0:T(8,128)(2,1)S(1)}, u32[]{:S(2)}, u32[]{:S(2)}) %collective-permute-start.4) | collective-permute-done | bytes 163872 | tf_op jit(solution)/shard_map/ppermute | solution.py:999
  78.1 1.9 %collective-permute-done.5 = bf16[4,2,80,128]{3,2,1,0:T(8,128)(2,1)S(1)} collective-permute-done((bf16[4,2,80,128]{3,2,1,0:T(8,128)(2,1)S(1)}, bf16[4,2,80,128]{3,2,1,0:T(8,128)(2,1)S(1)}, u32[]{:S(2)}, u32[]{:S(2)}) %collective-permute-start.5) | collective-permute-done | bytes 163872 | tf_op jit(solution)/shard_map/ppermute | solution.py:999
  80.1 0.7 collective-permute-done.6
  80.8 0.1 fusion.1
  80.9 1.3 %collective-permute-start.7 = (bf16[2,2,80,128]{3,2,1,0:T(8,128)(2,1)S(1)}, bf16[2,2,80,128]{3,2,1,0:T(8,128)(2,1)S(1)}, u32[]{:S(2)}, u32[]{:S(2)}) collective-permute-start(bf16[2,2,80,128]{3,2,1,0:T(8,128)(2,1)S(1)} %dynamic-slice_convert_fusion), channel_id=1, source_target_pairs={{0,8},{8,0},{16,24},{24,16},{1,9},{9,1},{17,25},{25,17},{2,10},{10... | collective-permute-start | bytes 245768 | tf_op jit(solution)/shard_map/ppermute | solution.py:974
  82.2 3.2 %collective-permute-done.7 = bf16[2,2,80,128]{3,2,1,0:T(8,128)(2,1)S(1)} collective-permute-done((bf16[2,2,80,128]{3,2,1,0:T(8,128)(2,1)S(1)}, bf16[2,2,80,128]{3,2,1,0:T(8,128)(2,1)S(1)}, u32[]{:S(2)}, u32[]{:S(2)}) %collective-permute-start.7) | collective-permute-done | bytes 81952 | tf_op jit(solution)/shard_map/ppermute | solution.py:974
  85.5 2.4 %collective-permute-start.8 = (bf16[1,2,80,128]{3,2,1,0:T(8,128)(2,1)S(1)}, bf16[1,2,80,128]{3,2,1,0:T(8,128)(2,1)S(1)}, u32[]{:S(2)}, u32[]{:S(2)}) collective-permute-start(bf16[1,2,80,128]{3,2,1,0:T(8,128)(2,1)S(1)} %dynamic-slice_convert_fusion.1), channel_id=1, source_target_pairs={{0,16},{8,24},{16,0},{24,8},{1,17},{9,25},{17,1},{25,9},{2,18},{10... | collective-permute-start | bytes 122888 | tf_op jit(solution)/shard_map/ppermute | solution.py:974
  87.9 2.6 %collective-permute-done.8 = bf16[1,2,80,128]{3,2,1,0:T(8,128)(2,1)S(1)} collective-permute-done((bf16[1,2,80,128]{3,2,1,0:T(8,128)(2,1)S(1)}, bf16[1,2,80,128]{3,2,1,0:T(8,128)(2,1)S(1)}, u32[]{:S(2)}, u32[]{:S(2)}) %collective-permute-start.8) | collective-permute-done | bytes 40992 | tf_op jit(solution)/shard_map/ppermute | solution.py:974
  90.5 0.8 slice_select_fusion
  (9 shorter events, 0.2 us)
Async XLA Ops:
  1.6 6.5 %collective-permute-start = (bf16[1,2,80,128]{3,2,1,0:T(8,128)(2,1)S(1)}, bf16[1,2,80,128]{3,2,1,0:T(8,128)(2,1)S(1)}, u32[]{:S(2)}, u32[]{:S(2)}) collective-permute-start(bf16[1,2,80,128]{3,2,1,0:T(8,128)(2,1)S(1)} %copy.14), channel_id=1, source_target_pairs={{0,16},{8,24},{16,0},{24,8},{1,17},{9,25},{17,1},{25,9},{2,18},{10... | collective-permute-start | bytes 122888 | tf_op jit(solution)/shard_map/ppermute | solution.py:974
  8.2 4.5 %collective-permute-start.1 = (bf16[2,2,80,128]{3,2,1,0:T(8,128)(2,1)S(1)}, bf16[2,2,80,128]{3,2,1,0:T(8,128)(2,1)S(1)}, u32[]{:S(2)}, u32[]{:S(2)}) collective-permute-start(bf16[2,2,80,128]{3,2,1,0:T(8,128)(2,1)S(1)} %pad_maximum_fusion.1), channel_id=1, source_target_pairs={{0,8},{8,0},{16,24},{24,16},{1,9},{9,1},{17,25},{25,17},{2,10},{10... | collective-permute-start | bytes 245768 | tf_op jit(solution)/shard_map/ppermute | solution.py:974
  24.3 2.1 %collective-permute-start.2 = (bf16[4,4,2,80,128]{4,3,2,1,0:T(8,128)(2,1)S(1)}, bf16[4,4,2,80,128]{4,3,2,1,0:T(8,128)(2,1)S(1)}, u32[]{:S(2)}, u32[]{:S(2)}) collective-permute-start(bf16[4,4,2,80,128]{4,3,2,1,0:T(8,128)(2,1)S(1)} %bitcast.29), channel_id=1, source_target_pairs={{0,1},{1,0},{2,3},{3,2},{4,5},{5,4},{6,7},{7,6},{8,9},{9,8},{10,11... | collective-permute-start | bytes 1966088 | tf_op jit(solution)/shard_map/ppermute | solution.py:974
  67.7 2.2 %collective-permute-start.3 = (bf16[4,4,2,80,128]{4,3,2,1,0:T(8,128)(2,1)S(1)}, bf16[4,4,2,80,128]{4,3,2,1,0:T(8,128)(2,1)S(1)}, u32[]{:S(2)}, u32[]{:S(2)}) collective-permute-start(bf16[4,4,2,80,128]{4,3,2,1,0:T(8,128)(2,1)S(1)} %get-tuple-element.10), channel_id=1, source_target_pairs={{0,1},{1,0},{2,3},{3,2},{4,5},{5,4},{6,7},{7,6},{8,9},{9,8},{10,11... | collective-permute-start | bytes 1966088 | tf_op jit(solution)/shard_map/ppermute | solution.py:974
  70.1 8.1 %collective-permute-start.4 = (bf16[4,2,80,128]{3,2,1,0:T(8,128)(2,1)S(1)}, bf16[4,2,80,128]{3,2,1,0:T(8,128)(2,1)S(1)}, u32[]{:S(2)}, u32[]{:S(2)}) collective-permute-start(bf16[4,2,80,128]{3,2,1,0:T(8,128)(2,1)S(1)} %get-tuple-element.11), channel_id=1, source_target_pairs={{0,6},{2,4},{4,2},{6,0},{1,7},{3,5},{5,3},{7,1},{8,14},{10,12},{12... | collective-permute-start | bytes 491528 | tf_op jit(solution)/shard_map/ppermute | solution.py:999
  71.6 8.5 %collective-permute-start.5 = (bf16[4,2,80,128]{3,2,1,0:T(8,128)(2,1)S(1)}, bf16[4,2,80,128]{3,2,1,0:T(8,128)(2,1)S(1)}, u32[]{:S(2)}, u32[]{:S(2)}) collective-permute-start(bf16[4,2,80,128]{3,2,1,0:T(8,128)(2,1)S(1)} %get-tuple-element.13), channel_id=1, source_target_pairs={{0,4},{2,6},{4,0},{6,2},{1,5},{3,7},{5,1},{7,3},{8,12},{10,14},{12... | collective-permute-start | bytes 491528 | tf_op jit(solution)/shard_map/ppermute | solution.py:999
  72.4 8.5 %collective-permute-start.6 = (bf16[4,2,80,128]{3,2,1,0:T(8,128)(2,1)S(1)}, bf16[4,2,80,128]{3,2,1,0:T(8,128)(2,1)S(1)}, u32[]{:S(2)}, u32[]{:S(2)}) collective-permute-start(bf16[4,2,80,128]{3,2,1,0:T(8,128)(2,1)S(1)} %get-tuple-element.12), channel_id=1, source_target_pairs={{0,2},{2,0},{4,6},{6,4},{1,3},{3,1},{5,7},{7,5},{8,10},{10,8},{12,... | collective-permute-start | bytes 491528 | tf_op jit(solution)/shard_map/ppermute | solution.py:999
  80.9 4.5 %collective-permute-start.7 = (bf16[2,2,80,128]{3,2,1,0:T(8,128)(2,1)S(1)}, bf16[2,2,80,128]{3,2,1,0:T(8,128)(2,1)S(1)}, u32[]{:S(2)}, u32[]{:S(2)}) collective-permute-start(bf16[2,2,80,128]{3,2,1,0:T(8,128)(2,1)S(1)} %dynamic-slice_convert_fusion), channel_id=1, source_target_pairs={{0,8},{8,0},{16,24},{24,16},{1,9},{9,1},{17,25},{25,17},{2,10},{10... | collective-permute-start | bytes 245768 | tf_op jit(solution)/shard_map/ppermute | solution.py:974
  85.5 5.0 %collective-permute-start.8 = (bf16[1,2,80,128]{3,2,1,0:T(8,128)(2,1)S(1)}, bf16[1,2,80,128]{3,2,1,0:T(8,128)(2,1)S(1)}, u32[]{:S(2)}, u32[]{:S(2)}) collective-permute-start(bf16[1,2,80,128]{3,2,1,0:T(8,128)(2,1)S(1)} %dynamic-slice_convert_fusion.1), channel_id=1, source_target_pairs={{0,16},{8,24},{16,0},{24,8},{1,17},{9,25},{17,1},{25,9},{2,18},{10... | collective-permute-start | bytes 122888 | tf_op jit(solution)/shard_map/ppermute | solution.py:974

commit v7 on v6

--- a/solution.py
+++ b/solution.py
@@ -68,12 +68,12 @@
 
 
 def gather_flat(own, other, place, layer, flat):
-    z, core = place[0], place[1]
+    z, core, xy = place
     for chip in range(FLAT // 145):
         turn = z ^ (chip // 4)
         at = (turn & 1) * 2 + turn // 2
-        mine = own[chip % 4, at, layer].astype(F32)
-        theirs = other[chip % 4, at, layer].astype(F32)
+        mine = own[xy ^ (chip % 4), at, layer].astype(F32)
+        theirs = other[xy ^ (chip % 4), at, layer].astype(F32)
         first = jnp.where(core == 0, mine, theirs)
         second = jnp.where(core == 0, theirs, mine)
         base = 145 * chip
@@ -145,7 +145,13 @@
     tmp[0, pl.ds(1, 96, stride=2), :] = splice(e[1], e[2])
     tmp[1, pl.ds(1, 96, stride=2), :] = low_half(swap(e[2]))
     w_out = jnp.concatenate([tmp[0, 0:D, :], tmp[1, 0:D, :]], axis=1)
-    w["out_t"][...] = jnp.transpose(w_out.astype(BF16))[0:D]
+    bias_rows = jnp.where(
+        lax.broadcasted_iota(jnp.int32, (64, 2 * LANES), 0) == 0,
+        jnp.broadcast_to(vectors[2], (64, 2 * LANES)),
+        0.0,
+    )
+    w_out = jnp.concatenate([w_out, bias_rows], axis=0).astype(BF16)
+    w["out_t"][...] = jnp.transpose(w_out)[0:D]
 
     g = [rows(1162 + j, 192, 4) for j in range(5)]
     tiles = [splice(g[j], g[j + 1]) for j in range(4)]
@@ -180,7 +186,7 @@
     )
 
 
-def pack(flat, acc, sums, tmp):
+def pack(flat, w, acc, sums, tmp):
     def put(start, count, stride, value):
         flat[pl.ds(start, count, stride=stride), :] = value
 
@@ -190,11 +196,22 @@
     def down(j, start, count, stride):
         return acc["down"][j, pl.ds(start, count, stride=stride), :]
 
+    def through(weight, name):
+        total = jnp.zeros((D, LANES), F32)
+        for j in range(acc[name].shape[0]):
+            part = weight[0:D, j * LANES : (j + 1) * LANES].astype(F32)
+            total += part * acc[name][j, D : D + 1, :]
+        return row_of(total)
+
     g1 = row_of(sums[0])
-    b1 = row_of(sums[1])
-    g2 = row_of(sums[2])
-    b2 = row_of(sums[3])
-    bo = row_of(sums[4])
+    b1 = through(w["qkv"], "qkv")
+    g2 = row_of(sums[1])
+    b2 = through(w["gu"], "gu")
+    w_out = jnp.transpose(acc["out_t"][...])
+    bo = (
+        w_out[D : D + 1, 0:LANES],
+        jnp.concatenate([w_out[D : D + 1, LANES:], jnp.zeros((1, 64), F32)], axis=1),
+    )
     put_row(0, g1[0])
     put_row(1, after(g1[1], b1[0]))
     put_row(2, splice(b1[0], b1[1]))
@@ -215,11 +232,8 @@
     put_row(868, after(bias[1], bias[4]))
     put_row(869, splice(bias[4], bias[5]))
 
-    w_out = jnp.transpose(
-        jnp.concatenate([acc["out_t"][...], jnp.zeros((64, D), F32)], axis=0)
-    )
-    tmp[0, 0:D, :] = w_out[:, 0:LANES]
-    tmp[1, 0:D, :] = w_out[:, LANES:]
+    tmp[0, 0:D, :] = w_out[0:D, 0:LANES]
+    tmp[1, 0:D, 0 : D - LANES] = w_out[0:D, LANES:]
     even = [tmp[j, pl.ds(0, 96, stride=2), :] for j in range(2)]
     odd = [tmp[j, pl.ds(1, 96, stride=2), :] for j in range(2)]
     put(870, 96, 3, even[0])
@@ -496,8 +510,8 @@
                 return
             tail = dot(low, at["values"], 0, 0)
             main, last = heads_joined(at["tiles"], tail, env["heads"])
-            s["mixed"][at["g"], 0:LANES, :] = main
-            s["mixed"][at["g"], LANES:GT, :] = last
+            s["mixed"][at["g"], 0:LANES, 0:D] = main
+            s["mixed"][at["g"], LANES:GT, 0:D] = last
 
         staged([(u, t) for u in range(FORWARD_GROUPS) for t in range(5)], scores, mix)
 
@@ -512,7 +526,7 @@
     def normed(c, product):
         lows = []
         for half in HALVES:
-            middle = view(s["x"], c).at[:, half][...] + (product[:, half] + w["cols"][2])
+            middle = view(s["x"], c).at[:, half][...] + product[:, half]
             view(s["middle"], c).at[:, half][...] = middle
             xhat, rstd, low = norm(middle, w["cols"][3], w["cols"][4])
             view(s["xhat2"], c).at[:, half][...] = xhat
@@ -577,19 +591,16 @@
         for half in HALVES:
             xhat = view(s["xhat2"], c).at[:, half][...]
             part = d_normed[:, half]
-            sums[2] += part * xhat
-            sums[3] += part
+            sums[1] += part * xhat
             g = view(s["g"], c).at[:, half]
             d_middle = g[...] + norm_back(
                 part, xhat, view(s["rstd2"], c).at[:, half][...], w["cols"][3]
             )
             g[...] = d_middle
-            low = d_middle.astype(BF16)
-            sums[4] += low.astype(F32)
-            lows.append(low)
+            lows.append(d_middle.astype(BF16))
         d_attended = jnp.concatenate(lows, axis=1)
         mixed = from_groups(s["mixed"][:, group_rows(c), :].astype(F32)).astype(BF16)
-        return dot(d_attended, w["out_t"][...], 0, 0), dot(d_attended, mixed, 1, 0)
+        return dot(d_attended, w["out_t"][:, 0:D], 0, 0), dot(d_attended, mixed, 1, 0)
 
     def finish(c, held):
         d_mixed, grad_out = held
@@ -687,7 +698,6 @@
             xhat = view(s["xhat1"], c).at[:, half][...]
             part = d_normed[:, half]
             sums[0] += part * xhat
-            sums[1] += part
             back = norm_back(part, xhat, view(s["rstd1"], c).at[:, half][...], w["cols"][0])
             done(c, i, view(s["g"], c).at[:, half][...] + back)
 
@@ -703,7 +713,7 @@
         "k": ((GROUPS, GT, D), BF16),
         "v": ((GROUPS, GT, D), BF16),
         "att": ((GROUPS, 24, QL), F32),
-        "mixed": ((GROUPS, GT, D), BF16),
+        "mixed": ((GROUPS, GT, 2 * LANES), BF16),
         "xhat2": ((D, TOKENS), F32),
         "rstd2": ((1, TOKENS), F32),
         "h2": ((D + 16, TOKENS), BF16),
@@ -717,7 +727,7 @@
     return {
         "cols": ((6, D, LANES), F32),
         "qkv": ((D + 16, 6 * LANES), BF16),
-        "out_t": ((D, D), BF16),
+        "out_t": ((D, 2 * LANES), BF16),
         "gu": ((D, 2 * FF), BF16),
         "gu_t": ((2 * FF, D + 16), BF16),
         "down": ((FF, D), BF16),
@@ -728,10 +738,10 @@
 def accumulators():
     return {
         "qkv": ((6, D + 16, LANES), F32),
-        "out_t": ((D, D), F32),
+        "out_t": ((D, 2 * LANES), F32),
         "gu": ((4, D + 16, LANES), F32),
         "down": ((2, FF + 16, LANES), F32),
-        "sums": ((5, D, LANES), F32),
+        "sums": ((2, D, LANES), F32),
     }
 
 
@@ -827,7 +837,10 @@
     acc = [table["acc0"], table["acc1"]]
     s, w = [table["s0"], table["s1"]], [table["w0"], table["w1"]]
     sums = [part["sums"] for part in acc]
-    place = (lax.axis_index("z"), lax.axis_index("core")) if four else (0, 0)
+    place = (0, 0, 0)
+    if four:
+        xy = 2 * lax.axis_index("x") + lax.axis_index("y")
+        place = (lax.axis_index("z"), lax.axis_index("core"), xy)
 
     copies = [
         pltpu.make_async_copy(source, env[name], sems.at[i])
@@ -844,6 +857,8 @@
     for part in range(3):
         env["dqkv"][:, :, 2 * LANES * part + D : 2 * LANES * (part + 1)] = pad
     for layer in range(LAYERS):
+        mark = lax.broadcasted_iota(jnp.int32, (GROUPS, GT, 2 * LANES - D), 2) == 0
+        s[layer]["mixed"][:, :, D:] = jnp.where(mark, 1.0, 0.0).astype(BF16)
         ones_below(s[layer]["h1"], D)
         ones_below(s[layer]["h2"], D)
         ones_below(s[layer]["act"], FF)
@@ -915,7 +930,7 @@
     skewed((products, finish_down, gate_up, normed_back, finish_back))
 
     def send(layer):
-        pack(env["flat"], acc[layer], sums[layer], env["tmp"])
+        pack(env["flat"], w[layer], acc[layer], sums[layer], env["tmp"])
         scatter_blocks(env["flat"], place, layer, keep_out, give_out)
 
     send(1)
@@ -984,7 +999,11 @@
     ).reshape(1, LAYERS, BLOCK, LANES)
     for bit in (2, 1):
         part = jnp.concatenate([part, swap_along(part, "z", bit)], axis=0)
-    own = lax.all_gather(part, ("x", "y"), axis=0, tiled=False)
+    parts = [part]
+    for away in (1, 2, 3):
+        pairs = [(i, i ^ away) for i in range(4)]
+        parts.append(lax.ppermute(part, ("x", "y"), pairs))
+    own = jnp.stack(parts)
     return own, swap_along(own, "core", 1)
 
 

time: 91.5 us -> 90 us (0.984)
  blocking collectives: 11.6 us -> 0 us
  waiting for transfers between devices: 22.4 us -> 28.3 us
  starting transfers between devices: 13.1 us -> 16.7 us
    all_gather x1 -> x0, blocking collectives: 11.6 us -> none  [gather_pairs(): own = lax.all_gather(part, ('x', 'y'), axis=0, tiled=False)]
    ppermute x0 -> x3, waiting for transfers between devices: none -> 5.95 us  [gather_pairs(): parts.append(lax.ppermute(part, ('x', 'y'), pairs))]
    ppermute x0 -> x3, starting transfers between devices: none -> 3.55 us  [gather_pairs(): parts.append(lax.ppermute(part, ('x', 'y'), pairs))]
  transfers between devices with their start and end apart: 9 -> 12, of which waited for: 9 -> 12; matrix products, arithmetic and copies ran while one was open for 0% -> 0% of each run, Pallas kernels for 0% -> 0%
where the time goes in v7:
time: 90 us; the launch traced here: 89.8 us
  Pallas kernels  41.7 us (46%)
  waiting for transfers between devices  28.3 us (31%)
  starting transfers between devices  16.7 us (19%)
  other arithmetic  2.11 us (2%)
    pallas_call x1, Pallas kernels, run_kernel(): pl.pallas_call(body, out_shape=(full, full, blocks, blocks), in_specs=[an...  41.7 us
    ppermute x6, waiting for transfers between devices, swap_along(): return lax.ppermute(x, axis, pairs)  15.2 us
    ppermute x6, starting transfers between devices, swap_along(): return lax.ppermute(x, axis, pairs)  9.63 us
    ppermute x3, waiting for transfers between devices, reduce_pairs(): total += lax.ppermute(theirs, ('x', 'y'), pairs).astype(F32)  7.16 us
    ppermute x3, waiting for transfers between devices, gather_pairs(): parts.append(lax.ppermute(part, ('x', 'y'), pairs))  5.95 us
    ppermute x3, starting transfers between devices, reduce_pairs(): total += lax.ppermute(theirs, ('x', 'y'), pairs).astype(F32)  3.55 us
    ppermute x3, starting transfers between devices, gather_pairs(): parts.append(lax.ppermute(part, ('x', 'y'), pairs))  3.55 us
  transfers between devices with their start and end apart: 12, of which 12 were waited for; matrix products, arithmetic and copies ran while one was open for 0% of the time, Pallas kernels for 0%

profile of v7, /device:TPU:0, one launch (start us, length us, event | category | flops | bytes accessed | tf_op | source)
XLA Modules:
  0.0 89.8 jit_solution(2901690394532647146)
XLA Ops:
  0.6 1.0 %fusion.2 = bf16[1,2,80,128]{3,1,2,0:T(2,128)(2,1)S(1)} fusion(pred[]{:T(512)S(6)} %eq.7, bf16[2,9280]{1,0:T(2,128)(2,1)} %param.8), kind=kLoop, calls=%fused_computation.16 | loop fusion | flops 20480 | bytes 78081
  1.6 4.1 %collective-permute-start = (bf16[1,2,80,128]{3,2,1,0:T(8,128)(2,1)S(1)}, bf16[1,2,80,128]{3,2,1,0:T(8,128)(2,1)S(1)}, u32[]{:S(2)}, u32[]{:S(2)}) collective-permute-start(bf16[1,2,80,128]{3,2,1,0:T(8,128)(2,1)S(1)} %get-tuple-element.14), channel_id=1, source_target_pairs={{0,16},{8,24},{16,0},{24,8},{1,17},{9,25},{17,1},{25,9},{2,18},{10... | collective-permute-start | bytes 122888 | tf_op jit(solution)/shard_map/ppermute | solution.py:989
  5.7 2.4 %collective-permute-done = bf16[1,2,80,128]{3,2,1,0:T(8,128)(2,1)S(1)} collective-permute-done((bf16[1,2,80,128]{3,2,1,0:T(8,128)(2,1)S(1)}, bf16[1,2,80,128]{3,2,1,0:T(8,128)(2,1)S(1)}, u32[]{:S(2)}, u32[]{:S(2)}) %collective-permute-start) | collective-permute-done | bytes 40992 | tf_op jit(solution)/shard_map/ppermute | solution.py:989
  8.2 1.5 %collective-permute-start.1 = (bf16[2,2,80,128]{3,2,1,0:T(8,128)(2,1)S(1)}, bf16[2,2,80,128]{3,2,1,0:T(8,128)(2,1)S(1)}, u32[]{:S(2)}, u32[]{:S(2)}) collective-permute-start(bf16[2,2,80,128]{3,2,1,0:T(8,128)(2,1)S(1)} %pad_maximum_fusion.1), channel_id=1, source_target_pairs={{0,8},{8,0},{16,24},{24,16},{1,9},{9,1},{17,25},{25,17},{2,10},{10... | collective-permute-start | bytes 245768 | tf_op jit(solution)/shard_map/ppermute | solution.py:989
  9.7 3.0 %collective-permute-done.1 = bf16[2,2,80,128]{3,2,1,0:T(8,128)(2,1)S(1)} collective-permute-done((bf16[2,2,80,128]{3,2,1,0:T(8,128)(2,1)S(1)}, bf16[2,2,80,128]{3,2,1,0:T(8,128)(2,1)S(1)}, u32[]{:S(2)}, u32[]{:S(2)}) %collective-permute-start.1) | collective-permute-done | bytes 81952 | tf_op jit(solution)/shard_map/ppermute | solution.py:989
  12.7 1.8 %collective-permute-start.2 = (bf16[4,2,80,128]{3,2,1,0:T(8,128)(2,1)S(1)}, bf16[4,2,80,128]{3,2,1,0:T(8,128)(2,1)S(1)}, u32[]{:S(2)}, u32[]{:S(2)}) collective-permute-start(bf16[4,2,80,128]{3,2,1,0:T(8,128)(2,1)S(1)} %constant_dynamic-update-slice_fusion), channel_id=1, source_target_pairs={{0,2},{2,0},{4,6},{6,4},{1,3},{3,1},{5,7},{7,5},{8,10},{10,8},{12,... | collective-permute-start | bytes 491528 | tf_op jit(solution)/shard_map/ppermute | solution.py:1005
  14.5 1.5 %collective-permute-start.3 = (bf16[4,2,80,128]{3,2,1,0:T(8,128)(2,1)S(1)}, bf16[4,2,80,128]{3,2,1,0:T(8,128)(2,1)S(1)}, u32[]{:S(2)}, u32[]{:S(2)}) collective-permute-start(bf16[4,2,80,128]{3,2,1,0:T(8,128)(2,1)S(1)} %constant_dynamic-update-slice_fusion), channel_id=1, source_target_pairs={{0,4},{2,6},{4,0},{6,2},{1,5},{3,7},{5,1},{7,3},{8,12},{10,14},{12... | collective-permute-start | bytes 491528 | tf_op jit(solution)/shard_map/ppermute | solution.py:1005
  16.0 0.3 collective-permute-start.4
  16.2 3.4 %collective-permute-done.2 = bf16[4,2,80,128]{3,2,1,0:T(8,128)(2,1)S(1)} collective-permute-done((bf16[4,2,80,128]{3,2,1,0:T(8,128)(2,1)S(1)}, bf16[4,2,80,128]{3,2,1,0:T(8,128)(2,1)S(1)}, u32[]{:S(2)}, u32[]{:S(2)}) %collective-permute-start.2) | collective-permute-done | bytes 163872 | tf_op jit(solution)/shard_map/ppermute | solution.py:1005
  19.6 0.2 collective-permute-done.3
  19.8 2.4 %collective-permute-done.4 = bf16[4,2,80,128]{3,2,1,0:T(8,128)(2,1)S(1)} collective-permute-done((bf16[4,2,80,128]{3,2,1,0:T(8,128)(2,1)S(1)}, bf16[4,2,80,128]{3,2,1,0:T(8,128)(2,1)S(1)}, u32[]{:S(2)}, u32[]{:S(2)}) %collective-permute-start.4) | collective-permute-done | bytes 163872 | tf_op jit(solution)/shard_map/ppermute | solution.py:1005
  22.2 0.1 pad_maximum_fusion.refs_2_
  22.3 0.1 collective-permute-start.5
  22.3 2.1 %collective-permute-done.5.refs_3_ = bf16[4,4,2,80,128]{4,3,2,1,0:T(8,128)(2,1)S(1)} collective-permute-done((bf16[4,4,2,80,128]{4,3,2,1,0:T(8,128)(2,1)S(1)}, bf16[4,4,2,80,128]{4,3,2,1,0:T(8,128)(2,1)S(1)}, u32[]{:S(2)}, u32[]{:S(2)}) %collective-permute-start.5) | collective-permute-done | bytes 655392 | tf_op jit(solution)/shard_map/ppermute | solution.py:989
  24.4 41.7 %shard_map.85 = (f32[17,192,128]{2,1,0:T(8,128)}, f32[17,192,128]{2,1,0:T(8,128)}, bf16[4,4,2,80,128]{4,3,2,1,0:T(8,128)(2,1)S(1)}, bf16[4,4,2,80,128]{4,3,2,1,0:T(8,128)(2,1)S(1)}) custom-call(bf16[17,192,128]{2,1,0:T(8,128)(2,1)} %bitcast.33, bf16[17,192,128]{2,1,0:T(8,128)(2,1)} %bitcast.34, bf16[4,4,2,80,128]{4,3,2,1,0:T(8,128)(2,1)S(1)} %pad_maximum_fusion.refs_2_, ...), custom_call_target="tpu_custom_call" | custom-call | tf_op jit(solution)/shard_map/pallas_call | solution.py:957
  66.2 0.2 collective-permute-start.6
  66.4 2.0 %collective-permute-done.6 = bf16[4,4,2,80,128]{4,3,2,1,0:T(8,128)(2,1)S(1)} collective-permute-done((bf16[4,4,2,80,128]{4,3,2,1,0:T(8,128)(2,1)S(1)}, bf16[4,4,2,80,128]{4,3,2,1,0:T(8,128)(2,1)S(1)}, u32[]{:S(2)}, u32[]{:S(2)}) %collective-permute-start.6) | collective-permute-done | bytes 655392 | tf_op jit(solution)/shard_map/ppermute | solution.py:989
  68.3 0.2 add_convert_fusion
  68.6 1.8 %collective-permute-start.7 = (bf16[4,2,80,128]{3,2,1,0:T(8,128)(2,1)S(1)}, bf16[4,2,80,128]{3,2,1,0:T(8,128)(2,1)S(1)}, u32[]{:S(2)}, u32[]{:S(2)}) collective-permute-start(bf16[4,2,80,128]{3,2,1,0:T(8,128)(2,1)S(1)} %get-tuple-element.11), channel_id=1, source_target_pairs={{0,6},{2,4},{4,2},{6,0},{1,7},{3,5},{5,3},{7,1},{8,14},{10,12},{12... | collective-permute-start | bytes 491528 | tf_op jit(solution)/shard_map/ppermute | solution.py:1018
  70.4 0.5 collective-permute-start.8
  70.9 1.2 %collective-permute-start.9 = (bf16[4,2,80,128]{3,2,1,0:T(8,128)(2,1)S(1)}, bf16[4,2,80,128]{3,2,1,0:T(8,128)(2,1)S(1)}, u32[]{:S(2)}, u32[]{:S(2)}) collective-permute-start(bf16[4,2,80,128]{3,2,1,0:T(8,128)(2,1)S(1)} %get-tuple-element.12), channel_id=1, source_target_pairs={{0,2},{2,0},{4,6},{6,4},{1,3},{3,1},{5,7},{7,5},{8,10},{10,8},{12,... | collective-permute-start | bytes 491528 | tf_op jit(solution)/shard_map/ppermute | solution.py:1018
  72.1 4.5 %collective-permute-done.7 = bf16[4,2,80,128]{3,2,1,0:T(8,128)(2,1)S(1)} collective-permute-done((bf16[4,2,80,128]{3,2,1,0:T(8,128)(2,1)S(1)}, bf16[4,2,80,128]{3,2,1,0:T(8,128)(2,1)S(1)}, u32[]{:S(2)}, u32[]{:S(2)}) %collective-permute-start.7) | collective-permute-done | bytes 163872 | tf_op jit(solution)/shard_map/ppermute | solution.py:1018
  76.6 2.0 %collective-permute-done.8 = bf16[4,2,80,128]{3,2,1,0:T(8,128)(2,1)S(1)} collective-permute-done((bf16[4,2,80,128]{3,2,1,0:T(8,128)(2,1)S(1)}, bf16[4,2,80,128]{3,2,1,0:T(8,128)(2,1)S(1)}, u32[]{:S(2)}, u32[]{:S(2)}) %collective-permute-start.8) | collective-permute-done | bytes 163872 | tf_op jit(solution)/shard_map/ppermute | solution.py:1018
  78.7 0.6 collective-permute-done.9
  79.3 0.1 fusion.1
  79.4 1.3 %collective-permute-start.10 = (bf16[2,2,80,128]{3,2,1,0:T(8,128)(2,1)S(1)}, bf16[2,2,80,128]{3,2,1,0:T(8,128)(2,1)S(1)}, u32[]{:S(2)}, u32[]{:S(2)}) collective-permute-start(bf16[2,2,80,128]{3,2,1,0:T(8,128)(2,1)S(1)} %dynamic-slice_convert_fusion), channel_id=1, source_target_pairs={{0,8},{8,0},{16,24},{24,16},{1,9},{9,1},{17,25},{25,17},{2,10},{10... | collective-permute-start | bytes 245768 | tf_op jit(solution)/shard_map/ppermute | solution.py:989
  80.7 3.2 %collective-permute-done.10 = bf16[2,2,80,128]{3,2,1,0:T(8,128)(2,1)S(1)} collective-permute-done((bf16[2,2,80,128]{3,2,1,0:T(8,128)(2,1)S(1)}, bf16[2,2,80,128]{3,2,1,0:T(8,128)(2,1)S(1)}, u32[]{:S(2)}, u32[]{:S(2)}) %collective-permute-start.10) | collective-permute-done | bytes 81952 | tf_op jit(solution)/shard_map/ppermute | solution.py:989
  83.9 2.4 %collective-permute-start.11 = (bf16[1,2,80,128]{3,2,1,0:T(8,128)(2,1)S(1)}, bf16[1,2,80,128]{3,2,1,0:T(8,128)(2,1)S(1)}, u32[]{:S(2)}, u32[]{:S(2)}) collective-permute-start(bf16[1,2,80,128]{3,2,1,0:T(8,128)(2,1)S(1)} %dynamic-slice_convert_fusion.1), channel_id=1, source_target_pairs={{0,16},{8,24},{16,0},{24,8},{1,17},{9,25},{17,1},{25,9},{2,18},{10... | collective-permute-start | bytes 122888 | tf_op jit(solution)/shard_map/ppermute | solution.py:989
  86.4 2.6 %collective-permute-done.11 = bf16[1,2,80,128]{3,2,1,0:T(8,128)(2,1)S(1)} collective-permute-done((bf16[1,2,80,128]{3,2,1,0:T(8,128)(2,1)S(1)}, bf16[1,2,80,128]{3,2,1,0:T(8,128)(2,1)S(1)}, u32[]{:S(2)}, u32[]{:S(2)}) %collective-permute-start.11) | collective-permute-done | bytes 40992 | tf_op jit(solution)/shard_map/ppermute | solution.py:989
  89.0 0.8 slice_select_fusion
  (10 shorter events, 0.2 us)
Async XLA Ops:
  1.6 6.5 %collective-permute-start = (bf16[1,2,80,128]{3,2,1,0:T(8,128)(2,1)S(1)}, bf16[1,2,80,128]{3,2,1,0:T(8,128)(2,1)S(1)}, u32[]{:S(2)}, u32[]{:S(2)}) collective-permute-start(bf16[1,2,80,128]{3,2,1,0:T(8,128)(2,1)S(1)} %get-tuple-element.14), channel_id=1, source_target_pairs={{0,16},{8,24},{16,0},{24,8},{1,17},{9,25},{17,1},{25,9},{2,18},{10... | collective-permute-start | bytes 122888 | tf_op jit(solution)/shard_map/ppermute | solution.py:989
  8.2 4.5 %collective-permute-start.1 = (bf16[2,2,80,128]{3,2,1,0:T(8,128)(2,1)S(1)}, bf16[2,2,80,128]{3,2,1,0:T(8,128)(2,1)S(1)}, u32[]{:S(2)}, u32[]{:S(2)}) collective-permute-start(bf16[2,2,80,128]{3,2,1,0:T(8,128)(2,1)S(1)} %pad_maximum_fusion.1), channel_id=1, source_target_pairs={{0,8},{8,0},{16,24},{24,16},{1,9},{9,1},{17,25},{25,17},{2,10},{10... | collective-permute-start | bytes 245768 | tf_op jit(solution)/shard_map/ppermute | solution.py:989
  12.7 6.9 %collective-permute-start.2 = (bf16[4,2,80,128]{3,2,1,0:T(8,128)(2,1)S(1)}, bf16[4,2,80,128]{3,2,1,0:T(8,128)(2,1)S(1)}, u32[]{:S(2)}, u32[]{:S(2)}) collective-permute-start(bf16[4,2,80,128]{3,2,1,0:T(8,128)(2,1)S(1)} %constant_dynamic-update-slice_fusion), channel_id=1, source_target_pairs={{0,2},{2,0},{4,6},{6,4},{1,3},{3,1},{5,7},{7,5},{8,10},{10,8},{12,... | collective-permute-start | bytes 491528 | tf_op jit(solution)/shard_map/ppermute | solution.py:1005
  14.5 5.3 %collective-permute-start.3 = (bf16[4,2,80,128]{3,2,1,0:T(8,128)(2,1)S(1)}, bf16[4,2,80,128]{3,2,1,0:T(8,128)(2,1)S(1)}, u32[]{:S(2)}, u32[]{:S(2)}) collective-permute-start(bf16[4,2,80,128]{3,2,1,0:T(8,128)(2,1)S(1)} %constant_dynamic-update-slice_fusion), channel_id=1, source_target_pairs={{0,4},{2,6},{4,0},{6,2},{1,5},{3,7},{5,1},{7,3},{8,12},{10,14},{12... | collective-permute-start | bytes 491528 | tf_op jit(solution)/shard_map/ppermute | solution.py:1005
  16.0 6.2 %collective-permute-start.4 = (bf16[4,2,80,128]{3,2,1,0:T(8,128)(2,1)S(1)}, bf16[4,2,80,128]{3,2,1,0:T(8,128)(2,1)S(1)}, u32[]{:S(2)}, u32[]{:S(2)}) collective-permute-start(bf16[4,2,80,128]{3,2,1,0:T(8,128)(2,1)S(1)} %constant_dynamic-update-slice_fusion), channel_id=1, source_target_pairs={{0,6},{2,4},{4,2},{6,0},{1,7},{3,5},{5,3},{7,1},{8,14},{10,12},{12... | collective-permute-start | bytes 491528 | tf_op jit(solution)/shard_map/ppermute | solution.py:1005
  22.3 2.2 %collective-permute-start.5 = (bf16[4,4,2,80,128]{4,3,2,1,0:T(8,128)(2,1)S(1)}, bf16[4,4,2,80,128]{4,3,2,1,0:T(8,128)(2,1)S(1)}, u32[]{:S(2)}, u32[]{:S(2)}) collective-permute-start(bf16[4,4,2,80,128]{4,3,2,1,0:T(8,128)(2,1)S(1)} %pad_maximum_fusion.refs_2_), channel_id=1, source_target_pairs={{0,1},{1,0},{2,3},{3,2},{4,5},{5,4},{6,7},{7,6},{8,9},{9,8},{10,11... | collective-permute-start | bytes 1966088 | tf_op jit(solution)/shard_map/ppermute | solution.py:989
  66.2 2.2 %collective-permute-start.6 = (bf16[4,4,2,80,128]{4,3,2,1,0:T(8,128)(2,1)S(1)}, bf16[4,4,2,80,128]{4,3,2,1,0:T(8,128)(2,1)S(1)}, u32[]{:S(2)}, u32[]{:S(2)}) collective-permute-start(bf16[4,4,2,80,128]{4,3,2,1,0:T(8,128)(2,1)S(1)} %get-tuple-element.10), channel_id=1, source_target_pairs={{0,1},{1,0},{2,3},{3,2},{4,5},{5,4},{6,7},{7,6},{8,9},{9,8},{10,11... | collective-permute-start | bytes 1966088 | tf_op jit(solution)/shard_map/ppermute | solution.py:989
  68.6 8.1 %collective-permute-start.7 = (bf16[4,2,80,128]{3,2,1,0:T(8,128)(2,1)S(1)}, bf16[4,2,80,128]{3,2,1,0:T(8,128)(2,1)S(1)}, u32[]{:S(2)}, u32[]{:S(2)}) collective-permute-start(bf16[4,2,80,128]{3,2,1,0:T(8,128)(2,1)S(1)} %get-tuple-element.11), channel_id=1, source_target_pairs={{0,6},{2,4},{4,2},{6,0},{1,7},{3,5},{5,3},{7,1},{8,14},{10,12},{12... | collective-permute-start | bytes 491528 | tf_op jit(solution)/shard_map/ppermute | solution.py:1018
  70.4 8.3 %collective-permute-start.8 = (bf16[4,2,80,128]{3,2,1,0:T(8,128)(2,1)S(1)}, bf16[4,2,80,128]{3,2,1,0:T(8,128)(2,1)S(1)}, u32[]{:S(2)}, u32[]{:S(2)}) collective-permute-start(bf16[4,2,80,128]{3,2,1,0:T(8,128)(2,1)S(1)} %get-tuple-element.13), channel_id=1, source_target_pairs={{0,4},{2,6},{4,0},{6,2},{1,5},{3,7},{5,1},{7,3},{8,12},{10,14},{12... | collective-permute-start | bytes 491528 | tf_op jit(solution)/shard_map/ppermute | solution.py:1018
  70.9 8.4 %collective-permute-start.9 = (bf16[4,2,80,128]{3,2,1,0:T(8,128)(2,1)S(1)}, bf16[4,2,80,128]{3,2,1,0:T(8,128)(2,1)S(1)}, u32[]{:S(2)}, u32[]{:S(2)}) collective-permute-start(bf16[4,2,80,128]{3,2,1,0:T(8,128)(2,1)S(1)} %get-tuple-element.12), channel_id=1, source_target_pairs={{0,2},{2,0},{4,6},{6,4},{1,3},{3,1},{5,7},{7,5},{8,10},{10,8},{12,... | collective-permute-start | bytes 491528 | tf_op jit(solution)/shard_map/ppermute | solution.py:1018
  79.4 4.5 %collective-permute-start.10 = (bf16[2,2,80,128]{3,2,1,0:T(8,128)(2,1)S(1)}, bf16[2,2,80,128]{3,2,1,0:T(8,128)(2,1)S(1)}, u32[]{:S(2)}, u32[]{:S(2)}) collective-permute-start(bf16[2,2,80,128]{3,2,1,0:T(8,128)(2,1)S(1)} %dynamic-slice_convert_fusion), channel_id=1, source_target_pairs={{0,8},{8,0},{16,24},{24,16},{1,9},{9,1},{17,25},{25,17},{2,10},{10... | collective-permute-start | bytes 245768 | tf_op jit(solution)/shard_map/ppermute | solution.py:989
  83.9 5.0 %collective-permute-start.11 = (bf16[1,2,80,128]{3,2,1,0:T(8,128)(2,1)S(1)}, bf16[1,2,80,128]{3,2,1,0:T(8,128)(2,1)S(1)}, u32[]{:S(2)}, u32[]{:S(2)}) collective-permute-start(bf16[1,2,80,128]{3,2,1,0:T(8,128)(2,1)S(1)} %dynamic-slice_convert_fusion.1), channel_id=1, source_target_pairs={{0,16},{8,24},{16,0},{24,8},{1,17},{9,25},{17,1},{25,9},{2,18},{10... | collective-permute-start | bytes 122888 | tf_op jit(solution)/shard_map/ppermute | solution.py:989

commit v8 on v7

--- a/solution.py
+++ b/solution.py
@@ -1003,20 +1003,21 @@
     for away in (1, 2, 3):
         pairs = [(i, i ^ away) for i in range(4)]
         parts.append(lax.ppermute(part, ("x", "y"), pairs))
-    own = jnp.stack(parts)
-    return own, swap_along(own, "core", 1)
+    others = [swap_along(part, "core", 1) for part in parts]
+    return jnp.stack(parts), jnp.stack(others)
 
 
 def reduce_pairs(keep, give, size):
-    got = swap_along(give, "core", 1)
-    part = (keep.astype(F32) + got.astype(F32)).astype(BF16)
     me = 2 * lax.axis_index("x") + lax.axis_index("y")
-    total = lax.dynamic_index_in_dim(part, me, 0, False).astype(F32)
-    for away in (3, 2, 1):
-        pairs = [(i, i ^ away) for i in range(4)]
-        theirs = lax.dynamic_index_in_dim(part, me ^ away, 0, False)
-        total += lax.ppermute(theirs, ("x", "y"), pairs).astype(F32)
-    part = total
+    part = 0.0
+    for away in (3, 2, 1, 0):
+        theirs = lax.dynamic_index_in_dim(give, me ^ away, 0, False)
+        mine = lax.dynamic_index_in_dim(keep, me ^ away, 0, False)
+        both = mine.astype(F32) + swap_along(theirs, "core", 1).astype(F32)
+        if away:
+            pairs = [(i, i ^ away) for i in range(4)]
+            both = lax.ppermute(both.astype(BF16), ("x", "y"), pairs).astype(F32)
+        part += both
     z = lax.axis_index("z")
     for bit, count in ((1, 2), (2, 1)):
         high = (z // bit) % 2

time: 90 us -> 89.1 us (0.990)
  waiting for transfers between devices: 28.3 us -> 26.1 us
  starting transfers between devices: 16.7 us -> 17.9 us
    ppermute x6 -> x12, waiting for transfers between devices: 15.2 us -> 13.3 us  [swap_along(): return lax.ppermute(x, axis, pairs)]
    ppermute x6 -> x12, starting transfers between devices: 9.63 us -> 10.8 us  [swap_along(): return lax.ppermute(x, axis, pairs)]
  transfers between devices with their start and end apart: 12 -> 18, of which waited for: 12 -> 14; matrix products, arithmetic and copies ran while one was open for 0% -> 0% of each run, Pallas kernels for 0% -> 0%
where the time goes in v8:
time: 89.1 us; the launch traced here: 88.9 us
  Pallas kernels  41.7 us (47%)
  waiting for transfers between devices  26.1 us (29%)
  starting transfers between devices  17.9 us (20%)
  other arithmetic  2.18 us (2%)
    pallas_call x1, Pallas kernels, run_kernel(): pl.pallas_call(body, out_shape=(full, full, blocks, blocks), in_specs=[an...  41.7 us
    ppermute x12, waiting for transfers between devices, swap_along(): return lax.ppermute(x, axis, pairs)  13.3 us
    ppermute x12, starting transfers between devices, swap_along(): return lax.ppermute(x, axis, pairs)  10.8 us
    ppermute x3, waiting for transfers between devices, reduce_pairs(): both = lax.ppermute(both.astype(BF16), ('x', 'y'), pairs).astype(F32)  7.25 us
    ppermute x3, waiting for transfers between devices, gather_pairs(): parts.append(lax.ppermute(part, ('x', 'y'), pairs))  5.59 us
    ppermute x3, starting transfers between devices, reduce_pairs(): both = lax.ppermute(both.astype(BF16), ('x', 'y'), pairs).astype(F32)  3.55 us
    ppermute x3, starting transfers between devices, gather_pairs(): parts.append(lax.ppermute(part, ('x', 'y'), pairs))  3.55 us
  transfers between devices with their start and end apart: 18, of which 14 were waited for; matrix products, arithmetic and copies ran while one was open for 0% of the time, Pallas kernels for 0%

profile of v8, /device:TPU:0, one launch (start us, length us, event | category | flops | bytes accessed | tf_op | source)
XLA Modules:
  0.0 88.9 jit_solution(10676062497690990020)
XLA Ops:
  0.6 1.0 %fusion.4 = bf16[1,2,80,128]{3,1,2,0:T(2,128)(2,1)S(1)} fusion(pred[]{:T(512)S(6)} %eq.7, bf16[2,9280]{1,0:T(2,128)(2,1)} %param.8), kind=kLoop, calls=%fused_computation.22 | loop fusion | flops 20480 | bytes 78081
  1.6 4.1 %collective-permute-start = (bf16[1,2,80,128]{3,2,1,0:T(8,128)(2,1)S(1)}, bf16[1,2,80,128]{3,2,1,0:T(8,128)(2,1)S(1)}, u32[]{:S(2)}, u32[]{:S(2)}) collective-permute-start(bf16[1,2,80,128]{3,2,1,0:T(8,128)(2,1)S(1)} %get-tuple-element.18), channel_id=1, source_target_pairs={{0,16},{8,24},{16,0},{24,8},{1,17},{9,25},{17,1},{25,9},{2,18},{10... | collective-permute-start | bytes 122888 | tf_op jit(solution)/shard_map/ppermute | solution.py:989
  5.7 2.4 %collective-permute-done = bf16[1,2,80,128]{3,2,1,0:T(8,128)(2,1)S(1)} collective-permute-done((bf16[1,2,80,128]{3,2,1,0:T(8,128)(2,1)S(1)}, bf16[1,2,80,128]{3,2,1,0:T(8,128)(2,1)S(1)}, u32[]{:S(2)}, u32[]{:S(2)}) %collective-permute-start) | collective-permute-done | bytes 40992 | tf_op jit(solution)/shard_map/ppermute | solution.py:989
  8.2 1.5 %collective-permute-start.1 = (bf16[2,2,80,128]{3,2,1,0:T(8,128)(2,1)S(1)}, bf16[2,2,80,128]{3,2,1,0:T(8,128)(2,1)S(1)}, u32[]{:S(2)}, u32[]{:S(2)}) collective-permute-start(bf16[2,2,80,128]{3,2,1,0:T(8,128)(2,1)S(1)} %pad_maximum_fusion.2), channel_id=1, source_target_pairs={{0,8},{8,0},{16,24},{24,16},{1,9},{9,1},{17,25},{25,17},{2,10},{10... | collective-permute-start | bytes 245768 | tf_op jit(solution)/shard_map/ppermute | solution.py:989
  9.7 3.0 %collective-permute-done.1 = bf16[2,2,80,128]{3,2,1,0:T(8,128)(2,1)S(1)} collective-permute-done((bf16[2,2,80,128]{3,2,1,0:T(8,128)(2,1)S(1)}, bf16[2,2,80,128]{3,2,1,0:T(8,128)(2,1)S(1)}, u32[]{:S(2)}, u32[]{:S(2)}) %collective-permute-start.1) | collective-permute-done | bytes 81952 | tf_op jit(solution)/shard_map/ppermute | solution.py:989
  12.7 1.8 %collective-permute-start.2 = (bf16[4,2,80,128]{3,2,1,0:T(8,128)(2,1)S(1)}, bf16[4,2,80,128]{3,2,1,0:T(8,128)(2,1)S(1)}, u32[]{:S(2)}, u32[]{:S(2)}) collective-permute-start(bf16[4,2,80,128]{3,2,1,0:T(8,128)(2,1)S(1)} %constant_dynamic-update-slice_fusion), channel_id=1, source_target_pairs={{0,2},{2,0},{4,6},{6,4},{1,3},{3,1},{5,7},{7,5},{8,10},{10,8},{12,... | collective-permute-start | bytes 491528 | tf_op jit(solution)/shard_map/ppermute | solution.py:1005
  14.5 1.5 %collective-permute-start.3 = (bf16[4,2,80,128]{3,2,1,0:T(8,128)(2,1)S(1)}, bf16[4,2,80,128]{3,2,1,0:T(8,128)(2,1)S(1)}, u32[]{:S(2)}, u32[]{:S(2)}) collective-permute-start(bf16[4,2,80,128]{3,2,1,0:T(8,128)(2,1)S(1)} %constant_dynamic-update-slice_fusion), channel_id=1, source_target_pairs={{0,4},{2,6},{4,0},{6,2},{1,5},{3,7},{5,1},{7,3},{8,12},{10,14},{12... | collective-permute-start | bytes 491528 | tf_op jit(solution)/shard_map/ppermute | solution.py:1005
  16.0 0.3 collective-permute-start.4
  16.2 0.0 collective-permute-start.5
  16.2 3.4 %collective-permute-done.2 = bf16[4,2,80,128]{3,2,1,0:T(8,128)(2,1)S(1)} collective-permute-done((bf16[4,2,80,128]{3,2,1,0:T(8,128)(2,1)S(1)}, bf16[4,2,80,128]{3,2,1,0:T(8,128)(2,1)S(1)}, u32[]{:S(2)}, u32[]{:S(2)}) %collective-permute-start.2) | collective-permute-done | bytes 163872 | tf_op jit(solution)/shard_map/ppermute | solution.py:1005
  19.6 0.0 collective-permute-start.6
  19.6 0.2 collective-permute-done.3
  19.8 0.3 collective-permute-start.7
  20.1 2.0 %collective-permute-done.4 = bf16[4,2,80,128]{3,2,1,0:T(8,128)(2,1)S(1)} collective-permute-done((bf16[4,2,80,128]{3,2,1,0:T(8,128)(2,1)S(1)}, bf16[4,2,80,128]{3,2,1,0:T(8,128)(2,1)S(1)}, u32[]{:S(2)}, u32[]{:S(2)}) %collective-permute-start.4) | collective-permute-done | bytes 163872 | tf_op jit(solution)/shard_map/ppermute | solution.py:1005
  22.2 0.0 collective-permute-start.8
  22.2 0.1 pad_maximum_fusion.refs_2_
  22.3 0.0 collective-permute-done.5
  22.3 0.0 collective-permute-done.6
  22.3 0.0 collective-permute-done.7
  22.3 1.3 %collective-permute-done.8 = bf16[4,2,80,128]{3,2,1,0:T(8,128)(2,1)S(1)} collective-permute-done((bf16[4,2,80,128]{3,2,1,0:T(8,128)(2,1)S(1)}, bf16[4,2,80,128]{3,2,1,0:T(8,128)(2,1)S(1)}, u32[]{:S(2)}, u32[]{:S(2)}) %collective-permute-start.8) | collective-permute-done | bytes 163872 | tf_op jit(solution)/shard_map/ppermute | solution.py:989
  23.6 0.1 pad_maximum_fusion.1.refs_3_
  23.7 41.7 %shard_map.85 = (f32[17,192,128]{2,1,0:T(8,128)}, f32[17,192,128]{2,1,0:T(8,128)}, bf16[4,4,2,80,128]{4,3,2,1,0:T(8,128)(2,1)S(1)}, bf16[4,4,2,80,128]{4,3,2,1,0:T(8,128)(2,1)S(1)}) custom-call(bf16[17,192,128]{2,1,0:T(8,128)(2,1)} %bitcast.48, bf16[17,192,128]{2,1,0:T(8,128)(2,1)} %bitcast.49, bf16[4,4,2,80,128]{4,3,2,1,0:T(8,128)(2,1)S(1)} %pad_maximum_fusion.refs_2_, ...), custom_call_target="tpu_custom_call" | custom-call | tf_op jit(solution)/shard_map/pallas_call | solution.py:957
  65.4 0.1 dynamic-slice_bitcast_fusion.3
  65.5 0.2 collective-permute-start.11
  65.7 0.4 collective-permute-start.13
  66.1 0.1 collective-permute-start.9
  66.2 0.4 collective-permute-start.15
  66.6 0.4 collective-permute-done.11
  66.9 0.2 collective-permute-done.13
  67.2 0.3 collective-permute-done.9
  67.5 0.1 fusion.3
  67.6 1.8 %collective-permute-start.10 = (bf16[4,2,80,128]{3,2,1,0:T(8,128)(2,1)S(1)}, bf16[4,2,80,128]{3,2,1,0:T(8,128)(2,1)S(1)}, u32[]{:S(2)}, u32[]{:S(2)}) collective-permute-start(bf16[4,2,80,128]{3,2,1,0:T(8,128)(2,1)S(1)} %get-tuple-element.11), channel_id=1, source_target_pairs={{0,6},{2,4},{4,2},{6,0},{1,7},{3,5},{5,3},{7,1},{8,14},{10,12},{12... | collective-permute-start | bytes 491528 | tf_op jit(solution)/shard_map/ppermute | solution.py:1019
  69.4 0.5 collective-permute-start.12
  70.0 1.2 %collective-permute-start.14 = (bf16[4,2,80,128]{3,2,1,0:T(8,128)(2,1)S(1)}, bf16[4,2,80,128]{3,2,1,0:T(8,128)(2,1)S(1)}, u32[]{:S(2)}, u32[]{:S(2)}) collective-permute-start(bf16[4,2,80,128]{3,2,1,0:T(8,128)(2,1)S(1)} %get-tuple-element.12), channel_id=1, source_target_pairs={{0,2},{2,0},{4,6},{6,4},{1,3},{3,1},{5,7},{7,5},{8,10},{10,8},{12,... | collective-permute-start | bytes 491528 | tf_op jit(solution)/shard_map/ppermute | solution.py:1019
  71.1 0.0 collective-permute-done.15
  71.2 4.5 %collective-permute-done.10 = bf16[4,2,80,128]{3,2,1,0:T(8,128)(2,1)S(1)} collective-permute-done((bf16[4,2,80,128]{3,2,1,0:T(8,128)(2,1)S(1)}, bf16[4,2,80,128]{3,2,1,0:T(8,128)(2,1)S(1)}, u32[]{:S(2)}, u32[]{:S(2)}) %collective-permute-start.10) | collective-permute-done | bytes 163872 | tf_op jit(solution)/shard_map/ppermute | solution.py:1019
  75.6 2.2 %collective-permute-done.12 = bf16[4,2,80,128]{3,2,1,0:T(8,128)(2,1)S(1)} collective-permute-done((bf16[4,2,80,128]{3,2,1,0:T(8,128)(2,1)S(1)}, bf16[4,2,80,128]{3,2,1,0:T(8,128)(2,1)S(1)}, u32[]{:S(2)}, u32[]{:S(2)}) %collective-permute-start.12) | collective-permute-done | bytes 163872 | tf_op jit(solution)/shard_map/ppermute | solution.py:1019
  77.8 0.6 collective-permute-done.14
  78.4 0.1 fusion
  78.5 1.3 %collective-permute-start.16 = (bf16[2,2,80,128]{3,2,1,0:T(8,128)(2,1)S(1)}, bf16[2,2,80,128]{3,2,1,0:T(8,128)(2,1)S(1)}, u32[]{:S(2)}, u32[]{:S(2)}) collective-permute-start(bf16[2,2,80,128]{3,2,1,0:T(8,128)(2,1)S(1)} %dynamic-slice_convert_fusion), channel_id=1, source_target_pairs={{0,8},{8,0},{16,24},{24,16},{1,9},{9,1},{17,25},{25,17},{2,10},{10... | collective-permute-start | bytes 245768 | tf_op jit(solution)/shard_map/ppermute | solution.py:989
  79.9 3.2 %collective-permute-done.16 = bf16[2,2,80,128]{3,2,1,0:T(8,128)(2,1)S(1)} collective-permute-done((bf16[2,2,80,128]{3,2,1,0:T(8,128)(2,1)S(1)}, bf16[2,2,80,128]{3,2,1,0:T(8,128)(2,1)S(1)}, u32[]{:S(2)}, u32[]{:S(2)}) %collective-permute-start.16) | collective-permute-done | bytes 81952 | tf_op jit(solution)/shard_map/ppermute | solution.py:989
  83.1 2.4 %collective-permute-start.17 = (bf16[1,2,80,128]{3,2,1,0:T(8,128)(2,1)S(1)}, bf16[1,2,80,128]{3,2,1,0:T(8,128)(2,1)S(1)}, u32[]{:S(2)}, u32[]{:S(2)}) collective-permute-start(bf16[1,2,80,128]{3,2,1,0:T(8,128)(2,1)S(1)} %dynamic-slice_convert_fusion.1), channel_id=1, source_target_pairs={{0,16},{8,24},{16,0},{24,8},{1,17},{9,25},{17,1},{25,9},{2,18},{10... | collective-permute-start | bytes 122888 | tf_op jit(solution)/shard_map/ppermute | solution.py:989
  85.5 2.6 %collective-permute-done.17 = bf16[1,2,80,128]{3,2,1,0:T(8,128)(2,1)S(1)} collective-permute-done((bf16[1,2,80,128]{3,2,1,0:T(8,128)(2,1)S(1)}, bf16[1,2,80,128]{3,2,1,0:T(8,128)(2,1)S(1)}, u32[]{:S(2)}, u32[]{:S(2)}) %collective-permute-start.17) | collective-permute-done | bytes 40992 | tf_op jit(solution)/shard_map/ppermute | solution.py:989
  88.1 0.8 slice_select_fusion
  (9 shorter events, 0.2 us)
Async XLA Ops:
  1.6 6.5 %collective-permute-start = (bf16[1,2,80,128]{3,2,1,0:T(8,128)(2,1)S(1)}, bf16[1,2,80,128]{3,2,1,0:T(8,128)(2,1)S(1)}, u32[]{:S(2)}, u32[]{:S(2)}) collective-permute-start(bf16[1,2,80,128]{3,2,1,0:T(8,128)(2,1)S(1)} %get-tuple-element.18), channel_id=1, source_target_pairs={{0,16},{8,24},{16,0},{24,8},{1,17},{9,25},{17,1},{25,9},{2,18},{10... | collective-permute-start | bytes 122888 | tf_op jit(solution)/shard_map/ppermute | solution.py:989
  8.2 4.5 %collective-permute-start.1 = (bf16[2,2,80,128]{3,2,1,0:T(8,128)(2,1)S(1)}, bf16[2,2,80,128]{3,2,1,0:T(8,128)(2,1)S(1)}, u32[]{:S(2)}, u32[]{:S(2)}) collective-permute-start(bf16[2,2,80,128]{3,2,1,0:T(8,128)(2,1)S(1)} %pad_maximum_fusion.2), channel_id=1, source_target_pairs={{0,8},{8,0},{16,24},{24,16},{1,9},{9,1},{17,25},{25,17},{2,10},{10... | collective-permute-start | bytes 245768 | tf_op jit(solution)/shard_map/ppermute | solution.py:989
  12.7 6.9 %collective-permute-start.2 = (bf16[4,2,80,128]{3,2,1,0:T(8,128)(2,1)S(1)}, bf16[4,2,80,128]{3,2,1,0:T(8,128)(2,1)S(1)}, u32[]{:S(2)}, u32[]{:S(2)}) collective-permute-start(bf16[4,2,80,128]{3,2,1,0:T(8,128)(2,1)S(1)} %constant_dynamic-update-slice_fusion), channel_id=1, source_target_pairs={{0,2},{2,0},{4,6},{6,4},{1,3},{3,1},{5,7},{7,5},{8,10},{10,8},{12,... | collective-permute-start | bytes 491528 | tf_op jit(solution)/shard_map/ppermute | solution.py:1005
  14.5 5.3 %collective-permute-start.3 = (bf16[4,2,80,128]{3,2,1,0:T(8,128)(2,1)S(1)}, bf16[4,2,80,128]{3,2,1,0:T(8,128)(2,1)S(1)}, u32[]{:S(2)}, u32[]{:S(2)}) collective-permute-start(bf16[4,2,80,128]{3,2,1,0:T(8,128)(2,1)S(1)} %constant_dynamic-update-slice_fusion), channel_id=1, source_target_pairs={{0,4},{2,6},{4,0},{6,2},{1,5},{3,7},{5,1},{7,3},{8,12},{10,14},{12... | collective-permute-start | bytes 491528 | tf_op jit(solution)/shard_map/ppermute | solution.py:1005
  16.0 6.2 %collective-permute-start.4 = (bf16[4,2,80,128]{3,2,1,0:T(8,128)(2,1)S(1)}, bf16[4,2,80,128]{3,2,1,0:T(8,128)(2,1)S(1)}, u32[]{:S(2)}, u32[]{:S(2)}) collective-permute-start(bf16[4,2,80,128]{3,2,1,0:T(8,128)(2,1)S(1)} %constant_dynamic-update-slice_fusion), channel_id=1, source_target_pairs={{0,6},{2,4},{4,2},{6,0},{1,7},{3,5},{5,3},{7,1},{8,14},{10,12},{12... | collective-permute-start | bytes 491528 | tf_op jit(solution)/shard_map/ppermute | solution.py:1005
  16.2 6.0 %collective-permute-start.5 = (bf16[4,2,80,128]{3,2,1,0:T(8,128)(2,1)S(1)}, bf16[4,2,80,128]{3,2,1,0:T(8,128)(2,1)S(1)}, u32[]{:S(2)}, u32[]{:S(2)}) collective-permute-start(bf16[4,2,80,128]{3,2,1,0:T(8,128)(2,1)S(1)} %constant_dynamic-update-slice_fusion), channel_id=1, source_target_pairs={{0,1},{1,0},{2,3},{3,2},{4,5},{5,4},{6,7},{7,6},{8,9},{9,8},{10,11... | collective-permute-start | bytes 491528 | tf_op jit(solution)/shard_map/ppermute | solution.py:989
  19.6 2.7 %collective-permute-start.6 = (bf16[4,2,80,128]{3,2,1,0:T(8,128)(2,1)S(1)}, bf16[4,2,80,128]{3,2,1,0:T(8,128)(2,1)S(1)}, u32[]{:S(2)}, u32[]{:S(2)}) collective-permute-start(bf16[4,2,80,128]{3,2,1,0:T(8,128)(2,1)S(1)} %collective-permute-done.2), channel_id=1, source_target_pairs={{0,1},{1,0},{2,3},{3,2},{4,5},{5,4},{6,7},{7,6},{8,9},{9,8},{10,11... | collective-permute-start | bytes 491528 | tf_op jit(solution)/shard_map/ppermute | solution.py:989
  19.8 2.5 %collective-permute-start.7 = (bf16[4,2,80,128]{3,2,1,0:T(8,128)(2,1)S(1)}, bf16[4,2,80,128]{3,2,1,0:T(8,128)(2,1)S(1)}, u32[]{:S(2)}, u32[]{:S(2)}) collective-permute-start(bf16[4,2,80,128]{3,2,1,0:T(8,128)(2,1)S(1)} %collective-permute-done.3), channel_id=1, source_target_pairs={{0,1},{1,0},{2,3},{3,2},{4,5},{5,4},{6,7},{7,6},{8,9},{9,8},{10,11... | collective-permute-start | bytes 491528 | tf_op jit(solution)/shard_map/ppermute | solution.py:989
  22.2 1.4 %collective-permute-start.8 = (bf16[4,2,80,128]{3,2,1,0:T(8,128)(2,1)S(1)}, bf16[4,2,80,128]{3,2,1,0:T(8,128)(2,1)S(1)}, u32[]{:S(2)}, u32[]{:S(2)}) collective-permute-start(bf16[4,2,80,128]{3,2,1,0:T(8,128)(2,1)S(1)} %collective-permute-done.4), channel_id=1, source_target_pairs={{0,1},{1,0},{2,3},{3,2},{4,5},{5,4},{6,7},{7,6},{8,9},{9,8},{10,11... | collective-permute-start | bytes 491528 | tf_op jit(solution)/shard_map/ppermute | solution.py:989
  65.5 1.5 %collective-permute-start.11 = (bf16[4,2,80,128]{3,2,1,0:T(8,128)(2,1)S(1)}, bf16[4,2,80,128]{3,2,1,0:T(8,128)(2,1)S(1)}, u32[]{:S(2)}, u32[]{:S(2)}) collective-permute-start(bf16[4,2,80,128]{3,2,1,0:T(8,128)(2,1)S(1)} %get-tuple-element.17), channel_id=1, source_target_pairs={{0,1},{1,0},{2,3},{3,2},{4,5},{5,4},{6,7},{7,6},{8,9},{9,8},{10,11... | collective-permute-start | bytes 491528 | tf_op jit(solution)/shard_map/ppermute | solution.py:989
  65.7 1.5 %collective-permute-start.13 = (bf16[4,2,80,128]{3,2,1,0:T(8,128)(2,1)S(1)}, bf16[4,2,80,128]{3,2,1,0:T(8,128)(2,1)S(1)}, u32[]{:S(2)}, u32[]{:S(2)}) collective-permute-start(bf16[4,2,80,128]{3,2,1,0:T(8,128)(2,1)S(1)} %get-tuple-element.16), channel_id=1, source_target_pairs={{0,1},{1,0},{2,3},{3,2},{4,5},{5,4},{6,7},{7,6},{8,9},{9,8},{10,11... | collective-permute-start | bytes 491528 | tf_op jit(solution)/shard_map/ppermute | solution.py:989
  66.1 1.4 %collective-permute-start.9 = (bf16[4,2,80,128]{3,2,1,0:T(8,128)(2,1)S(1)}, bf16[4,2,80,128]{3,2,1,0:T(8,128)(2,1)S(1)}, u32[]{:S(2)}, u32[]{:S(2)}) collective-permute-start(bf16[4,2,80,128]{3,2,1,0:T(8,128)(2,1)S(1)} %get-tuple-element.14), channel_id=1, source_target_pairs={{0,1},{1,0},{2,3},{3,2},{4,5},{5,4},{6,7},{7,6},{8,9},{9,8},{10,11... | collective-permute-start | bytes 491528 | tf_op jit(solution)/shard_map/ppermute | solution.py:989
  66.2 5.0 %collective-permute-start.15 = (bf16[4,2,80,128]{3,2,1,0:T(8,128)(2,1)S(1)}, bf16[4,2,80,128]{3,2,1,0:T(8,128)(2,1)S(1)}, u32[]{:S(2)}, u32[]{:S(2)}) collective-permute-start(bf16[4,2,80,128]{3,2,1,0:T(8,128)(2,1)S(1)} %get-tuple-element.15), channel_id=1, source_target_pairs={{0,1},{1,0},{2,3},{3,2},{4,5},{5,4},{6,7},{7,6},{8,9},{9,8},{10,11... | collective-permute-start | bytes 491528 | tf_op jit(solution)/shard_map/ppermute | solution.py:989
  67.6 8.0 %collective-permute-start.10 = (bf16[4,2,80,128]{3,2,1,0:T(8,128)(2,1)S(1)}, bf16[4,2,80,128]{3,2,1,0:T(8,128)(2,1)S(1)}, u32[]{:S(2)}, u32[]{:S(2)}) collective-permute-start(bf16[4,2,80,128]{3,2,1,0:T(8,128)(2,1)S(1)} %get-tuple-element.11), channel_id=1, source_target_pairs={{0,6},{2,4},{4,2},{6,0},{1,7},{3,5},{5,3},{7,1},{8,14},{10,12},{12... | collective-permute-start | bytes 491528 | tf_op jit(solution)/shard_map/ppermute | solution.py:1019
  69.4 8.4 %collective-permute-start.12 = (bf16[4,2,80,128]{3,2,1,0:T(8,128)(2,1)S(1)}, bf16[4,2,80,128]{3,2,1,0:T(8,128)(2,1)S(1)}, u32[]{:S(2)}, u32[]{:S(2)}) collective-permute-start(bf16[4,2,80,128]{3,2,1,0:T(8,128)(2,1)S(1)} %get-tuple-element.13), channel_id=1, source_target_pairs={{0,4},{2,6},{4,0},{6,2},{1,5},{3,7},{5,1},{7,3},{8,12},{10,14},{12... | collective-permute-start | bytes 491528 | tf_op jit(solution)/shard_map/ppermute | solution.py:1019
  70.0 8.5 %collective-permute-start.14 = (bf16[4,2,80,128]{3,2,1,0:T(8,128)(2,1)S(1)}, bf16[4,2,80,128]{3,2,1,0:T(8,128)(2,1)S(1)}, u32[]{:S(2)}, u32[]{:S(2)}) collective-permute-start(bf16[4,2,80,128]{3,2,1,0:T(8,128)(2,1)S(1)} %get-tuple-element.12), channel_id=1, source_target_pairs={{0,2},{2,0},{4,6},{6,4},{1,3},{3,1},{5,7},{7,5},{8,10},{10,8},{12,... | collective-permute-start | bytes 491528 | tf_op jit(solution)/shard_map/ppermute | solution.py:1019
  78.5 4.5 %collective-permute-start.16 = (bf16[2,2,80,128]{3,2,1,0:T(8,128)(2,1)S(1)}, bf16[2,2,80,128]{3,2,1,0:T(8,128)(2,1)S(1)}, u32[]{:S(2)}, u32[]{:S(2)}) collective-permute-start(bf16[2,2,80,128]{3,2,1,0:T(8,128)(2,1)S(1)} %dynamic-slice_convert_fusion), channel_id=1, source_target_pairs={{0,8},{8,0},{16,24},{24,16},{1,9},{9,1},{17,25},{25,17},{2,10},{10... | collective-permute-start | bytes 245768 | tf_op jit(solution)/shard_map/ppermute | solution.py:989
  83.1 5.0 %collective-permute-start.17 = (bf16[1,2,80,128]{3,2,1,0:T(8,128)(2,1)S(1)}, bf16[1,2,80,128]{3,2,1,0:T(8,128)(2,1)S(1)}, u32[]{:S(2)}, u32[]{:S(2)}) collective-permute-start(bf16[1,2,80,128]{3,2,1,0:T(8,128)(2,1)S(1)} %dynamic-slice_convert_fusion.1), channel_id=1, source_target_pairs={{0,16},{8,24},{16,0},{24,8},{1,17},{9,25},{17,1},{25,9},{2,18},{10... | collective-permute-start | bytes 122888 | tf_op jit(solution)/shard_map/ppermute | solution.py:989
